TPU v7x, 32 devices: a whole 2x2x4 slice. The times are simulated.
32 devices in a mesh: gx: 4 (over y, x), gy: 2 (over core), gz: 4 (over z).
Axes of the slice: x: 2, y: 2, z: 4, core: 2. Of those that a mesh axis runs over, the one named last changes fastest.
Arguments:
- cell_weight: float32 [16, 32, 512], P('gx', 'gy', 'gz'), may hold values from 0.3 to 3
- weight_grad: float32 [16, 32, 512], P('gx', 'gy', 'gz'), may hold values from -4 to 4
- material: int32 [16, 32, 512], P('gx', 'gy', 'gz'), may hold values from 0 to 7
- modulus: float32 [8], replicated, may hold values from 0.25 to 2
- node_mass: float32 [16, 32, 512], P('gx', 'gy', 'gz'), may hold values from 0.05 to 0.5
- pinned: int32 [16, 32, 512], P('gx', 'gy', 'gz'), may hold values 0 or 1
- positions: float32 [3, 16, 32, 512], P(None, 'gx', 'gy', 'gz'), may hold values from -6 to 6
- forces: float32 [3, 16, 32, 512], P(None, 'gx', 'gy', 'gz'), may hold values from -6 to 6
Outputs:
- iterate: float32 [3, 16, 32, 512], P(None, 'gx', 'gy', 'gz')
- level_one: float32 [27, 8, 16, 256], P(None, 'gx', 'gy', 'gz')
All inputs are finite; a program needn't handle non-finite values. No bound on the sum of `pinned` on one device may be relied on, other than what follows from the above.
Results may differ from a plain program's by a relative error of at most 0.0065.
Values sent between devices are 32-bit elements; how exact they have to be, the bound alone decides.
No kernel may reach another device: no remote copies, remote signals or barrier semaphores. Data moves between devices by JAX's collectives and lax.ppermute only.
A program may use at most 64 MiB of HBM per device.

v0:
```python
import jax
import jax.numpy as jnp
import numpy as np
from jax import lax
from jax.experimental import pallas as pl
from jax.experimental.pallas import tpu as pltpu
from jax.sharding import PartitionSpec as P

OMEGA = 0.6
LEARN_RATE = 0.5
PIN_WEIGHT = 4.0
ELEMENT_TERMS = (1.0 / 3.0, 0.0, -1.0 / 12.0, -1.0 / 12.0)


def shifted(x, axis, by):
    peers = lax.axis_size(axis)
    pairs = [(i, i + by) for i in range(peers) if 0 <= i + by < peers]
    return lax.ppermute(x, axis, pairs)


def extended(block, sides, width):
    for axis, dim in sides:
        count = lax.axis_size(axis)
        forward = [(i, i + 1) for i in range(count - 1)]
        backward = [(target, source) for source, target in forward]
        low = lax.ppermute(
            lax.slice_in_dim(block, block.shape[dim] - width, None, axis=dim), axis, forward
        )
        high = lax.ppermute(lax.slice_in_dim(block, 0, width, axis=dim), axis, backward)
        block = jnp.concatenate([low, block, high], axis=dim)
    return block


def offset_list():
    return [
        (shift_x, shift_y, shift_z)
        for shift_x in (-1, 0, 1)
        for shift_y in (-1, 0, 1)
        for shift_z in (-1, 0, 1)
    ]


def corner_list():
    return [(bit_x, bit_y, bit_z) for bit_x in (0, 1) for bit_y in (0, 1) for bit_z in (0, 1)]


def hat_weight(distance):
    if distance == 0:
        return 1.0
    if abs(distance) == 1:
        return 0.5
    return 0.0


def galerkin_tables():
    offsets = offset_list()
    tables = np.zeros((27, 27, 27), np.float32)
    for slot_a, outer in enumerate(offsets):
        for slot_c, coarse in enumerate(offsets):
            for slot_f, inner in enumerate(offsets):
                factor = 1.0
                for axis_pos in range(3):
                    factor *= hat_weight(outer[axis_pos]) * hat_weight(
                        2 * coarse[axis_pos] - outer[axis_pos] - inner[axis_pos]
                    )
                tables[slot_a, slot_c, slot_f] = factor
    return tables


def stiffness_of(cell_weight, weight_grad, material, modulus):
    lookup = jnp.zeros(cell_weight.shape, jnp.float32)
    for index in range(modulus.shape[0]):
        lookup = lookup + jnp.where(material == index, modulus[index], 0.0)
    return cell_weight * jnp.exp(-LEARN_RATE * weight_grad) * lookup


def assemble(cell_rim, node_mass, pinned_weight):
    node_shape = node_mass.shape
    rows_out = []
    for offset in offset_list():
        total = jnp.zeros(node_shape, jnp.float32)
        for corner in corner_list():
            if all((0 <= corner[axis_pos] + offset[axis_pos] <= 1 for axis_pos in range(3))):
                total = (
                    total
                    + cell_rim[
                        1 - corner[0] : 1 - corner[0] + node_shape[0],
                        1 - corner[1] : 1 - corner[1] + node_shape[1],
                        1 - corner[2] : 1 - corner[2] + node_shape[2],
                    ]
                )
        nonzero = sum((1 for axis_pos in range(3) if offset[axis_pos] != 0))
        entry = ELEMENT_TERMS[nonzero] * total
        if nonzero == 0:
            entry = entry + node_mass + PIN_WEIGHT * pinned_weight
        rows_out.append(entry)
    return jnp.stack(rows_out)


def galerkin(op_rim, coarse_shape):
    tables = jnp.asarray(galerkin_tables())
    result = None
    for slot_a, outer in enumerate(offset_list()):
        piece = op_rim[
            :,
            outer[0] + 1 : outer[0] + 1 + 2 * coarse_shape[0] : 2,
            outer[1] + 1 : outer[1] + 1 + 2 * coarse_shape[1] : 2,
            outer[2] + 1 : outer[2] + 1 + 2 * coarse_shape[2] : 2,
        ]
        term = jnp.einsum("pk,kxyz->pxyz", tables[slot_a], piece, precision=lax.Precision.HIGHEST)
        result = term if result is None else result + term
    return result


def stencil_apply(stencil, padded):
    node_shape = stencil.shape[1:]
    result = None
    for slot, offset in enumerate(offset_list()):
        window = padded[
            :,
            1 + offset[0] : 1 + offset[0] + node_shape[0],
            1 + offset[1] : 1 + offset[1] + node_shape[1],
            1 + offset[2] : 1 + offset[2] + node_shape[2],
        ]
        term = stencil[slot][None] * window
        result = term if result is None else result + term
    return result


def relax(stencil, field, rhs_field, padded):
    return field + OMEGA * (rhs_field - stencil_apply(stencil, padded)) / stencil[13][None]


def restrict_axis(field, axis_pos, coarse_len):
    below = lax.slice_in_dim(field, 0, 2 * coarse_len - 1, 2, axis_pos)
    centre = lax.slice_in_dim(field, 1, 2 * coarse_len, 2, axis_pos)
    above = lax.slice_in_dim(field, 2, 2 * coarse_len + 1, 2, axis_pos)
    return 0.5 * below + centre + 0.5 * above


def restrict(rim_field, coarse_shape):
    field = rim_field
    for axis_pos in (1, 2, 3):
        field = restrict_axis(field, axis_pos, coarse_shape[axis_pos - 1])
    return field


def prolong_axis(field, axis_pos, coarse_len):
    lower = lax.slice_in_dim(field, 0, coarse_len, 1, axis_pos)
    upper = lax.slice_in_dim(field, 1, coarse_len + 1, 1, axis_pos)
    middle = 0.5 * (lower + upper)
    paired = jnp.stack([lower, middle], axis=axis_pos + 1)
    new_shape = list(lower.shape)
    new_shape[axis_pos] = 2 * coarse_len
    return paired.reshape(new_shape)


def prolong(rim_field, coarse_shape):
    field = rim_field
    for axis_pos in (1, 2, 3):
        field = prolong_axis(field, axis_pos, coarse_shape[axis_pos - 1])
    return field


def boundary_layer(field, axis_pos, forward):
    extent = field.shape[axis_pos]
    if forward:
        return lax.slice_in_dim(field, extent - 1, extent, 1, axis_pos)
    return lax.slice_in_dim(field, 0, 1, 1, axis_pos)


def attach(field, layer_in, axis_pos, forward):
    if forward:
        return jnp.concatenate([layer_in, field], axis=axis_pos)
    return jnp.concatenate([field, layer_in], axis=axis_pos)


def extend(field, leading, forward):
    step = 1 if forward else -1
    got_x = shifted(boundary_layer(field, leading, forward), "gx", step)
    field = attach(field, got_x, leading, forward)
    got_y = shifted(boundary_layer(field, leading + 1, forward), "gy", step)
    field = attach(field, got_y, leading + 1, forward)
    got_z = shifted(boundary_layer(field, leading + 2, forward), "gz", step)
    return attach(field, got_z, leading + 2, forward)


def faces(field):
    return extended(field, (("gx", 1), ("gy", 2), ("gz", 3)), 1)


def shards(cell_weight, weight_grad, material, modulus, node_mass, pinned, positions, forces):
    stiffness = stiffness_of(cell_weight, weight_grad, material, modulus)
    fine_shape = node_mass.shape
    mid_shape = tuple((extent // 2 for extent in fine_shape))
    low_shape = tuple((extent // 4 for extent in fine_shape))
    pinned_weight = pinned.astype(jnp.float32)
    level_zero = assemble(extend(stiffness, 0, True), node_mass, pinned_weight)
    zero_rim = extend(level_zero, 1, True)
    level_one = galerkin(zero_rim, mid_shape)
    level_two = galerkin(extend(level_one, 1, True), low_shape)
    iterate = positions
    for sweep in range(2):
        iterate = relax(level_zero, iterate, forces, faces(iterate))
    residual_zero = forces - stencil_apply(level_zero, faces(iterate))
    rhs_one = restrict(extend(residual_zero, 1, True), mid_shape)
    corr_one = OMEGA * rhs_one / level_one[13][None]
    corr_one = relax(level_one, corr_one, rhs_one, faces(corr_one))
    residual_one = rhs_one - stencil_apply(level_one, faces(corr_one))
    rhs_two = restrict(extend(residual_one, 1, True), low_shape)
    corr_two = OMEGA * rhs_two / level_two[13][None]
    for sweep in range(3):
        corr_two = relax(level_two, corr_two, rhs_two, faces(corr_two))
    corr_one = corr_one + prolong(extend(corr_two, 1, False), low_shape)
    for sweep in range(2):
        corr_one = relax(level_one, corr_one, rhs_one, faces(corr_one))
    iterate = iterate + prolong(extend(corr_one, 1, False), mid_shape)
    for sweep in range(2):
        iterate = relax(level_zero, iterate, forces, faces(iterate))
    return (iterate, level_one)


LANES = 128
ROWS = 8
TILE = (ROWS, LANES)
SNAKE = (0, 1, 3, 2)


def lane_roll(x, by):
    return pltpu.roll(x, by % LANES, x.ndim - 1)


def row_roll(x, by):
    return pltpu.roll(x, by % ROWS, x.ndim - 2)


def lane_ids(shape):
    return lax.broadcasted_iota(jnp.int32, shape, len(shape) - 1)


def row_ids(shape):
    return lax.broadcasted_iota(jnp.int32, shape, len(shape) - 2)


def x_below(x):
    return jnp.where(lane_ids(x.shape) >= 32, lane_roll(x, 32), 0.0)


def x_above(x):
    return jnp.where(lane_ids(x.shape) < 96, lane_roll(x, -32), 0.0)


def y_below(x):
    return jnp.where(row_ids(x.shape) >= 1, row_roll(x, 1), 0.0)


def y_above(x):
    return jnp.where(row_ids(x.shape) < ROWS - 1, row_roll(x, -1), 0.0)


def z_below(x):
    return lane_roll(x, 1)


def z_above(x):
    return lane_roll(x, -1)


def swap_groups(parts, unit):
    group = lane_ids(TILE) // unit
    parts = list(parts)
    for bit in (1, 2):
        low = (group & bit) == 0
        for i in range(4):
            if i & bit == 0:
                a, b = parts[i], parts[i + bit]
                parts[i] = jnp.where(low, a, lane_roll(b, unit * bit))
                parts[i + bit] = jnp.where(low, lane_roll(a, -unit * bit), b)
    return parts


def three_pieces(x):
    first = x.astype(jnp.bfloat16)
    rest = x - first.astype(jnp.float32)
    second = rest.astype(jnp.bfloat16)
    third = (rest - second.astype(jnp.float32)).astype(jnp.bfloat16)
    return first, second, third


def reorder(x, table):
    total = None
    for piece in three_pieces(x):
        term = jnp.dot(piece, table, preferred_element_type=jnp.float32)
        total = term if total is None else total + term
    return total


def pack_table():
    table = np.zeros((512, 512), np.float32)
    for xp in range(4):
        for z in range(128):
            t, q, p = z // 32, (z % 32) // 4, z % 4
            table[xp * 128 + z, t * 128 + xp * 32 + p * 8 + q] = 1.0
    return table


def coarse_table():
    table = np.zeros((512, 512), np.float32)
    for t in range(4):
        for o in range(4):
            for xp in range(2):
                for zp in range(2):
                    for zq in range(8):
                        src = t * 128 + o * 32 + xp * 16 + zp * 8 + zq
                        table[src, o * 128 + xp * 64 + 16 * t + 2 * zq + zp] = 1.0
    return table


def pack_kernel(mod_ref, cw_ref, wg_ref, mat_ref, mass_ref, pin_ref, pos_ref, force_ref, table_ref, out_ref):
    material = mat_ref[...]
    lookup = jnp.zeros(material.shape, jnp.float32)
    for index in range(mod_ref.shape[0]):
        lookup = jnp.where(material == index, mod_ref[index], lookup)
    stiff = cw_ref[...] * jnp.exp(-LEARN_RATE * wg_ref[...]) * lookup
    mass = mass_ref[...] + PIN_WEIGHT * pin_ref[...].astype(jnp.float32)
    fields = [stiff, mass] + [pos_ref[c] for c in range(3)] + [force_ref[c] for c in range(3)]
    rows = [jnp.concatenate([field[x] for x in range(4)], axis=-1) for field in fields]
    moved = reorder(jnp.concatenate(rows, axis=0), table_ref[...])
    for t in range(4):
        for f in range(8):
            out_ref[t, f] = moved[16 * f:16 * f + 16, 128 * t:128 * t + 128]


def unpack_kernel(idx_ref, own_ref, got_ref, table_ref, coarse_ref, iterate_ref, level_ref):
    take_own = idx_ref[0] == 1

    def block(t):
        j = idx_ref[1 + t]
        return jnp.where(take_own, own_ref[j], got_ref[j])

    whole = jnp.concatenate([block(t) for t in range(4)], axis=-1)
    fine = reorder(whole[:48], table_ref[...])
    for c in range(3):
        for x in range(4):
            iterate_ref[c, x] = fine[16 * c:16 * c + 16, 128 * x:128 * x + 128]
    coarse = reorder(whole[48:], coarse_ref[...])
    for o in range(27):
        for x in range(2):
            col = (o % 4) * 128 + x * 64
            level_ref[o, x] = coarse[8 * (o // 4):8 * (o // 4) + 8, col:col + 64]


def fill_low(ref, n):
    ref[0, 1:, 1:] = x_below(ref[n, 1:, 1:])
    ref[:, 0, 1:] = y_below(ref[:, n, 1:])
    ref[:, :, 0] = z_below(ref[:, :, n])


def fill_both(ref, n):
    mid = slice(1, n + 1)
    ref[0, mid, mid] = x_below(ref[n, mid, mid])
    ref[n + 1, mid, mid] = x_above(ref[1, mid, mid])
    ref[:, 0, mid] = y_below(ref[:, n, mid])
    ref[:, n + 1, mid] = y_above(ref[:, 1, mid])
    ref[:, :, 0] = z_below(ref[:, :, n])
    ref[:, :, n + 1] = z_above(ref[:, :, 1])


def coarsen(low, mid, high, low_before, mid_before, high_before):
    out = []
    for i in range(len(mid) // 2):
        if i:
            mid_b, high_b, low_b = mid[2 * i - 1], high[2 * i - 1], low[2 * i - 1]
        else:
            mid_b, high_b, low_b = mid_before, high_before, low_before
        down = 0.5 * (low[2 * i] + low_b) + 0.25 * mid_b
        here = mid[2 * i] + 0.5 * (low[2 * i] + high[2 * i] + low[2 * i + 1] + high_b) + 0.25 * (
            mid[2 * i + 1] + mid_b
        )
        up = 0.5 * (high[2 * i] + high[2 * i + 1]) + 0.25 * mid[2 * i + 1]
        out.append((down, here, up))
    return out


def triple_product(src, mid_a, mid_b, dst, n):
    half = n // 2

    def pass_x(j, carry):
        parts = [[src[9 * f + j, i] for i in range(n)] for f in range(3)]
        before = [x_below(part[n - 1]) for part in parts]
        for i, trio in enumerate(coarsen(*parts, *before)):
            for c in range(3):
                mid_a[9 * c + j, i] = trio[c]
        return carry

    lax.fori_loop(0, 9, pass_x, 0)

    def pass_y(j, carry):
        base = 9 * (j // 3) + j % 3
        parts = [[mid_a[base + 3 * f, :, i] for i in range(n)] for f in range(3)]
        before = [y_below(part[n - 1]) for part in parts]
        for i, trio in enumerate(coarsen(*parts, *before)):
            for c in range(3):
                mid_b[base + 3 * c, :, i] = trio[c]
        return carry

    lax.fori_loop(0, 9, pass_y, 0)

    def pass_z(j, carry):
        parts = [[mid_b[3 * j + f, :, :, i] for i in range(n)] for f in range(3)]
        before = [z_below(part[n - 1]) for part in parts]
        for i, trio in enumerate(coarsen(*parts, *before)):
            for c in range(3):
                dst[3 * j + c, :, :, i] = trio[c]
        return carry

    lax.fori_loop(0, 9, pass_z, 0)


def sweep(level, field, n, store, skip_faces):
    def body(step, carry):
        x, y = step // n, step % n
        sums = [[None] * n for _ in range(3)]
        for o0 in range(3):
            for o1 in range(3):
                columns = [[field[c, x + o0, y + o1, z] for z in range(n + 2)] for c in range(3)]
                for o2 in range(3):
                    if skip_faces and (o0 != 1) + (o1 != 1) + (o2 != 1) == 1:
                        continue
                    for z in range(n):
                        coef = level[9 * o0 + 3 * o1 + o2, x, y, z]
                        for c in range(3):
                            term = coef * columns[c][z + o2]
                            sums[c][z] = term if sums[c][z] is None else sums[c][z] + term
        for c in range(3):
            for z in range(n):
                store(c, x, y, z, sums[c][z])
        return carry

    if n == 1:
        body(0, 0)
    else:
        lax.fori_loop(0, n * n, body, 0)


def relax_into(level, weight, rhs, src, dst, n, skip_faces=False):
    def store(c, x, y, z, value):
        dst[c, 1 + x, 1 + y, 1 + z] = src[c, 1 + x, 1 + y, 1 + z] + weight[x, y, z] * (rhs[c, x, y, z] - value)

    sweep(level, src, n, store, skip_faces)


def residual_down(level, rhs, src, res, coarse_rhs, n, skip_faces=False):
    half = n // 2

    def store(c, x, y, z, value):
        res[c, 1 + x, 1 + y, 1 + z] = rhs[c, x, y, z] - value

    sweep(level, src, n, store, skip_faces)

    def body(c, carry):
        fill_low(res.at[c], n)
        for i in range(half):
            part = 0.5 * (res[c, 2 * i] + res[c, 2 * i + 2]) + res[c, 2 * i + 1]
            for j in range(half):
                line = 0.5 * (part[2 * j] + part[2 * j + 2]) + part[2 * j + 1]
                for k in range(half):
                    coarse_rhs[c, i, j, k] = 0.5 * (line[2 * k] + line[2 * k + 2]) + line[2 * k + 1]
        return carry

    lax.fori_loop(0, 3, body, 0)


def add_prolonged(coarse, fine, inside, half):
    def between(values):
        out = []
        for i in range(half):
            out += [values[i], 0.5 * (values[i] + values[i + 1])]
        return out

    def body(c, carry):
        planes = between([coarse[c, 1 + i, 1:, 1:] for i in range(half + 1)])
        for x, plane in enumerate(planes):
            for y, line in enumerate(between([plane[j] for j in range(half + 1)])):
                for z, value in enumerate(between([line[k] for k in range(half + 1)])):
                    fine[c, 1 + x, 1 + y, 1 + z] += jnp.where(inside, value, 0.0)
        return carry

    lax.fori_loop(0, 3, body, 0)


def fill_all(ref, n):
    def body(c, carry):
        fill_both(ref.at[c], n)
        return carry

    lax.fori_loop(0, 3, body, 0)


def cycle_kernel(
    idx_ref, prev_ref, own_ref, next_ref, out_ref,
    fields, cells, level_a, weight_a, mid_a, mid_b, level_b, weight_b, mid_c, mid_d, level_c, weight_c,
    va, va2, vb, vb2, vc, vc2, res_a, res_b, rhs_b, rhs_c,
):
    gx_prev, gx_own, gx_next = idx_ref[0], idx_ref[1], idx_ref[2]
    slab = (lane_ids(TILE) // 8) % 4
    inside = (slab == 1) | ((slab == 0) & (idx_ref[3] == 1)) | ((slab == 2) & (idx_ref[4] == 1))

    def arrange(step, carry):
        f = step
        for yp in range(4):
            by_source = []
            for source in range(4):
                tiles = [
                    ref[lax.bitwise_xor(gx, source), f, pl.ds(yp, ROWS, stride=4), :]
                    for ref, gx in ((prev_ref, gx_prev), (own_ref, gx_own), (next_ref, gx_next))
                ]
                by_source.append(swap_groups(tiles + [jnp.zeros(TILE, jnp.float32)], 8))
            for zp in range(4):
                moved = swap_groups([by_source[source][zp] for source in range(4)], 32)
                for xp in range(4):
                    fields[f, xp, yp, zp] = moved[xp]
        return carry

    lax.fori_loop(0, 8, arrange, 0)

    for x in range(4):
        cells[1 + x, 1:, 1:] = fields[0, x] * ELEMENT_TERMS[3]
    fill_low(cells, 4)

    def build(step, carry):
        x, y = step // 4, step % 4
        near = [[[cells[x + 1 - s0, y + 1 - s1, z] for z in range(5)] for s1 in (0, 1)] for s0 in (0, 1)]
        for z in range(4):
            for slot, offset in enumerate(offset_list()):
                nonzero = sum(1 for part in offset if part != 0)
                if nonzero == 1:
                    level_a[slot, x, y, z] = jnp.zeros(TILE, jnp.float32)
                    continue
                total = None
                for s in corner_list():
                    if all(0 <= s[d] + offset[d] <= 1 for d in range(3)):
                        term = near[s[0]][s[1]][z + 1 - s[2]]
                        total = term if total is None else total + term
                if nonzero == 0:
                    total = (ELEMENT_TERMS[0] / ELEMENT_TERMS[3]) * total + fields[1, x, y, z]
                    weight_a[x, y, z] = jnp.where(inside, OMEGA / jnp.where(inside, total, 1.0), 0.0)
                level_a[slot, x, y, z] = total
        return carry

    lax.fori_loop(0, 16, build, 0)

    triple_product(level_a, mid_a, mid_b, level_b, 4)
    weight_b[...] = jnp.where(inside, OMEGA / jnp.where(inside, level_b[13], 1.0), 0.0)
    triple_product(level_b, mid_c, mid_d, level_c, 2)
    weight_c[...] = jnp.where(inside, OMEGA / jnp.where(inside, level_c[13], 1.0), 0.0)

    position, force = fields.at[2:5], fields.at[5:8]

    def load(c, carry):
        for x in range(4):
            va[c, 1 + x, 1:5, 1:5] = position[c, x]
        return carry

    lax.fori_loop(0, 3, load, 0)
    fill_all(va, 4)
    relax_into(level_a, weight_a, force, va, va2, 4, True)
    fill_all(va2, 4)
    relax_into(level_a, weight_a, force, va2, va, 4, True)
    fill_all(va, 4)
    residual_down(level_a, force, va, res_a, rhs_b, 4, True)

    for c in range(3):
        for x in range(2):
            vb[c, 1 + x, 1:3, 1:3] = weight_b[x] * rhs_b[c, x]
    fill_all(vb, 2)
    relax_into(level_b, weight_b, rhs_b, vb, vb2, 2)
    fill_all(vb2, 2)
    residual_down(level_b, rhs_b, vb2, res_b, rhs_c, 2)

    for c in range(3):
        vc[c, 1, 1, 1] = weight_c[0, 0, 0] * rhs_c[c, 0, 0, 0]
    fill_all(vc, 1)
    relax_into(level_c, weight_c, rhs_c, vc, vc2, 1)
    fill_all(vc2, 1)
    relax_into(level_c, weight_c, rhs_c, vc2, vc, 1)
    fill_all(vc, 1)
    relax_into(level_c, weight_c, rhs_c, vc, vc2, 1)
    fill_all(vc2, 1)

    add_prolonged(vc2, vb2, inside, 1)
    fill_all(vb2, 2)
    relax_into(level_b, weight_b, rhs_b, vb2, vb, 2)
    fill_all(vb, 2)
    relax_into(level_b, weight_b, rhs_b, vb, vb2, 2)
    fill_all(vb2, 2)

    add_prolonged(vb2, va, inside, 2)
    fill_all(va, 4)
    relax_into(level_a, weight_a, force, va, va2, 4, True)
    fill_all(va2, 4)
    relax_into(level_a, weight_a, force, va2, va, 4, True)

    def own_slab(tiles):
        total = None
        for group, tile in enumerate(tiles):
            moved = lane_roll(tile, 8 * group - 8)
            total = moved if total is None else jnp.where(slab == group, moved, total)
        return total

    for c in range(3):
        for yp in range(4):
            lines = [own_slab([va[c, 1 + xp, 1 + yp, 1 + zp] for zp in range(4)]) for xp in range(4)]
            for dest, tile in enumerate(swap_groups(lines, 32)):
                out_ref[lax.bitwise_xor(gx_own, dest), pl.ds(32 * c + yp, ROWS, stride=4), :] = tile
    for g in range(7):
        for yp in range(2):
            lines = [
                own_slab([level_b[min(4 * g + o, 26), xp, yp, zp] for xp in range(2) for zp in range(2)])
                for o in range(4)
            ]
            for dest, tile in enumerate(swap_groups(lines, 32)):
                out_ref[lax.bitwise_xor(gx_own, dest), pl.ds(96 + 16 * g + yp, ROWS, stride=2), :] = tile


def slab_place(gx, gz):
    order = jnp.where(gx < 2, gx, 5 - gx)
    return jnp.where(gz % 2 == 0, order, 3 - order)


def slab_owner(place, gz):
    order = place if gz % 2 == 0 else 3 - place
    return SNAKE[order]


def vmem_specs(count):
    return [pl.BlockSpec(memory_space=pltpu.VMEM)] * count


def shards_by_slab(cell_weight, weight_grad, material, modulus, node_mass, pinned, positions, forces):
    table = pack_table()
    smem = pl.BlockSpec(memory_space=pltpu.SMEM)
    gx, gy, gz = lax.axis_index("gx"), lax.axis_index("gy"), lax.axis_index("gz")
    f32 = jnp.float32
    packed = pl.pallas_call(
        pack_kernel,
        out_shape=jax.ShapeDtypeStruct((4, 8, 16, LANES), f32),
        in_specs=[smem] + vmem_specs(8),
        out_specs=vmem_specs(1)[0],
        name="pack",
    )(modulus, cell_weight, weight_grad, material, node_mass, pinned, positions, forces,
      jnp.asarray(table, jnp.bfloat16))

    lower = lax.ppermute(packed, "gy", [(0, 1)])
    block = jnp.concatenate([lower, packed], axis=2)
    by_partner = [
        lax.dynamic_index_in_dim(block, slab_place(gx ^ j, gz), 0, keepdims=False) for j in range(4)
    ]
    own = [by_partner[0]]
    for j in range(1, 4):
        pairs = [(2 * i + 1, 2 * (i ^ j) + 1) for i in range(4)]
        own.append(lax.ppermute(by_partner[j], ("gx", "gy"), pairs))
    own = jnp.stack(own)

    chain = [(slab_owner(place, z) * 2 + 1) * 4 + z for z in range(4) for place in range(4)]
    ahead = list(zip(chain[:-1], chain[1:]))
    behind = [(b, a) for a, b in ahead]
    everywhere = ("gx", "gy", "gz")
    before = lax.ppermute(own, everywhere, ahead)
    after = lax.ppermute(own, everywhere, behind)

    place = slab_place(gx, gz)

    def owner_of(place, z):
        order = jnp.where(z % 2 == 0, place, 3 - place)
        return jnp.where(order < 2, order, 5 - order)

    index = 4 * gz + place
    gx_before = owner_of((index - 1) % 4, (index - 1) // 4)
    gx_after = owner_of((index + 1) % 4, (index + 1) // 4)
    scalars = jnp.stack(
        [gx_before, gx, gx_after, (index > 0).astype(jnp.int32), (index < 15).astype(jnp.int32)]
    ).astype(jnp.int32)

    def buf(*dims):
        return pltpu.VMEM(tuple(dims) + TILE, f32)

    message = pl.pallas_call(
        cycle_kernel,
        out_shape=jax.ShapeDtypeStruct((4, 208, LANES), f32),
        in_specs=[smem] + vmem_specs(3),
        out_specs=vmem_specs(1)[0],
        scratch_shapes=[
            buf(8, 4, 4, 4), buf(5, 5, 5), buf(27, 4, 4, 4), buf(4, 4, 4),
            buf(27, 2, 4, 4), buf(27, 2, 2, 4), buf(27, 2, 2, 2), buf(2, 2, 2),
            buf(27, 1, 2, 2), buf(27, 1, 1, 2), buf(27, 1, 1, 1), buf(1, 1, 1),
            buf(3, 6, 6, 6), buf(3, 6, 6, 6), buf(3, 4, 4, 4), buf(3, 4, 4, 4), buf(3, 3, 3, 3), buf(3, 3, 3, 3),
            buf(3, 5, 5, 5), buf(3, 3, 3, 3), buf(3, 2, 2, 2), buf(3, 1, 1, 1),
        ],
        compiler_params=pltpu.CompilerParams(vmem_limit_bytes=48 * 1024 * 1024),
        name="cycle",
    )(scalars, before, own, after)

    back = [message[0]]
    for j in range(1, 4):
        pairs = [(2 * i + 1, 2 * (i ^ j) + 1) for i in range(4)]
        back.append(lax.ppermute(message[j], ("gx", "gy"), pairs))
    back = jnp.stack(back)
    fine = back[:, :96].reshape(4, 3, 2, 16, LANES)
    coarse = back[:, 96:].reshape(4, 7, 2, 8, LANES)

    def half(side):
        return jnp.concatenate(
            [fine[:, :, side].reshape(4, 48, LANES), coarse[:, :, side].reshape(4, 56, LANES)], axis=1
        )

    got = lax.ppermute(half(0), "gy", [(1, 0)])
    scalars = jnp.stack([gy] + [gx ^ owner_of(t, gz) for t in range(4)]).astype(jnp.int32)
    return pl.pallas_call(
        unpack_kernel,
        out_shape=[
            jax.ShapeDtypeStruct(positions.shape, f32),
            jax.ShapeDtypeStruct((27, 2, 8, 64), f32),
        ],
        in_specs=[smem] + vmem_specs(4),
        out_specs=vmem_specs(2),
        name="unpack",
    )(scalars, half(1), got, jnp.asarray(unpack_table(), jnp.bfloat16), jnp.asarray(coarse_table(), jnp.bfloat16))


def unpack_table():
    return np.ascontiguousarray(pack_table().T)


def solution(mesh):
    placed = (
        P("gx", "gy", "gz"),
        P("gx", "gy", "gz"),
        P("gx", "gy", "gz"),
        P(),
        P("gx", "gy", "gz"),
        P("gx", "gy", "gz"),
        P(None, "gx", "gy", "gz"),
        P(None, "gx", "gy", "gz"),
    )
    sizes = tuple(mesh.shape[axis] for axis in ("gx", "gy", "gz"))

    def choose(cell_weight, *rest):
        fits = sizes == (4, 2, 4) and cell_weight.shape == (4, 16, 128)
        return (shards_by_slab if fits else shards)(cell_weight, *rest)

    return jax.shard_map(
        choose,
        mesh=mesh,
        in_specs=placed,
        out_specs=(P(None, "gx", "gy", "gz"), P(None, "gx", "gy", "gz")),
        check_vma=False,
    )
```

profile of v0, /device:TPU:0, one launch (start us, length us, event | category | flops | bytes accessed | tf_op | source)
XLA Modules:
  0.0 80.7 jit_solution(64561961940944256)
XLA Ops:
  0.6 2.3 %pack.1 = f32[4,8,16,128]{3,2,1,0:T(8,128)} custom-call(f32[8]{0:T(128)} %mod_ref.1, f32[4,16,128]{2,1,0:T(8,128)} %cw_ref.1, f32[4,16,128]{2,1,0:T(8,128)} %wg_ref.1, s32[4,16,128]{2,1,0:T(8,128)} %mat_ref.1, f32[4,16,128]{2,1,0:T(8,128)} %mass_ref.1, s32[4,16,128]{2,1,0:T(8,128)} %pin_ref.1, f32[3,4,16,128]{3,2,1,0:T(8,128)} %pos_ref.1, ...), custom_call_target="tpu_custom_call" | custom-call | tf_op jit(solution)/shard_map/pack/pallas_call | solution.py:645
  3.0 2.4 %collective-permute-start = (f32[4,8,16,128]{3,2,1,0:T(8,128)}, f32[4,8,16,128]{3,2,1,0:T(8,128)S(1)}, u32[]{:S(2)}, u32[]{:S(2)}) collective-permute-start(f32[4,8,16,128]{3,2,1,0:T(8,128)} %pack.1), channel_id=1, source_target_pairs={{0,4},{1,5},{2,6},{3,7},{8,12},{9,13},{10,14},{11,15},{16,20},{17,... | collective-permute-start | bytes 786440 | tf_op jit(solution)/shard_map/ppermute | solution.py:654
  5.4 1.3 %collective-permute-done = f32[4,8,16,128]{3,2,1,0:T(8,128)S(1)} collective-permute-done((f32[4,8,16,128]{3,2,1,0:T(8,128)}, f32[4,8,16,128]{3,2,1,0:T(8,128)S(1)}, u32[]{:S(2)}, u32[]{:S(2)}) %collective-permute-start) | collective-permute-done | bytes 262176 | tf_op jit(solution)/shard_map/ppermute | solution.py:654
  6.7 1.0 %fusion.2 = (f32[1,8,32,128]{3,2,1,0:T(8,128)S(1)}, f32[8,32,128]{2,1,0:T(8,128)S(1)}, f32[8,32,128]{2,1,0:T(8,128)S(1)}, f32[8,32,128]{2,1,0:T(8,128)S(1)}) fusion(s32[]{:T(128)S(6)} %select_n.144, f32[4,8,16,128]{3,2,1,0:T(8,128)S(1)} %collective-permute-done, f32[4,8,16,128]{3,2,1,0:T(8,128)} %pack.1, s32[]{:T(128)S(6)} %select_n.147, s32[]{:T(128)S(6)} %select_n.150, ...), kind=kLoop, calls=%fused_computation.17 | loop fusion | flops 131072 | bytes 1048592 | tf_op jit(solution)/shard_map/concatenate | solution.py:655
  7.7 0.7 collective-permute-start.1
  8.3 0.7 collective-permute-start.2
  9.0 0.7 collective-permute-start.3
  9.7 0.0 collective-permute-done.1
  9.7 0.0 collective-permute-done.2
  9.7 0.0 collective-permute-done.3
  9.8 0.7 collective-permute-start.5
  10.5 0.7 collective-permute-start.4
  11.3 0.1 stack.80.idx_ref
  11.4 0.0 collective-permute-done.5.next_ref
  11.4 0.0 collective-permute-done.4.prev_ref
  11.4 29.2 %cycle.1 = f32[4,208,128]{2,1,0:T(8,128)S(1)} custom-call(s32[5]{0:T(128)S(1)} %stack.80.idx_ref, f32[4,8,32,128]{3,2,1,0:T(8,128)S(1)} %collective-permute-done.4.prev_ref, f32[4,8,32,128]{3,2,1,0:T(8,128)S(1)} %pad_maximum_fusion.own_ref, f32[4,8,32,128]{3,2,1,0:T(8,128)S(1)} %collective-permute-done.5.next_ref), custom_call_target="tpu_custom_call" | custom-call | tf_op jit(solution)/shard_map/cycle/pallas_call | solution.py:688
  40.6 0.7 collective-permute-start.8
  41.3 0.7 collective-permute-start.7
  41.9 0.7 collective-permute-start.6
  42.6 0.0 collective-permute-done.8
  42.6 0.0 collective-permute-done.7
  42.6 0.0 collective-permute-done.6
  42.8 1.3 %collective-permute-start.9 = (f32[4,104,128]{2,1,0:T(8,128)S(1)}, f32[4,104,128]{2,1,0:T(8,128)S(1)}, u32[]{:S(2)}, u32[]{:S(2)}) collective-permute-start(f32[4,104,128]{2,1,0:T(8,128)S(1)} %pad_maximum_fusion.5), channel_id=1, source_target_pairs={{4,0},{5,1},{6,2},{7,3},{12,8},{13,9},{14,10},{15,11},{20,16},{21,... | collective-permute-start | bytes 638984 | tf_op jit(solution)/shard_map/ppermute | solution.py:717
  44.1 0.7 stack.72.idx_ref
  44.8 0.7 pad_maximum_fusion.4.own_ref
  45.5 31.7 %collective-permute-done.9.got_ref = f32[4,104,128]{2,1,0:T(8,128)S(1)} collective-permute-done((f32[4,104,128]{2,1,0:T(8,128)S(1)}, f32[4,104,128]{2,1,0:T(8,128)S(1)}, u32[]{:S(2)}, u32[]{:S(2)}) %collective-permute-start.9) | collective-permute-done | bytes 213024 | tf_op jit(solution)/shard_map/ppermute | solution.py:717
  77.1 0.0 copy-start
  77.1 0.7 copy-done
  77.8 2.9 %unpack.1 = (f32[3,4,16,128]{3,2,1,0:T(8,128)}, f32[27,2,8,64]{3,2,1,0:T(8,128)}) custom-call(s32[5]{0:T(128)} %stack.72.idx_ref, f32[4,104,128]{2,1,0:T(8,128)} %pad_maximum_fusion.4.own_ref, f32[4,104,128]{2,1,0:T(8,128)} %copy-done, bf16[512,512]{1,0:T(8,128)(2,1)} %constant.106.clone.table_ref, bf16[512,512]{1,0:T(8,128)(2,1)} %constant.107.clone.coarse_ref), custom_call_target="tpu_custom_call" | custom-call | tf_op jit(solution)/shard_map/unpack/pallas_call | solution.py:719
  (7 shorter events, 0.1 us)
Async XLA Ops:
  3.0 3.7 %collective-permute-start = (f32[4,8,16,128]{3,2,1,0:T(8,128)}, f32[4,8,16,128]{3,2,1,0:T(8,128)S(1)}, u32[]{:S(2)}, u32[]{:S(2)}) collective-permute-start(f32[4,8,16,128]{3,2,1,0:T(8,128)} %pack.1), channel_id=1, source_target_pairs={{0,4},{1,5},{2,6},{3,7},{8,12},{9,13},{10,14},{11,15},{16,20},{17,... | collective-permute-start | bytes 786440 | tf_op jit(solution)/shard_map/ppermute | solution.py:654
  7.7 2.0 %collective-permute-start.1 = (f32[8,32,128]{2,1,0:T(8,128)S(1)}, f32[8,32,128]{2,1,0:T(8,128)S(1)}, u32[]{:S(2)}, u32[]{:S(2)}) collective-permute-start(f32[8,32,128]{2,1,0:T(8,128)S(1)} %get-tuple-element.3), channel_id=1, source_target_pairs={{4,12},{12,4},{20,28},{28,20},{5,13},{13,5},{21,29},{29,21},{6,14}... | collective-permute-start | bytes 393224 | tf_op jit(solution)/shard_map/ppermute | solution.py:662
  8.3 1.4 %collective-permute-start.2 = (f32[8,32,128]{2,1,0:T(8,128)S(1)}, f32[8,32,128]{2,1,0:T(8,128)S(1)}, u32[]{:S(2)}, u32[]{:S(2)}) collective-permute-start(f32[8,32,128]{2,1,0:T(8,128)S(1)} %get-tuple-element.4), channel_id=1, source_target_pairs={{4,20},{12,28},{20,4},{28,12},{5,21},{13,29},{21,5},{29,13},{6,22}... | collective-permute-start | bytes 393224 | tf_op jit(solution)/shard_map/ppermute | solution.py:662
  9.0 0.7 collective-permute-start.3
  9.8 1.6 %collective-permute-start.5 = (f32[4,8,32,128]{3,2,1,0:T(8,128)S(1)}, f32[4,8,32,128]{3,2,1,0:T(8,128)S(1)}, u32[]{:S(2)}, u32[]{:S(2)}) collective-permute-start(f32[4,8,32,128]{3,2,1,0:T(8,128)S(1)} %pad_maximum_fusion.own_ref), channel_id=1, source_target_pairs={{12,4},{28,12},{20,28},{21,20},{29,21},{13,29},{5,13},{6,5},{14,6}... | collective-permute-start | bytes 1572872 | tf_op jit(solution)/shard_map/ppermute | solution.py:670
  10.5 0.9 %collective-permute-start.4 = (f32[4,8,32,128]{3,2,1,0:T(8,128)S(1)}, f32[4,8,32,128]{3,2,1,0:T(8,128)S(1)}, u32[]{:S(2)}, u32[]{:S(2)}) collective-permute-start(f32[4,8,32,128]{3,2,1,0:T(8,128)S(1)} %pad_maximum_fusion.own_ref), channel_id=1, source_target_pairs={{4,12},{12,28},{28,20},{20,21},{21,29},{29,13},{13,5},{5,6},{6,14}... | collective-permute-start | bytes 1572872 | tf_op jit(solution)/shard_map/ppermute | solution.py:669
  40.6 2.0 %collective-permute-start.8 = (f32[208,128]{1,0:T(8,128)S(1)}, f32[208,128]{1,0:T(8,128)S(1)}, u32[]{:S(2)}, u32[]{:S(2)}) collective-permute-start(f32[208,128]{1,0:T(8,128)S(1)} %get-tuple-element.7), channel_id=1, source_target_pairs={{4,28},{12,20},{20,12},{28,4},{5,29},{13,21},{21,13},{29,5},{6,30}... | collective-permute-start | bytes 319496 | tf_op jit(solution)/shard_map/ppermute | solution.py:707
  41.3 1.4 %collective-permute-start.7 = (f32[208,128]{1,0:T(8,128)S(1)}, f32[208,128]{1,0:T(8,128)S(1)}, u32[]{:S(2)}, u32[]{:S(2)}) collective-permute-start(f32[208,128]{1,0:T(8,128)S(1)} %get-tuple-element.8), channel_id=1, source_target_pairs={{4,20},{12,28},{20,4},{28,12},{5,21},{13,29},{21,5},{29,13},{6,22}... | collective-permute-start | bytes 319496 | tf_op jit(solution)/shard_map/ppermute | solution.py:707
  41.9 0.7 collective-permute-start.6
  42.8 34.4 %collective-permute-start.9 = (f32[4,104,128]{2,1,0:T(8,128)S(1)}, f32[4,104,128]{2,1,0:T(8,128)S(1)}, u32[]{:S(2)}, u32[]{:S(2)}) collective-permute-start(f32[4,104,128]{2,1,0:T(8,128)S(1)} %pad_maximum_fusion.5), channel_id=1, source_target_pairs={{4,0},{5,1},{6,2},{7,3},{12,8},{13,9},{14,10},{15,11},{20,16},{21,... | collective-permute-start | bytes 638984 | tf_op jit(solution)/shard_map/ppermute | solution.py:717
  77.1 0.7 copy-start
where the time goes:
time: 81.1 us; the launch traced here: 80.7 us
  Pallas kernels  34.4 us (42%)
  waiting for transfers between devices  33 us (41%)
  starting transfers between devices  9.05 us (11%)
  other arithmetic  1.77 us (2%)
  local copies, waits for them, and re-layouts  1.49 us (2%)
  between operations  1.04 us (1%)
    ppermute x1, waiting for transfers between devices, shards_by_slab(): got = lax.ppermute(half(0), 'gy', [(1, 0)])  31.7 us
    pallas_call x1, Pallas kernels, shards_by_slab(): pl.pallas_call(cycle_kernel, out_shape=jax.ShapeDtypeStruct((4, 208, LANE...  29.2 us
    pallas_call x1, Pallas kernels, shards_by_slab(): pl.pallas_call(unpack_kernel, out_shape=[jax.ShapeDtypeStruct(positions.s...  2.85 us
    ppermute x1, starting transfers between devices, shards_by_slab(): lower = lax.ppermute(packed, 'gy', [(0, 1)])  2.36 us
    pallas_call x1, Pallas kernels, shards_by_slab(): pl.pallas_call(pack_kernel, out_shape=jax.ShapeDtypeStruct((4, 8, 16, LAN...  2.34 us
    ppermute x3, starting transfers between devices, shards_by_slab(): own.append(lax.ppermute(by_partner[j], ('gx', 'gy'), pairs))  2.01 us
    ppermute x3, starting transfers between devices, shards_by_slab(): back.append(lax.ppermute(message[j], ('gx', 'gy'), pairs))  2 us
  transfers between devices with their start and end apart: 10, of which 2 were waited for; matrix products, arithmetic and copies ran while one was open for 2% of the time, Pallas kernels for 0%

commit v1 on v0

--- a/solution.py
+++ b/solution.py
@@ -331,14 +331,8 @@
             out_ref[t, f] = moved[16 * f:16 * f + 16, 128 * t:128 * t + 128]
 
 
-def unpack_kernel(idx_ref, own_ref, got_ref, table_ref, coarse_ref, iterate_ref, level_ref):
-    take_own = idx_ref[0] == 1
-
-    def block(t):
-        j = idx_ref[1 + t]
-        return jnp.where(take_own, own_ref[j], got_ref[j])
-
-    whole = jnp.concatenate([block(t) for t in range(4)], axis=-1)
+def unpack_kernel(idx_ref, in_ref, table_ref, coarse_ref, iterate_ref, level_ref):
+    whole = jnp.concatenate([in_ref[idx_ref[t]] for t in range(4)], axis=-1)
     fine = reorder(whole[:48], table_ref[...])
     for c in range(3):
         for x in range(4):
@@ -383,7 +377,7 @@
 
 
 def triple_product(src, mid_a, mid_b, dst, n):
-    half = n // 2
+    unroll = n == 2
 
     def pass_x(j, carry):
         parts = [[src[9 * f + j, i] for i in range(n)] for f in range(3)]
@@ -393,7 +387,7 @@
                 mid_a[9 * c + j, i] = trio[c]
         return carry
 
-    lax.fori_loop(0, 9, pass_x, 0)
+    lax.fori_loop(0, 9, pass_x, 0, unroll=unroll)
 
     def pass_y(j, carry):
         base = 9 * (j // 3) + j % 3
@@ -404,7 +398,7 @@
                 mid_b[base + 3 * c, :, i] = trio[c]
         return carry
 
-    lax.fori_loop(0, 9, pass_y, 0)
+    lax.fori_loop(0, 9, pass_y, 0, unroll=unroll)
 
     def pass_z(j, carry):
         parts = [[mid_b[3 * j + f, :, :, i] for i in range(n)] for f in range(3)]
@@ -414,7 +408,7 @@
                 dst[3 * j + c, :, :, i] = trio[c]
         return carry
 
-    lax.fori_loop(0, 9, pass_z, 0)
+    lax.fori_loop(0, 9, pass_z, 0, unroll=unroll)
 
 
 def sweep(level, field, n, store, skip_faces):
@@ -437,10 +431,7 @@
                 store(c, x, y, z, sums[c][z])
         return carry
 
-    if n == 1:
-        body(0, 0)
-    else:
-        lax.fori_loop(0, n * n, body, 0)
+    lax.fori_loop(0, n * n, body, 0, unroll=n < 4)
 
 
 def relax_into(level, weight, rhs, src, dst, n, skip_faces=False):
@@ -468,7 +459,7 @@
                     coarse_rhs[c, i, j, k] = 0.5 * (line[2 * k] + line[2 * k + 2]) + line[2 * k + 1]
         return carry
 
-    lax.fori_loop(0, 3, body, 0)
+    lax.fori_loop(0, 3, body, 0, unroll=n < 4)
 
 
 def add_prolonged(coarse, fine, inside, half):
@@ -486,7 +477,7 @@
                     fine[c, 1 + x, 1 + y, 1 + z] += jnp.where(inside, value, 0.0)
         return carry
 
-    lax.fori_loop(0, 3, body, 0)
+    lax.fori_loop(0, 3, body, 0, unroll=half < 2)
 
 
 def fill_all(ref, n):
@@ -494,7 +485,7 @@
         fill_both(ref.at[c], n)
         return carry
 
-    lax.fori_loop(0, 3, body, 0)
+    lax.fori_loop(0, 3, body, 0, unroll=n < 4)
 
 
 def cycle_kernel(
@@ -651,31 +642,41 @@
     )(modulus, cell_weight, weight_grad, material, node_mass, pinned, positions, forces,
       jnp.asarray(table, jnp.bfloat16))
 
-    lower = lax.ppermute(packed, "gy", [(0, 1)])
-    block = jnp.concatenate([lower, packed], axis=2)
-    by_partner = [
-        lax.dynamic_index_in_dim(block, slab_place(gx ^ j, gz), 0, keepdims=False) for j in range(4)
-    ]
-    own = [by_partner[0]]
+    place = slab_place(gx, gz)
+    index = 4 * gz + place
+    mine = [lax.dynamic_index_in_dim(packed, slab_place(gx ^ j, gz), 0, keepdims=False) for j in range(4)]
     for j in range(1, 4):
-        pairs = [(2 * i + 1, 2 * (i ^ j) + 1) for i in range(4)]
-        own.append(lax.ppermute(by_partner[j], ("gx", "gy"), pairs))
-    own = jnp.stack(own)
-
-    chain = [(slab_owner(place, z) * 2 + 1) * 4 + z for z in range(4) for place in range(4)]
-    ahead = list(zip(chain[:-1], chain[1:]))
-    behind = [(b, a) for a, b in ahead]
-    everywhere = ("gx", "gy", "gz")
-    before = lax.ppermute(own, everywhere, ahead)
-    after = lax.ppermute(own, everywhere, behind)
-
-    place = slab_place(gx, gz)
+        mine[j] = lax.ppermute(mine[j], "gx", [(i, i ^ j) for i in range(4)])
+    mine = jnp.stack(mine)
+
+    def swap_in_chain(first):
+        pairs = []
+        for core in range(2):
+            chain = [(slab_owner(at, z) * 2 + core) * 4 + z for z in range(4) for at in range(4)]
+            for at in range(first, 15, 2):
+                pairs += [(chain[at], chain[at + 1]), (chain[at + 1], chain[at])]
+            if first:
+                pairs += [(chain[end], chain[end] ^ 4) for end in (0, 15)]
+        return lax.ppermute(mine, ("gx", "gy", "gz"), pairs)
+
+    even, odd = swap_in_chain(0), swap_in_chain(1)
+
+    def both_halves(half, present):
+        other = lax.ppermute(half, "gy", [(0, 1), (1, 0)])
+        rows = jnp.concatenate([jnp.where(gy == 0, half, other), jnp.where(gy == 0, other, half)], axis=2)
+        return jnp.where(present, rows, 0.0)
+
+    odd_place = index % 2 == 1
+    own = both_halves(mine, True)
+    even = both_halves(even, True)
+    odd = both_halves(odd, (index > 0) & (index < 15))
+    before = jnp.where(odd_place, even, odd)
+    after = jnp.where(odd_place, odd, even)
 
     def owner_of(place, z):
         order = jnp.where(z % 2 == 0, place, 3 - place)
         return jnp.where(order < 2, order, 5 - order)
 
-    index = 4 * gz + place
     gx_before = owner_of((index - 1) % 4, (index - 1) // 4)
     gx_after = owner_of((index + 1) % 4, (index + 1) // 4)
     scalars = jnp.stack(
@@ -701,31 +702,29 @@
         name="cycle",
     )(scalars, before, own, after)
 
-    back = [message[0]]
-    for j in range(1, 4):
-        pairs = [(2 * i + 1, 2 * (i ^ j) + 1) for i in range(4)]
-        back.append(lax.ppermute(message[j], ("gx", "gy"), pairs))
-    back = jnp.stack(back)
-    fine = back[:, :96].reshape(4, 3, 2, 16, LANES)
-    coarse = back[:, 96:].reshape(4, 7, 2, 8, LANES)
+    fine = message[:, :96].reshape(4, 3, 2, 16, LANES)
+    coarse = message[:, 96:].reshape(4, 7, 2, 8, LANES)
 
     def half(side):
         return jnp.concatenate(
             [fine[:, :, side].reshape(4, 48, LANES), coarse[:, :, side].reshape(4, 56, LANES)], axis=1
         )
 
-    got = lax.ppermute(half(0), "gy", [(1, 0)])
-    scalars = jnp.stack([gy] + [gx ^ owner_of(t, gz) for t in range(4)]).astype(jnp.int32)
+    message = jnp.where(gy == 0, half(0), half(1))
+    back = [message[0]]
+    for j in range(1, 4):
+        back.append(lax.ppermute(message[j], "gx", [(i, i ^ j) for i in range(4)]))
+    scalars = jnp.stack([gx ^ owner_of(t, gz) for t in range(4)]).astype(jnp.int32)
     return pl.pallas_call(
         unpack_kernel,
         out_shape=[
             jax.ShapeDtypeStruct(positions.shape, f32),
             jax.ShapeDtypeStruct((27, 2, 8, 64), f32),
         ],
-        in_specs=[smem] + vmem_specs(4),
+        in_specs=[smem] + vmem_specs(3),
         out_specs=vmem_specs(2),
         name="unpack",
-    )(scalars, half(1), got, jnp.asarray(unpack_table(), jnp.bfloat16), jnp.asarray(coarse_table(), jnp.bfloat16))
+    )(scalars, jnp.stack(back), jnp.asarray(unpack_table(), jnp.bfloat16), jnp.asarray(coarse_table(), jnp.bfloat16))
 
 
 def unpack_table():

time: 81.1 us -> 58.6 us (0.72)
  waiting for transfers between devices: 33 us -> 13.3 us
  Pallas kernels: 34.4 us -> 29 us
  starting transfers between devices: 9.05 us -> 10.8 us
  local copies, waits for them, and re-layouts: 1.49 us -> 2.75 us
    ppermute x10 -> x11, waiting for transfers between devices: 33 us -> 13.3 us  [the longest x2 6.08 us: swap_in_chain(): return lax.ppermute(mine, ('gx', 'gy', 'gz'), pairs)]
    pallas_call x1, Pallas kernels: 29.2 us -> 24 us  [shards_by_slab(): pl.pallas_call(cycle_kernel, out_shape=jax.ShapeDtypeStruct((4, 208, LANE...]
    ppermute x10 -> x11, starting transfers between devices: 9.05 us -> 10.8 us  [the longest x3 4.6 us: shards_by_slab(): mine[j] = lax.ppermute(mine[j], 'gx', [(i, i ^ j) for i in range(4)])]
    concatenate x3 -> x1, other arithmetic: 1.7 us -> 0.06 us  [both_halves(): jnp.concatenate([jnp.where(gy == 0, half, other), jnp.where(gy == 0, othe...]
    another operation x2 -> x3, other arithmetic: 0.05 us -> 1.33 us  [the longest x1 0.69 us: shards_by_slab(): jnp.stack(back)]
    dynamic_slice x0 -> x1, local copies, waits for them, and re-layouts: none -> 0.95 us  [shards_by_slab(): lax.dynamic_index_in_dim(packed, slab_place(gx ^ j, gz), 0, keepdims=False)]
    slice x0 -> x3, local copies, waits for them, and re-layouts: none -> 0.94 us  [the longest x2 0.92 us: shards_by_slab(): coarse = message[:, 96:].reshape(4, 7, 2, 8, LANES)]
  transfers between devices with their start and end apart: 10 -> 11, of which waited for: 2 -> 7; matrix products, arithmetic and copies ran while one was open for 2% -> 1% of each run, Pallas kernels for 0% -> 0%
where the time goes in v1:
time: 58.6 us; the launch traced here: 58.4 us
  Pallas kernels  29 us (49%)
  waiting for transfers between devices  13.3 us (23%)
  starting transfers between devices  10.8 us (18%)
  local copies, waits for them, and re-layouts  2.75 us (5%)
  other arithmetic  1.67 us (3%)
  between operations  0.82 us (1%)
    pallas_call x1, Pallas kernels, shards_by_slab(): pl.pallas_call(cycle_kernel, out_shape=jax.ShapeDtypeStruct((4, 208, LANE...  24 us
    ppermute x2, waiting for transfers between devices, swap_in_chain(): return lax.ppermute(mine, ('gx', 'gy', 'gz'), pairs)  6.08 us
    ppermute x3, starting transfers between devices, shards_by_slab(): mine[j] = lax.ppermute(mine[j], 'gx', [(i, i ^ j) for i in range(4)])  4.6 us
    ppermute x3, waiting for transfers between devices, shards_by_slab(): mine[j] = lax.ppermute(mine[j], 'gx', [(i, i ^ j) for i in range(4)])  4.13 us
    ppermute x3, starting transfers between devices, shards_by_slab(): back.append(lax.ppermute(message[j], 'gx', [(i, i ^ j) for i in range(4)]))  3.55 us
    pallas_call x1, Pallas kernels, shards_by_slab(): pl.pallas_call(unpack_kernel, out_shape=[jax.ShapeDtypeStruct(positions.s...  2.7 us
    pallas_call x1, Pallas kernels, shards_by_slab(): pl.pallas_call(pack_kernel, out_shape=jax.ShapeDtypeStruct((4, 8, 16, LAN...  2.33 us
    ppermute x2, starting transfers between devices, swap_in_chain(): return lax.ppermute(mine, ('gx', 'gy', 'gz'), pairs)  2.11 us
  transfers between devices with their start and end apart: 11, of which 7 were waited for; matrix products, arithmetic and copies ran while one was open for 1% of the time, Pallas kernels for 0%

profile of v1, /device:TPU:0, one launch (start us, length us, event | category | flops | bytes accessed | tf_op | source)
XLA Modules:
  0.0 58.4 jit_solution(13714032170908456820)
XLA Ops:
  0.7 2.3 %pack.1 = f32[4,8,16,128]{3,2,1,0:T(8,128)} custom-call(f32[8]{0:T(128)} %mod_ref.1, f32[4,16,128]{2,1,0:T(8,128)} %cw_ref.1, f32[4,16,128]{2,1,0:T(8,128)} %wg_ref.1, s32[4,16,128]{2,1,0:T(8,128)} %mat_ref.1, f32[4,16,128]{2,1,0:T(8,128)} %mass_ref.1, s32[4,16,128]{2,1,0:T(8,128)} %pin_ref.1, f32[3,4,16,128]{3,2,1,0:T(8,128)} %pos_ref.1, ...), custom_call_target="tpu_custom_call" | custom-call | tf_op jit(solution)/shard_map/pack/pallas_call | solution.py:636
  3.0 1.0 %constant_dynamic-slice_fusion = (f32[1,8,16,128]{3,2,1,0:T(8,128)S(1)}, f32[8,16,128]{2,1,0:T(8,128)S(1)}, f32[8,16,128]{2,1,0:T(8,128)S(1)}, f32[8,16,128]{2,1,0:T(8,128)S(1)}) fusion(f32[4,8,16,128]{3,2,1,0:T(8,128)} %pack.1, s32[]{:T(128)S(6)} %select_n.214, s32[]{:T(128)S(6)} %select_n.223, s32[]{:T(128)S(6)} %select_n.220, s32[]{:T(128)S(6)} %select_n.217), kind=kLoop, calls=%fused_computation.22 | loop fusion | bytes 524304 | tf_op jit(solution)/shard_map/jit(dynamic_index_in_dim)/dynamic_slice | solution.py:647
  4.0 4.0 %collective-permute-start.2 = (f32[8,16,128]{2,1,0:T(8,128)S(1)}, f32[8,16,128]{2,1,0:T(8,128)S(1)}, u32[]{:S(2)}, u32[]{:S(2)}) collective-permute-start(f32[8,16,128]{2,1,0:T(8,128)S(1)} %get-tuple-element.11), channel_id=1, source_target_pairs={{0,24},{8,16},{16,8},{24,0},{1,25},{9,17},{17,9},{25,1},{2,26},{10... | collective-permute-start | bytes 196616 | tf_op jit(solution)/shard_map/ppermute | solution.py:649
  8.0 0.5 collective-permute-start.1
  8.5 0.1 collective-permute-start
  8.6 1.6 %collective-permute-done.2 = f32[8,16,128]{2,1,0:T(8,128)S(1)} collective-permute-done((f32[8,16,128]{2,1,0:T(8,128)S(1)}, f32[8,16,128]{2,1,0:T(8,128)S(1)}, u32[]{:S(2)}, u32[]{:S(2)}) %collective-permute-start.2) | collective-permute-done | bytes 65568 | tf_op jit(solution)/shard_map/ppermute | solution.py:649
  10.2 2.0 %collective-permute-done.1 = f32[8,16,128]{2,1,0:T(8,128)S(1)} collective-permute-done((f32[8,16,128]{2,1,0:T(8,128)S(1)}, f32[8,16,128]{2,1,0:T(8,128)S(1)}, u32[]{:S(2)}, u32[]{:S(2)}) %collective-permute-start.1) | collective-permute-done | bytes 65568 | tf_op jit(solution)/shard_map/ppermute | solution.py:649
  12.2 0.5 collective-permute-done
  12.7 0.1 collective-permute-start.5
  12.8 2.0 %collective-permute-start.3 = (f32[4,8,16,128]{3,2,1,0:T(8,128)S(1)}, f32[4,8,16,128]{3,2,1,0:T(8,128)S(1)}, u32[]{:S(2)}, u32[]{:S(2)}) collective-permute-start(f32[4,8,16,128]{3,2,1,0:T(8,128)S(1)} %pad_maximum_fusion.2), channel_id=1, source_target_pairs={{0,8},{8,0},{24,16},{16,24},{17,25},{25,17},{9,1},{1,9},{2,10},{10... | collective-permute-start | bytes 786440 | tf_op jit(solution)/shard_map/ppermute | solution.py:660
  14.9 0.0 collective-permute-start.7
  14.9 0.1 stack.76.idx_ref
  15.0 0.0 collective-permute-done.5
  15.0 0.5 collective-permute-start.6
  15.5 6.1 %collective-permute-done.3 = f32[4,8,16,128]{3,2,1,0:T(8,128)S(1)} collective-permute-done((f32[4,8,16,128]{3,2,1,0:T(8,128)S(1)}, f32[4,8,16,128]{3,2,1,0:T(8,128)S(1)}, u32[]{:S(2)}, u32[]{:S(2)}) %collective-permute-start.3) | collective-permute-done | bytes 262176 | tf_op jit(solution)/shard_map/ppermute | solution.py:660
  21.6 0.0 collective-permute-start.4
  21.6 0.0 collective-permute-done.7
  21.6 0.1 pad_maximum_fusion.1.own_ref
  21.7 0.0 collective-permute-done.6
  21.7 1.4 %collective-permute-done.4 = f32[4,8,16,128]{3,2,1,0:T(8,128)S(1)} collective-permute-done((f32[4,8,16,128]{3,2,1,0:T(8,128)S(1)}, f32[4,8,16,128]{3,2,1,0:T(8,128)S(1)}, u32[]{:S(2)}, u32[]{:S(2)}) %collective-permute-start.4) | collective-permute-done | bytes 262176 | tf_op jit(solution)/shard_map/ppermute | solution.py:665
  23.1 0.1 fusion
  23.3 24.0 %cycle.1 = f32[4,208,128]{2,1,0:T(8,128)S(1)} custom-call(s32[5]{0:T(128)S(1)} %stack.76.idx_ref, f32[4,8,32,128]{3,2,1,0:T(8,128)S(1)} %get-tuple-element.3.prev_ref, f32[4,8,32,128]{3,2,1,0:T(8,128)S(1)} %pad_maximum_fusion.1.own_ref, f32[4,8,32,128]{3,2,1,0:T(8,128)S(1)} %get-tuple-element.2.next_ref), custom_call_target="tpu_custom_call" | custom-call | tf_op jit(solution)/shard_map/cycle/pallas_call | solution.py:689
  47.3 0.0 copy-start
  47.3 0.7 %copy-done = f32[4,208,128]{2,1,0:T(8,128)} copy-done((f32[4,208,128]{2,1,0:T(8,128)}, f32[4,208,128]{2,1,0:T(8,128)S(1)}, u32[]{:S(2)}) %copy-start) | copy-done | bytes 426008
  48.0 0.0 slice-start
  48.1 0.9 %slice-done = f32[4,112,128]{2,1,0:T(8,128)S(1)} async-done(((f32[4,208,128]{2,1,0:T(8,128)}), f32[4,112,128]{2,1,0:T(8,128)S(1)}, s32[]{:S(2)}) %slice-start) | async-done | bytes 229400 | tf_op jit(solution)/shard_map/slice | solution.py:706
  49.0 0.5 collective-permute-start.10
  49.5 1.3 %collective-permute-start.9 = (f32[104,128]{1,0:T(8,128)S(1)}, f32[104,128]{1,0:T(8,128)S(1)}, u32[]{:S(2)}, u32[]{:S(2)}) collective-permute-start(f32[104,128]{1,0:T(8,128)S(1)} %get-tuple-element.18), channel_id=1, source_target_pairs={{0,16},{8,24},{16,0},{24,8},{1,17},{9,25},{17,1},{25,9},{2,18},{10... | collective-permute-start | bytes 159752 | tf_op jit(solution)/shard_map/ppermute | solution.py:716
  50.8 1.8 %collective-permute-start.8 = (f32[104,128]{1,0:T(8,128)S(1)}, f32[104,128]{1,0:T(8,128)S(1)}, u32[]{:S(2)}, u32[]{:S(2)}) collective-permute-start(f32[104,128]{1,0:T(8,128)S(1)} %get-tuple-element.19), channel_id=1, source_target_pairs={{0,8},{8,0},{16,24},{24,16},{1,9},{9,1},{17,25},{25,17},{2,10},{10... | collective-permute-start | bytes 159752 | tf_op jit(solution)/shard_map/ppermute | solution.py:716
  52.6 0.6 %pad_add_fusion.idx_ref = s32[4]{0:T(128)} fusion(s32[1]{0:T(128)} %bitcast.3, s32[1]{0:T(128)} %bitcast.2, s32[1]{0:T(128)} %bitcast.1, s32[1]{0:T(128)} %bitcast), kind=kLoop, calls=%fused_computation.23 | loop fusion | flops 12 | bytes 32 | tf_op jit(solution)/shard_map/stack | solution.py:717
  53.2 1.2 %collective-permute-done.10 = f32[104,128]{1,0:T(8,128)S(1)} collective-permute-done((f32[104,128]{1,0:T(8,128)S(1)}, f32[104,128]{1,0:T(8,128)S(1)}, u32[]{:S(2)}, u32[]{:S(2)}) %collective-permute-start.10) | collective-permute-done | bytes 53280 | tf_op jit(solution)/shard_map/ppermute | solution.py:716
  54.5 0.0 collective-permute-done.9
  54.5 0.5 collective-permute-done.8
  55.0 0.7 %pad_maximum_fusion.3.in_ref = f32[4,104,128]{2,1,0:T(8,128)} fusion(f32[1,104,128]{2,1,0:T(8,128)S(1)} %bitcast.53, f32[1,104,128]{2,1,0:T(8,128)S(1)} %bitcast.54, f32[1,104,128]{2,1,0:T(8,128)S(1)} %bitcast.55, f32[1,104,128]{2,1,0:T(8,128)S(1)} %get-tuple-element.16), kind=kLoop, calls=%fused_computation.7 | loop fusion | flops 159744 | bytes 425984 | tf_op jit(solution)/shard_map/stack | solution.py:727
  55.7 2.7 %unpack.1 = (f32[3,4,16,128]{3,2,1,0:T(8,128)}, f32[27,2,8,64]{3,2,1,0:T(8,128)}) custom-call(s32[4]{0:T(128)} %pad_add_fusion.idx_ref, f32[4,104,128]{2,1,0:T(8,128)} %pad_maximum_fusion.3.in_ref, bf16[512,512]{1,0:T(8,128)(2,1)} %constant.113.clone.table_ref, bf16[512,512]{1,0:T(8,128)(2,1)} %constant.114.clone.coarse_ref), custom_call_target="tpu_custom_call" | custom-call | tf_op jit(solution)/shard_map/unpack/pallas_call | solution.py:718
  (9 shorter events, 0.2 us)
Async XLA Ops:
  4.0 6.2 %collective-permute-start.2 = (f32[8,16,128]{2,1,0:T(8,128)S(1)}, f32[8,16,128]{2,1,0:T(8,128)S(1)}, u32[]{:S(2)}, u32[]{:S(2)}) collective-permute-start(f32[8,16,128]{2,1,0:T(8,128)S(1)} %get-tuple-element.11), channel_id=1, source_target_pairs={{0,24},{8,16},{16,8},{24,0},{1,25},{9,17},{17,9},{25,1},{2,26},{10... | collective-permute-start | bytes 196616 | tf_op jit(solution)/shard_map/ppermute | solution.py:649
  8.0 4.3 %collective-permute-start.1 = (f32[8,16,128]{2,1,0:T(8,128)S(1)}, f32[8,16,128]{2,1,0:T(8,128)S(1)}, u32[]{:S(2)}, u32[]{:S(2)}) collective-permute-start(f32[8,16,128]{2,1,0:T(8,128)S(1)} %get-tuple-element.12), channel_id=1, source_target_pairs={{0,16},{8,24},{16,0},{24,8},{1,17},{9,25},{17,1},{25,9},{2,18},{10... | collective-permute-start | bytes 196616 | tf_op jit(solution)/shard_map/ppermute | solution.py:649
  8.5 4.3 %collective-permute-start = (f32[8,16,128]{2,1,0:T(8,128)S(1)}, f32[8,16,128]{2,1,0:T(8,128)S(1)}, u32[]{:S(2)}, u32[]{:S(2)}) collective-permute-start(f32[8,16,128]{2,1,0:T(8,128)S(1)} %get-tuple-element.13), channel_id=1, source_target_pairs={{0,8},{8,0},{16,24},{24,16},{1,9},{9,1},{17,25},{25,17},{2,10},{10... | collective-permute-start | bytes 196616 | tf_op jit(solution)/shard_map/ppermute | solution.py:649
  12.7 2.2 %collective-permute-start.5 = (f32[4,8,16,128]{3,2,1,0:T(8,128)S(1)}, f32[4,8,16,128]{3,2,1,0:T(8,128)S(1)}, u32[]{:S(2)}, u32[]{:S(2)}) collective-permute-start(f32[4,8,16,128]{3,2,1,0:T(8,128)S(1)} %pad_maximum_fusion.2), channel_id=1, source_target_pairs={{8,24},{24,8},{16,17},{17,16},{25,9},{9,25},{1,2},{2,1},{10,26},{2... | collective-permute-start | bytes 786440 | tf_op jit(solution)/shard_map/ppermute | solution.py:660
  12.8 8.7 %collective-permute-start.3 = (f32[4,8,16,128]{3,2,1,0:T(8,128)S(1)}, f32[4,8,16,128]{3,2,1,0:T(8,128)S(1)}, u32[]{:S(2)}, u32[]{:S(2)}) collective-permute-start(f32[4,8,16,128]{3,2,1,0:T(8,128)S(1)} %pad_maximum_fusion.2), channel_id=1, source_target_pairs={{0,8},{8,0},{24,16},{16,24},{17,25},{25,17},{9,1},{1,9},{2,10},{10... | collective-permute-start | bytes 786440 | tf_op jit(solution)/shard_map/ppermute | solution.py:660
  14.9 6.7 %collective-permute-start.7 = (f32[4,8,16,128]{3,2,1,0:T(8,128)S(1)}, f32[4,8,16,128]{3,2,1,0:T(8,128)S(1)}, u32[]{:S(2)}, u32[]{:S(2)}) collective-permute-start(f32[4,8,16,128]{3,2,1,0:T(8,128)S(1)} %pad_maximum_fusion.2), channel_id=1, source_target_pairs={{0,4},{4,0},{1,5},{5,1},{2,6},{6,2},{3,7},{7,3},{8,12},{12,8},{9,1... | collective-permute-start | bytes 786440 | tf_op jit(solution)/shard_map/ppermute | solution.py:665
  15.0 6.7 %collective-permute-start.6 = (f32[4,8,16,128]{3,2,1,0:T(8,128)S(1)}, f32[4,8,16,128]{3,2,1,0:T(8,128)S(1)}, u32[]{:S(2)}, u32[]{:S(2)}) collective-permute-start(f32[4,8,16,128]{3,2,1,0:T(8,128)S(1)} %collective-permute-done.5), channel_id=1, source_target_pairs={{0,4},{4,0},{1,5},{5,1},{2,6},{6,2},{3,7},{7,3},{8,12},{12,8},{9,1... | collective-permute-start | bytes 786440 | tf_op jit(solution)/shard_map/ppermute | solution.py:665
  21.6 1.5 %collective-permute-start.4 = (f32[4,8,16,128]{3,2,1,0:T(8,128)S(1)}, f32[4,8,16,128]{3,2,1,0:T(8,128)S(1)}, u32[]{:S(2)}, u32[]{:S(2)}) collective-permute-start(f32[4,8,16,128]{3,2,1,0:T(8,128)S(1)} %collective-permute-done.3), channel_id=1, source_target_pairs={{0,4},{4,0},{1,5},{5,1},{2,6},{6,2},{3,7},{7,3},{8,12},{12,8},{9,1... | collective-permute-start | bytes 786440 | tf_op jit(solution)/shard_map/ppermute | solution.py:665
  47.3 0.8 %copy-start = (f32[4,208,128]{2,1,0:T(8,128)}, f32[4,208,128]{2,1,0:T(8,128)S(1)}, u32[]{:S(2)}) copy-start(f32[4,208,128]{2,1,0:T(8,128)S(1)} %cycle.1) | copy-start | bytes 1277956
  48.0 0.9 %slice-start = ((f32[4,208,128]{2,1,0:T(8,128)}), f32[4,112,128]{2,1,0:T(8,128)S(1)}, s32[]{:S(2)}) async-start(f32[4,208,128]{2,1,0:T(8,128)} %copy-done), calls=%async_computation | async-start | bytes 458752 | tf_op jit(solution)/shard_map/slice | solution.py:706
  49.0 5.4 %collective-permute-start.10 = (f32[104,128]{1,0:T(8,128)S(1)}, f32[104,128]{1,0:T(8,128)S(1)}, u32[]{:S(2)}, u32[]{:S(2)}) collective-permute-start(f32[104,128]{1,0:T(8,128)S(1)} %get-tuple-element.17), channel_id=1, source_target_pairs={{0,24},{8,16},{16,8},{24,0},{1,25},{9,17},{17,9},{25,1},{2,26},{10... | collective-permute-start | bytes 159752 | tf_op jit(solution)/shard_map/ppermute | solution.py:716
  49.5 4.9 %collective-permute-start.9 = (f32[104,128]{1,0:T(8,128)S(1)}, f32[104,128]{1,0:T(8,128)S(1)}, u32[]{:S(2)}, u32[]{:S(2)}) collective-permute-start(f32[104,128]{1,0:T(8,128)S(1)} %get-tuple-element.18), channel_id=1, source_target_pairs={{0,16},{8,24},{16,0},{24,8},{1,17},{9,25},{17,1},{25,9},{2,18},{10... | collective-permute-start | bytes 159752 | tf_op jit(solution)/shard_map/ppermute | solution.py:716
  50.8 4.1 %collective-permute-start.8 = (f32[104,128]{1,0:T(8,128)S(1)}, f32[104,128]{1,0:T(8,128)S(1)}, u32[]{:S(2)}, u32[]{:S(2)}) collective-permute-start(f32[104,128]{1,0:T(8,128)S(1)} %get-tuple-element.19), channel_id=1, source_target_pairs={{0,8},{8,0},{16,24},{24,16},{1,9},{9,1},{17,25},{25,17},{2,10},{10... | collective-permute-start | bytes 159752 | tf_op jit(solution)/shard_map/ppermute | solution.py:716

commit v2 on v1

--- a/solution.py
+++ b/solution.py
@@ -267,7 +267,7 @@
 
 
 def swap_groups(parts, unit):
-    group = lane_ids(TILE) // unit
+    group = lane_ids(parts[0].shape) // unit
     parts = list(parts)
     for bit in (1, 2):
         low = (group & bit) == 0
@@ -279,44 +279,11 @@
     return parts
 
 
-def three_pieces(x):
-    first = x.astype(jnp.bfloat16)
-    rest = x - first.astype(jnp.float32)
-    second = rest.astype(jnp.bfloat16)
-    third = (rest - second.astype(jnp.float32)).astype(jnp.bfloat16)
-    return first, second, third
-
-
-def reorder(x, table):
-    total = None
-    for piece in three_pieces(x):
-        term = jnp.dot(piece, table, preferred_element_type=jnp.float32)
-        total = term if total is None else total + term
-    return total
-
-
-def pack_table():
-    table = np.zeros((512, 512), np.float32)
-    for xp in range(4):
-        for z in range(128):
-            t, q, p = z // 32, (z % 32) // 4, z % 4
-            table[xp * 128 + z, t * 128 + xp * 32 + p * 8 + q] = 1.0
-    return table
-
-
-def coarse_table():
-    table = np.zeros((512, 512), np.float32)
-    for t in range(4):
-        for o in range(4):
-            for xp in range(2):
-                for zp in range(2):
-                    for zq in range(8):
-                        src = t * 128 + o * 32 + xp * 16 + zp * 8 + zq
-                        table[src, o * 128 + xp * 64 + 16 * t + 2 * zq + zp] = 1.0
-    return table
-
-
-def pack_kernel(mod_ref, cw_ref, wg_ref, mat_ref, mass_ref, pin_ref, pos_ref, force_ref, table_ref, out_ref):
+def pick_lanes(x, source):
+    return jnp.take_along_axis(x, jnp.broadcast_to(source, x.shape), axis=-1)
+
+
+def pack_kernel(place_ref, mod_ref, cw_ref, wg_ref, mat_ref, mass_ref, pin_ref, pos_ref, force_ref, out_ref):
     material = mat_ref[...]
     lookup = jnp.zeros(material.shape, jnp.float32)
     for index in range(mod_ref.shape[0]):
@@ -324,24 +291,32 @@
     stiff = cw_ref[...] * jnp.exp(-LEARN_RATE * wg_ref[...]) * lookup
     mass = mass_ref[...] + PIN_WEIGHT * pin_ref[...].astype(jnp.float32)
     fields = [stiff, mass] + [pos_ref[c] for c in range(3)] + [force_ref[c] for c in range(3)]
-    rows = [jnp.concatenate([field[x] for x in range(4)], axis=-1) for field in fields]
-    moved = reorder(jnp.concatenate(rows, axis=0), table_ref[...])
-    for t in range(4):
-        for f in range(8):
-            out_ref[t, f] = moved[16 * f:16 * f + 16, 128 * t:128 * t + 128]
-
-
-def unpack_kernel(idx_ref, in_ref, table_ref, coarse_ref, iterate_ref, level_ref):
-    whole = jnp.concatenate([in_ref[idx_ref[t]] for t in range(4)], axis=-1)
-    fine = reorder(whole[:48], table_ref[...])
+    lane = lane_ids((16, LANES))
+    source = (lane // 32) * 32 + (lane % 8) * 4 + (lane % 32) // 8
+    for f, field in enumerate(fields):
+        moved = swap_groups([pick_lanes(field[x], source) for x in range(4)], 32)
+        for t in range(4):
+            out_ref[place_ref[t], f] = moved[t]
+
+
+def unpack_kernel(place_ref, own_ref, one_ref, two_ref, three_ref, iterate_ref, level_ref, hold):
+    for j, ref in enumerate((own_ref, one_ref, two_ref, three_ref)):
+        hold[j] = ref[...]
+    blocks = [place_ref[t] for t in range(4)]
+    lane = lane_ids((16, LANES))
+    source = (lane // 32) * 32 + (lane % 4) * 8 + (lane % 32) // 4
     for c in range(3):
+        moved = swap_groups([hold[j, 16 * c:16 * c + 16] for j in blocks], 32)
         for x in range(4):
-            iterate_ref[c, x] = fine[16 * c:16 * c + 16, 128 * x:128 * x + 128]
-    coarse = reorder(whole[48:], coarse_ref[...])
-    for o in range(27):
-        for x in range(2):
-            col = (o % 4) * 128 + x * 64
-            level_ref[o, x] = coarse[8 * (o // 4):8 * (o // 4) + 8, col:col + 64]
+            iterate_ref[c, x] = pick_lanes(moved[x], source)
+    lane = lane_ids(TILE)
+    source = ((lane % 64) // 16) * 32 + (lane % 2) * 8 + (lane % 16) // 2
+    for g in range(7):
+        moved = swap_groups([hold[j, 48 + 8 * g:56 + 8 * g] for j in blocks], 32)
+        for o in range(4):
+            if 4 * g + o < 27:
+                for x in range(2):
+                    level_ref[4 * g + o, x] = pick_lanes(moved[o], source + 16 * x)[:, :64]
 
 
 def fill_low(ref, n):
@@ -431,7 +406,7 @@
                 store(c, x, y, z, sums[c][z])
         return carry
 
-    lax.fori_loop(0, n * n, body, 0, unroll=n < 4)
+    lax.fori_loop(0, n * n, body, 0, unroll=True)
 
 
 def relax_into(level, weight, rhs, src, dst, n, skip_faces=False):
@@ -489,9 +464,9 @@
 
 
 def cycle_kernel(
-    idx_ref, prev_ref, own_ref, next_ref, out_ref,
+    idx_ref, prev_ref, own_ref, next_ref, out_own, out_one, out_two, out_three,
     fields, cells, level_a, weight_a, mid_a, mid_b, level_b, weight_b, mid_c, mid_d, level_c, weight_c,
-    va, va2, vb, vb2, vc, vc2, res_a, res_b, rhs_b, rhs_c,
+    va, va2, vb, vb2, vc, vc2, res_a, res_b, rhs_b, rhs_c, out_ref,
 ):
     gx_prev, gx_own, gx_next = idx_ref[0], idx_ref[1], idx_ref[2]
     slab = (lane_ids(TILE) // 8) % 4
@@ -613,6 +588,13 @@
             for dest, tile in enumerate(swap_groups(lines, 32)):
                 out_ref[lax.bitwise_xor(gx_own, dest), pl.ds(96 + 16 * g + yp, ROWS, stride=2), :] = tile
 
+    side = idx_ref[5]
+    for j, ref in enumerate((out_own, out_one, out_two, out_three)):
+        for c in range(3):
+            ref[16 * c:16 * c + 16] = out_ref[j, pl.ds(pl.multiple_of(32 * c + 16 * side, 16), 16), :]
+        for g in range(7):
+            ref[48 + 8 * g:56 + 8 * g] = out_ref[j, pl.ds(pl.multiple_of(96 + 16 * g + 8 * side, 8), 8), :]
+
 
 def slab_place(gx, gz):
     order = jnp.where(gx < 2, gx, 5 - gx)
@@ -629,24 +611,28 @@
 
 
 def shards_by_slab(cell_weight, weight_grad, material, modulus, node_mass, pinned, positions, forces):
-    table = pack_table()
     smem = pl.BlockSpec(memory_space=pltpu.SMEM)
     gx, gy, gz = lax.axis_index("gx"), lax.axis_index("gy"), lax.axis_index("gz")
     f32 = jnp.float32
+    place = slab_place(gx, gz)
+    index = 4 * gz + place
+
+    def owner_of(place, z):
+        order = jnp.where(z % 2 == 0, place, 3 - place)
+        return jnp.where(order < 2, order, 5 - order)
+
+    partner = jnp.stack([gx ^ owner_of(t, gz) for t in range(4)]).astype(jnp.int32)
     packed = pl.pallas_call(
         pack_kernel,
         out_shape=jax.ShapeDtypeStruct((4, 8, 16, LANES), f32),
-        in_specs=[smem] + vmem_specs(8),
+        in_specs=[smem, smem] + vmem_specs(7),
         out_specs=vmem_specs(1)[0],
         name="pack",
-    )(modulus, cell_weight, weight_grad, material, node_mass, pinned, positions, forces,
-      jnp.asarray(table, jnp.bfloat16))
-
-    place = slab_place(gx, gz)
-    index = 4 * gz + place
-    mine = [lax.dynamic_index_in_dim(packed, slab_place(gx ^ j, gz), 0, keepdims=False) for j in range(4)]
+    )(partner, modulus, cell_weight, weight_grad, material, node_mass, pinned, positions, forces)
+
+    mine = [packed[0]]
     for j in range(1, 4):
-        mine[j] = lax.ppermute(mine[j], "gx", [(i, i ^ j) for i in range(4)])
+        mine.append(lax.ppermute(packed[j], "gx", [(i, i ^ j) for i in range(4)]))
     mine = jnp.stack(mine)
 
     def swap_in_chain(first):
@@ -673,14 +659,10 @@
     before = jnp.where(odd_place, even, odd)
     after = jnp.where(odd_place, odd, even)
 
-    def owner_of(place, z):
-        order = jnp.where(z % 2 == 0, place, 3 - place)
-        return jnp.where(order < 2, order, 5 - order)
-
     gx_before = owner_of((index - 1) % 4, (index - 1) // 4)
     gx_after = owner_of((index + 1) % 4, (index + 1) // 4)
     scalars = jnp.stack(
-        [gx_before, gx, gx_after, (index > 0).astype(jnp.int32), (index < 15).astype(jnp.int32)]
+        [gx_before, gx, gx_after, (index > 0).astype(jnp.int32), (index < 15).astype(jnp.int32), gy]
     ).astype(jnp.int32)
 
     def buf(*dims):
@@ -688,47 +670,35 @@
 
     message = pl.pallas_call(
         cycle_kernel,
-        out_shape=jax.ShapeDtypeStruct((4, 208, LANES), f32),
+        out_shape=[jax.ShapeDtypeStruct((104, LANES), f32)] * 4,
         in_specs=[smem] + vmem_specs(3),
-        out_specs=vmem_specs(1)[0],
+        out_specs=vmem_specs(4),
         scratch_shapes=[
             buf(8, 4, 4, 4), buf(5, 5, 5), buf(27, 4, 4, 4), buf(4, 4, 4),
             buf(27, 2, 4, 4), buf(27, 2, 2, 4), buf(27, 2, 2, 2), buf(2, 2, 2),
             buf(27, 1, 2, 2), buf(27, 1, 1, 2), buf(27, 1, 1, 1), buf(1, 1, 1),
             buf(3, 6, 6, 6), buf(3, 6, 6, 6), buf(3, 4, 4, 4), buf(3, 4, 4, 4), buf(3, 3, 3, 3), buf(3, 3, 3, 3),
             buf(3, 5, 5, 5), buf(3, 3, 3, 3), buf(3, 2, 2, 2), buf(3, 1, 1, 1),
+            pltpu.VMEM((4, 208, LANES), f32),
         ],
         compiler_params=pltpu.CompilerParams(vmem_limit_bytes=48 * 1024 * 1024),
         name="cycle",
     )(scalars, before, own, after)
 
-    fine = message[:, :96].reshape(4, 3, 2, 16, LANES)
-    coarse = message[:, 96:].reshape(4, 7, 2, 8, LANES)
-
-    def half(side):
-        return jnp.concatenate(
-            [fine[:, :, side].reshape(4, 48, LANES), coarse[:, :, side].reshape(4, 56, LANES)], axis=1
-        )
-
-    message = jnp.where(gy == 0, half(0), half(1))
     back = [message[0]]
     for j in range(1, 4):
         back.append(lax.ppermute(message[j], "gx", [(i, i ^ j) for i in range(4)]))
-    scalars = jnp.stack([gx ^ owner_of(t, gz) for t in range(4)]).astype(jnp.int32)
     return pl.pallas_call(
         unpack_kernel,
         out_shape=[
             jax.ShapeDtypeStruct(positions.shape, f32),
             jax.ShapeDtypeStruct((27, 2, 8, 64), f32),
         ],
-        in_specs=[smem] + vmem_specs(3),
+        in_specs=[smem] + vmem_specs(4),
         out_specs=vmem_specs(2),
+        scratch_shapes=[pltpu.VMEM((4, 104, LANES), f32)],
         name="unpack",
-    )(scalars, jnp.stack(back), jnp.asarray(unpack_table(), jnp.bfloat16), jnp.asarray(coarse_table(), jnp.bfloat16))
-
-
-def unpack_table():
-    return np.ascontiguousarray(pack_table().T)
+    )(partner, *back)
 
 
 def solution(mesh):

time: 58.6 us -> 54.7 us (0.933)
  Pallas kernels: 29 us -> 25.6 us
  waiting for transfers between devices: 13.3 us -> 14.1 us
  other arithmetic: 1.67 us -> 0.99 us
    pallas_call x1, Pallas kernels: 24 us -> 21.4 us  [shards_by_slab(): pl.pallas_call(cycle_kernel, out_shape=[jax.ShapeDtypeStruct((104, LANES)...]
    dynamic_slice x1 -> x0, local copies, waits for them, and re-layouts: 0.95 us -> none  [shards_by_slab(): lax.dynamic_index_in_dim(packed, slab_place(gx ^ j, gz), 0, keepdims=False)]
    ppermute x3, waiting for transfers between devices: 1.76 us -> 2.54 us  [shards_by_slab(): back.append(lax.ppermute(message[j], 'gx', [(i, i ^ j) for i in range(4)]))]
    another operation x1 -> x0, other arithmetic: 0.69 us -> none  [shards_by_slab(): jnp.stack(back)]
    pallas_call x1, Pallas kernels: 2.7 us -> 2.05 us  [shards_by_slab(): pl.pallas_call(unpack_kernel, out_shape=[jax.ShapeDtypeStruct(positions.s...]
    unnamed x2 -> x8, local copies, waits for them, and re-layouts: 0.73 us -> 1.24 us
  transfers between devices with their start and end apart: 11 -> 11, of which waited for: 7 -> 8; matrix products, arithmetic and copies ran while one was open for 1% -> 0% of each run, Pallas kernels for 0% -> 0%
where the time goes in v2:
time: 54.7 us; the launch traced here: 54.4 us
  Pallas kernels  25.6 us (47%)
  waiting for transfers between devices  14.1 us (26%)
  starting transfers between devices  10.7 us (20%)
  local copies, waits for them, and re-layouts  2.28 us (4%)
  other arithmetic  0.99 us (2%)
  between operations  0.77 us (1%)
    pallas_call x1, Pallas kernels, shards_by_slab(): pl.pallas_call(cycle_kernel, out_shape=[jax.ShapeDtypeStruct((104, LANES)...  21.4 us
    ppermute x2, waiting for transfers between devices, swap_in_chain(): return lax.ppermute(mine, ('gx', 'gy', 'gz'), pairs)  6.06 us
    ppermute x3, starting transfers between devices, shards_by_slab(): mine.append(lax.ppermute(packed[j], 'gx', [(i, i ^ j) for i in range(4)]))  4.6 us
    ppermute x3, waiting for transfers between devices, shards_by_slab(): mine.append(lax.ppermute(packed[j], 'gx', [(i, i ^ j) for i in range(4)]))  4.13 us
    ppermute x3, starting transfers between devices, shards_by_slab(): back.append(lax.ppermute(message[j], 'gx', [(i, i ^ j) for i in range(4)]))  3.49 us
    ppermute x3, waiting for transfers between devices, shards_by_slab(): back.append(lax.ppermute(message[j], 'gx', [(i, i ^ j) for i in range(4)]))  2.54 us
    pallas_call x1, Pallas kernels, shards_by_slab(): pl.pallas_call(pack_kernel, out_shape=jax.ShapeDtypeStruct((4, 8, 16, LAN...  2.14 us
    ppermute x2, starting transfers between devices, swap_in_chain(): return lax.ppermute(mine, ('gx', 'gy', 'gz'), pairs)  2.11 us
  transfers between devices with their start and end apart: 11, of which 8 were waited for; matrix products, arithmetic and copies ran while one was open for 0% of the time, Pallas kernels for 0%

profile of v2, /device:TPU:0, one launch (start us, length us, event | category | flops | bytes accessed | tf_op | source)
XLA Modules:
  0.0 54.4 jit_solution(5157372713254225058)
XLA Ops:
  0.7 0.7 %pad_add_fusion.place_ref = s32[4]{0:T(128)} fusion(s32[1]{0:T(128)} %bitcast.3, s32[1]{0:T(128)} %bitcast.2, s32[1]{0:T(128)} %bitcast.1, s32[1]{0:T(128)} %bitcast), kind=kLoop, calls=%fused_computation.15 | loop fusion | flops 12 | bytes 32 | tf_op jit(solution)/shard_map/stack | solution.py:624
  1.3 2.1 %pack.1 = f32[4,8,16,128]{3,2,1,0:T(8,128)} custom-call(s32[4]{0:T(128)} %pad_add_fusion.place_ref, f32[8]{0:T(128)} %mod_ref.1, f32[4,16,128]{2,1,0:T(8,128)} %cw_ref.1, f32[4,16,128]{2,1,0:T(8,128)} %wg_ref.1, s32[4,16,128]{2,1,0:T(8,128)} %mat_ref.1, f32[4,16,128]{2,1,0:T(8,128)} %mass_ref.1, s32[4,16,128]{2,1,0:T(8,128)} %pin_ref.1, ...), custom_call_target="tpu_custom_call" | custom-call | tf_op jit(solution)/shard_map/pack/pallas_call | solution.py:625
  3.5 1.0 %fusion.2 = (f32[1,8,16,128]{3,2,1,0:T(8,128)S(1)}, f32[8,16,128]{2,1,0:T(8,128)S(1)}, f32[8,16,128]{2,1,0:T(8,128)S(1)}, f32[8,16,128]{2,1,0:T(8,128)S(1)}) fusion(f32[4,8,16,128]{3,2,1,0:T(8,128)} %pack.1), kind=kLoop, calls=%fused_computation.16 | loop fusion | bytes 524288 | tf_op jit(solution)/shard_map/slice | solution.py:633
  4.4 4.0 %collective-permute-start.2 = (f32[8,16,128]{2,1,0:T(8,128)S(1)}, f32[8,16,128]{2,1,0:T(8,128)S(1)}, u32[]{:S(2)}, u32[]{:S(2)}) collective-permute-start(f32[8,16,128]{2,1,0:T(8,128)S(1)} %get-tuple-element.19), channel_id=1, source_target_pairs={{0,24},{8,16},{16,8},{24,0},{1,25},{9,17},{17,9},{25,1},{2,26},{10... | collective-permute-start | bytes 196616 | tf_op jit(solution)/shard_map/ppermute | solution.py:635
  8.4 0.5 collective-permute-start.1
  8.9 0.1 collective-permute-start
  9.0 1.6 %collective-permute-done.2 = f32[8,16,128]{2,1,0:T(8,128)S(1)} collective-permute-done((f32[8,16,128]{2,1,0:T(8,128)S(1)}, f32[8,16,128]{2,1,0:T(8,128)S(1)}, u32[]{:S(2)}, u32[]{:S(2)}) %collective-permute-start.2) | collective-permute-done | bytes 65568 | tf_op jit(solution)/shard_map/ppermute | solution.py:635
  10.6 2.0 %collective-permute-done.1 = f32[8,16,128]{2,1,0:T(8,128)S(1)} collective-permute-done((f32[8,16,128]{2,1,0:T(8,128)S(1)}, f32[8,16,128]{2,1,0:T(8,128)S(1)}, u32[]{:S(2)}, u32[]{:S(2)}) %collective-permute-start.1) | collective-permute-done | bytes 65568 | tf_op jit(solution)/shard_map/ppermute | solution.py:635
  12.7 0.5 collective-permute-done
  13.2 0.1 collective-permute-start.5
  13.3 2.0 %collective-permute-start.3 = (f32[4,8,16,128]{3,2,1,0:T(8,128)S(1)}, f32[4,8,16,128]{3,2,1,0:T(8,128)S(1)}, u32[]{:S(2)}, u32[]{:S(2)}) collective-permute-start(f32[4,8,16,128]{3,2,1,0:T(8,128)S(1)} %pad_maximum_fusion.2), channel_id=1, source_target_pairs={{0,8},{8,0},{24,16},{16,24},{17,25},{25,17},{9,1},{1,9},{2,10},{10... | collective-permute-start | bytes 786440 | tf_op jit(solution)/shard_map/ppermute | solution.py:646
  15.3 0.0 collective-permute-start.7
  15.3 0.1 stack.67.idx_ref
  15.4 0.0 collective-permute-done.5
  15.4 0.5 collective-permute-start.6
  15.9 6.1 %collective-permute-done.3 = f32[4,8,16,128]{3,2,1,0:T(8,128)S(1)} collective-permute-done((f32[4,8,16,128]{3,2,1,0:T(8,128)S(1)}, f32[4,8,16,128]{3,2,1,0:T(8,128)S(1)}, u32[]{:S(2)}, u32[]{:S(2)}) %collective-permute-start.3) | collective-permute-done | bytes 262176 | tf_op jit(solution)/shard_map/ppermute | solution.py:646
  22.0 0.0 collective-permute-start.4
  22.0 0.0 collective-permute-done.7
  22.0 0.1 pad_maximum_fusion.1.own_ref
  22.1 0.0 collective-permute-done.6
  22.2 1.4 %collective-permute-done.4 = f32[4,8,16,128]{3,2,1,0:T(8,128)S(1)} collective-permute-done((f32[4,8,16,128]{3,2,1,0:T(8,128)S(1)}, f32[4,8,16,128]{3,2,1,0:T(8,128)S(1)}, u32[]{:S(2)}, u32[]{:S(2)}) %collective-permute-start.4) | collective-permute-done | bytes 262176 | tf_op jit(solution)/shard_map/ppermute | solution.py:651
  23.6 0.1 fusion
  23.7 21.4 %cycle.1 = (f32[104,128]{1,0:T(8,128)S(1)}, f32[104,128]{1,0:T(8,128)S(1)}, f32[104,128]{1,0:T(8,128)S(1)}, f32[104,128]{1,0:T(8,128)S(1)}) custom-call(s32[6]{0:T(128)S(1)} %stack.67.idx_ref, f32[4,8,32,128]{3,2,1,0:T(8,128)S(1)} %get-tuple-element.11.prev_ref, f32[4,8,32,128]{3,2,1,0:T(8,128)S(1)} %pad_maximum_fusion.1.own_ref, ...), custom_call_target="tpu_custom_call" | custom-call | tf_op jit(solution)/shard_map/cycle/pallas_call | solution.py:671
  45.1 0.0 copy-start
  45.1 0.6 %copy-done = f32[104,128]{1,0:T(8,128)} copy-done((f32[104,128]{1,0:T(8,128)}, f32[104,128]{1,0:T(8,128)S(1)}, u32[]{:S(2)}) %copy-start) | copy-done | bytes 53272
  45.7 0.3 collective-permute-start.8
  46.0 0.7 %collective-permute-start.9 = (f32[104,128]{1,0:T(8,128)S(1)}, f32[104,128]{1,0:T(8,128)S(1)}, u32[]{:S(2)}, u32[]{:S(2)}) collective-permute-start(f32[104,128]{1,0:T(8,128)S(1)} %get-tuple-element.8), channel_id=1, source_target_pairs={{0,16},{8,24},{16,0},{24,8},{1,17},{9,25},{17,1},{25,9},{2,18},{10... | collective-permute-start | bytes 159752 | tf_op jit(solution)/shard_map/ppermute | solution.py:690
  46.7 2.5 %collective-permute-start.10 = (f32[104,128]{1,0:T(8,128)S(1)}, f32[104,128]{1,0:T(8,128)S(1)}, u32[]{:S(2)}, u32[]{:S(2)}) collective-permute-start(f32[104,128]{1,0:T(8,128)S(1)} %get-tuple-element.9), channel_id=1, source_target_pairs={{0,24},{8,16},{16,8},{24,0},{1,25},{9,17},{17,9},{25,1},{2,26},{10... | collective-permute-start | bytes 159752 | tf_op jit(solution)/shard_map/ppermute | solution.py:690
  49.2 1.0 %collective-permute-done.8.one_ref = f32[104,128]{1,0:T(8,128)S(1)} collective-permute-done((f32[104,128]{1,0:T(8,128)S(1)}, f32[104,128]{1,0:T(8,128)S(1)}, u32[]{:S(2)}, u32[]{:S(2)}) %collective-permute-start.8) | collective-permute-done | bytes 53280 | tf_op jit(solution)/shard_map/ppermute | solution.py:690
  50.2 0.0 copy-start.1
  50.2 0.5 collective-permute-done.9.two_ref
  50.7 0.0 copy-start.2
  50.7 1.1 %collective-permute-done.10.three_ref = f32[104,128]{1,0:T(8,128)S(1)} collective-permute-done((f32[104,128]{1,0:T(8,128)S(1)}, f32[104,128]{1,0:T(8,128)S(1)}, u32[]{:S(2)}, u32[]{:S(2)}) %collective-permute-start.10) | collective-permute-done | bytes 53280 | tf_op jit(solution)/shard_map/ppermute | solution.py:690
  51.7 0.0 copy-start.3
  51.7 0.0 copy-done.1
  51.7 0.0 copy-done.2
  51.8 0.6 %copy-done.3 = f32[104,128]{1,0:T(8,128)} copy-done((f32[104,128]{1,0:T(8,128)}, f32[104,128]{1,0:T(8,128)S(1)}, u32[]{:S(2)}) %copy-start.3) | copy-done | bytes 53272
  52.4 2.1 %unpack.1 = (f32[3,4,16,128]{3,2,1,0:T(8,128)}, f32[27,2,8,64]{3,2,1,0:T(8,128)}) custom-call(s32[4]{0:T(128)} %pad_add_fusion.place_ref, f32[104,128]{1,0:T(8,128)} %copy-done, f32[104,128]{1,0:T(8,128)} %copy-done.1, f32[104,128]{1,0:T(8,128)} %copy-done.2, f32[104,128]{1,0:T(8,128)} %copy-done.3), custom_call_target="tpu_custom_call" | custom-call | tf_op jit(solution)/shard_map/unpack/pallas_call | solution.py:691
  (4 shorter events, 0.1 us)
Async XLA Ops:
  4.4 6.2 %collective-permute-start.2 = (f32[8,16,128]{2,1,0:T(8,128)S(1)}, f32[8,16,128]{2,1,0:T(8,128)S(1)}, u32[]{:S(2)}, u32[]{:S(2)}) collective-permute-start(f32[8,16,128]{2,1,0:T(8,128)S(1)} %get-tuple-element.19), channel_id=1, source_target_pairs={{0,24},{8,16},{16,8},{24,0},{1,25},{9,17},{17,9},{25,1},{2,26},{10... | collective-permute-start | bytes 196616 | tf_op jit(solution)/shard_map/ppermute | solution.py:635
  8.4 4.3 %collective-permute-start.1 = (f32[8,16,128]{2,1,0:T(8,128)S(1)}, f32[8,16,128]{2,1,0:T(8,128)S(1)}, u32[]{:S(2)}, u32[]{:S(2)}) collective-permute-start(f32[8,16,128]{2,1,0:T(8,128)S(1)} %get-tuple-element.20), channel_id=1, source_target_pairs={{0,16},{8,24},{16,0},{24,8},{1,17},{9,25},{17,1},{25,9},{2,18},{10... | collective-permute-start | bytes 196616 | tf_op jit(solution)/shard_map/ppermute | solution.py:635
  8.9 4.3 %collective-permute-start = (f32[8,16,128]{2,1,0:T(8,128)S(1)}, f32[8,16,128]{2,1,0:T(8,128)S(1)}, u32[]{:S(2)}, u32[]{:S(2)}) collective-permute-start(f32[8,16,128]{2,1,0:T(8,128)S(1)} %get-tuple-element.21), channel_id=1, source_target_pairs={{0,8},{8,0},{16,24},{24,16},{1,9},{9,1},{17,25},{25,17},{2,10},{10... | collective-permute-start | bytes 196616 | tf_op jit(solution)/shard_map/ppermute | solution.py:635
  13.2 2.2 %collective-permute-start.5 = (f32[4,8,16,128]{3,2,1,0:T(8,128)S(1)}, f32[4,8,16,128]{3,2,1,0:T(8,128)S(1)}, u32[]{:S(2)}, u32[]{:S(2)}) collective-permute-start(f32[4,8,16,128]{3,2,1,0:T(8,128)S(1)} %pad_maximum_fusion.2), channel_id=1, source_target_pairs={{8,24},{24,8},{16,17},{17,16},{25,9},{9,25},{1,2},{2,1},{10,26},{2... | collective-permute-start | bytes 786440 | tf_op jit(solution)/shard_map/ppermute | solution.py:646
  13.3 8.7 %collective-permute-start.3 = (f32[4,8,16,128]{3,2,1,0:T(8,128)S(1)}, f32[4,8,16,128]{3,2,1,0:T(8,128)S(1)}, u32[]{:S(2)}, u32[]{:S(2)}) collective-permute-start(f32[4,8,16,128]{3,2,1,0:T(8,128)S(1)} %pad_maximum_fusion.2), channel_id=1, source_target_pairs={{0,8},{8,0},{24,16},{16,24},{17,25},{25,17},{9,1},{1,9},{2,10},{10... | collective-permute-start | bytes 786440 | tf_op jit(solution)/shard_map/ppermute | solution.py:646
  15.3 6.7 %collective-permute-start.7 = (f32[4,8,16,128]{3,2,1,0:T(8,128)S(1)}, f32[4,8,16,128]{3,2,1,0:T(8,128)S(1)}, u32[]{:S(2)}, u32[]{:S(2)}) collective-permute-start(f32[4,8,16,128]{3,2,1,0:T(8,128)S(1)} %pad_maximum_fusion.2), channel_id=1, source_target_pairs={{0,4},{4,0},{1,5},{5,1},{2,6},{6,2},{3,7},{7,3},{8,12},{12,8},{9,1... | collective-permute-start | bytes 786440 | tf_op jit(solution)/shard_map/ppermute | solution.py:651
  15.4 6.7 %collective-permute-start.6 = (f32[4,8,16,128]{3,2,1,0:T(8,128)S(1)}, f32[4,8,16,128]{3,2,1,0:T(8,128)S(1)}, u32[]{:S(2)}, u32[]{:S(2)}) collective-permute-start(f32[4,8,16,128]{3,2,1,0:T(8,128)S(1)} %collective-permute-done.5), channel_id=1, source_target_pairs={{0,4},{4,0},{1,5},{5,1},{2,6},{6,2},{3,7},{7,3},{8,12},{12,8},{9,1... | collective-permute-start | bytes 786440 | tf_op jit(solution)/shard_map/ppermute | solution.py:651
  22.0 1.5 %collective-permute-start.4 = (f32[4,8,16,128]{3,2,1,0:T(8,128)S(1)}, f32[4,8,16,128]{3,2,1,0:T(8,128)S(1)}, u32[]{:S(2)}, u32[]{:S(2)}) collective-permute-start(f32[4,8,16,128]{3,2,1,0:T(8,128)S(1)} %collective-permute-done.3), channel_id=1, source_target_pairs={{0,4},{4,0},{1,5},{5,1},{2,6},{6,2},{3,7},{7,3},{8,12},{12,8},{9,1... | collective-permute-start | bytes 786440 | tf_op jit(solution)/shard_map/ppermute | solution.py:651
  45.1 0.6 %copy-start = (f32[104,128]{1,0:T(8,128)}, f32[104,128]{1,0:T(8,128)S(1)}, u32[]{:S(2)}) copy-start(f32[104,128]{1,0:T(8,128)S(1)} %get-tuple-element.6.own_ref) | copy-start | bytes 159748
  45.7 4.4 %collective-permute-start.8 = (f32[104,128]{1,0:T(8,128)S(1)}, f32[104,128]{1,0:T(8,128)S(1)}, u32[]{:S(2)}, u32[]{:S(2)}) collective-permute-start(f32[104,128]{1,0:T(8,128)S(1)} %get-tuple-element.7), channel_id=1, source_target_pairs={{0,8},{8,0},{16,24},{24,16},{1,9},{9,1},{17,25},{25,17},{2,10},{10... | collective-permute-start | bytes 159752 | tf_op jit(solution)/shard_map/ppermute | solution.py:690
  46.0 4.7 %collective-permute-start.9 = (f32[104,128]{1,0:T(8,128)S(1)}, f32[104,128]{1,0:T(8,128)S(1)}, u32[]{:S(2)}, u32[]{:S(2)}) collective-permute-start(f32[104,128]{1,0:T(8,128)S(1)} %get-tuple-element.8), channel_id=1, source_target_pairs={{0,16},{8,24},{16,0},{24,8},{1,17},{9,25},{17,1},{25,9},{2,18},{10... | collective-permute-start | bytes 159752 | tf_op jit(solution)/shard_map/ppermute | solution.py:690
  46.7 5.0 %collective-permute-start.10 = (f32[104,128]{1,0:T(8,128)S(1)}, f32[104,128]{1,0:T(8,128)S(1)}, u32[]{:S(2)}, u32[]{:S(2)}) collective-permute-start(f32[104,128]{1,0:T(8,128)S(1)} %get-tuple-element.9), channel_id=1, source_target_pairs={{0,24},{8,16},{16,8},{24,0},{1,25},{9,17},{17,9},{25,1},{2,26},{10... | collective-permute-start | bytes 159752 | tf_op jit(solution)/shard_map/ppermute | solution.py:690
  50.2 1.6 %copy-start.1 = (f32[104,128]{1,0:T(8,128)}, f32[104,128]{1,0:T(8,128)S(1)}, u32[]{:S(2)}) copy-start(f32[104,128]{1,0:T(8,128)S(1)} %collective-permute-done.8.one_ref) | copy-start | bytes 159748
  50.7 1.1 %copy-start.2 = (f32[104,128]{1,0:T(8,128)}, f32[104,128]{1,0:T(8,128)S(1)}, u32[]{:S(2)}) copy-start(f32[104,128]{1,0:T(8,128)S(1)} %collective-permute-done.9.two_ref) | copy-start | bytes 159748
  51.7 0.6 %copy-start.3 = (f32[104,128]{1,0:T(8,128)}, f32[104,128]{1,0:T(8,128)S(1)}, u32[]{:S(2)}) copy-start(f32[104,128]{1,0:T(8,128)S(1)} %collective-permute-done.10.three_ref) | copy-start | bytes 159748

commit v3 on v2

--- a/solution.py
+++ b/solution.py
@@ -335,58 +335,79 @@
     ref[:, :, n + 1] = z_above(ref[:, :, 1])
 
 
-def coarsen(low, mid, high, low_before, mid_before, high_before):
+def add(*terms):
+    total = None
+    for term in terms:
+        if term is not None:
+            total = term if total is None else total + term
+    return total
+
+
+def coarsen(low, mid, high, before, count):
+    def scaled(x, factor):
+        return None if x is None else factor * x
+
+    leads = []
+    for i in range(count):
+        half = scaled(mid(2 * i + 1), 0.5)
+        leads.append((add(low(2 * i + 1), half), add(high(2 * i + 1), half)))
+    wrapped = tuple(None if x is None else before(x) for x in leads[-1])
     out = []
-    for i in range(len(mid) // 2):
-        if i:
-            mid_b, high_b, low_b = mid[2 * i - 1], high[2 * i - 1], low[2 * i - 1]
-        else:
-            mid_b, high_b, low_b = mid_before, high_before, low_before
-        down = 0.5 * (low[2 * i] + low_b) + 0.25 * mid_b
-        here = mid[2 * i] + 0.5 * (low[2 * i] + high[2 * i] + low[2 * i + 1] + high_b) + 0.25 * (
-            mid[2 * i + 1] + mid_b
-        )
-        up = 0.5 * (high[2 * i] + high[2 * i + 1]) + 0.25 * mid[2 * i + 1]
-        out.append((down, here, up))
+    for i in range(count):
+        to_low, to_high = leads[i]
+        from_low, from_high = leads[i - 1] if i else wrapped
+        here = add(scaled(mid(2 * i), 2.0), low(2 * i), high(2 * i), to_low, from_high)
+        out.append((add(low(2 * i), from_low), here, add(high(2 * i), to_high)))
     return out
 
 
-def triple_product(src, mid_a, mid_b, dst, n):
-    unroll = n == 2
-
-    def pass_x(j, carry):
-        parts = [[src[9 * f + j, i] for i in range(n)] for f in range(3)]
-        before = [x_below(part[n - 1]) for part in parts]
-        for i, trio in enumerate(coarsen(*parts, *before)):
+def triple_product(src, mid_a, mid_b, dst, n, faces):
+    half = n // 2
+    looped = n == 4
+
+    def pass_x(j, y, skip):
+        def part(f):
+            return lambda i: None if f in skip else src[9 * f + j, i, y]
+
+        for i, trio in enumerate(coarsen(part(0), part(1), part(2), x_below, half)):
             for c in range(3):
-                mid_a[9 * c + j, i] = trio[c]
-        return carry
-
-    lax.fori_loop(0, 9, pass_x, 0, unroll=unroll)
+                mid_a[9 * c + j, i, y] = trio[c]
+
+    def all_x(y, carry):
+        for j in range(9):
+            crossed = (j // 3 != 1) + (j % 3 != 1)
+            skip = () if not faces or crossed == 2 else ((1,) if crossed == 1 else (0, 2))
+            pass_x(j, y, skip)
+        return carry
+
+    lax.fori_loop(0, n, all_x, 0, unroll=not looped)
 
     def pass_y(j, carry):
         base = 9 * (j // 3) + j % 3
-        parts = [[mid_a[base + 3 * f, :, i] for i in range(n)] for f in range(3)]
-        before = [y_below(part[n - 1]) for part in parts]
-        for i, trio in enumerate(coarsen(*parts, *before)):
+
+        def part(f):
+            return lambda i: mid_a[base + 3 * f, :, i]
+
+        for i, trio in enumerate(coarsen(part(0), part(1), part(2), y_below, half)):
             for c in range(3):
                 mid_b[base + 3 * c, :, i] = trio[c]
         return carry
 
-    lax.fori_loop(0, 9, pass_y, 0, unroll=unroll)
+    lax.fori_loop(0, 9, pass_y, 0, unroll=not looped)
 
     def pass_z(j, carry):
-        parts = [[mid_b[3 * j + f, :, :, i] for i in range(n)] for f in range(3)]
-        before = [z_below(part[n - 1]) for part in parts]
-        for i, trio in enumerate(coarsen(*parts, *before)):
+        def part(f):
+            return lambda i: mid_b[3 * j + f, :, :, i]
+
+        for i, trio in enumerate(coarsen(part(0), part(1), part(2), z_below, half)):
             for c in range(3):
-                dst[3 * j + c, :, :, i] = trio[c]
-        return carry
-
-    lax.fori_loop(0, 9, pass_z, 0, unroll=unroll)
-
-
-def sweep(level, field, n, store, skip_faces):
+                dst[3 * j + c, :, :, i] = 0.125 * trio[c]
+        return carry
+
+    lax.fori_loop(0, 9, pass_z, 0, unroll=not looped)
+
+
+def sweep(level, field, n, store):
     def body(step, carry):
         x, y = step // n, step % n
         sums = [[None] * n for _ in range(3)]
@@ -394,8 +415,6 @@
             for o1 in range(3):
                 columns = [[field[c, x + o0, y + o1, z] for z in range(n + 2)] for c in range(3)]
                 for o2 in range(3):
-                    if skip_faces and (o0 != 1) + (o1 != 1) + (o2 != 1) == 1:
-                        continue
                     for z in range(n):
                         coef = level[9 * o0 + 3 * o1 + o2, x, y, z]
                         for c in range(3):
@@ -409,20 +428,61 @@
     lax.fori_loop(0, n * n, body, 0, unroll=True)
 
 
-def relax_into(level, weight, rhs, src, dst, n, skip_faces=False):
+def cell_sweep(parts, field, store):
+    cells, edge_x, edge_y, edge_z, diag, sums = parts
+
+    def gather(c, carry):
+        for x in range(4):
+            pair = [[field[c, 1 + x, 1 + y, 1 + z] + field[c, 2 + x, 1 + y, 1 + z] for z in range(5)] for y in range(5)]
+            for y in range(4):
+                quad = [pair[y][z] + pair[y + 1][z] for z in range(5)]
+                for z in range(4):
+                    sums[c, 1 + x, 1 + y, 1 + z] = cells[1 + x, 1 + y, 1 + z] * (quad[z] + quad[z + 1])
+        fill_low(sums.at[c], 4)
+        return carry
+
+    lax.fori_loop(0, 3, gather, 0, unroll=True)
+
+    for x in range(4):
+        for y in range(4):
+            for c in range(3):
+                near = [
+                    (sums[c, x, y, z] + sums[c, x, y + 1, z]) + (sums[c, x + 1, y, z] + sums[c, x + 1, y + 1, z])
+                    for z in range(5)
+                ]
+                line = [field[c, 1 + x, 1 + y, z] for z in range(6)]
+                for z in range(4):
+                    value = diag[x, y, z] * line[1 + z] + (near[z] + near[z + 1])
+                    value = value - edge_x[x, y, z] * field[c, x, 1 + y, 1 + z]
+                    value = value - edge_x[x + 1, y, z] * field[c, x + 2, 1 + y, 1 + z]
+                    value = value - edge_y[x, y, z] * field[c, 1 + x, y, 1 + z]
+                    value = value - edge_y[x, y + 1, z] * field[c, 1 + x, y + 2, 1 + z]
+                    value = value - edge_z[x, y, z] * line[z]
+                    value = value - edge_z[x, y, z + 1] * line[z + 2]
+                    store(c, x, y, z, value)
+
+
+def apply_level(level, field, n, store):
+    if n == 4:
+        cell_sweep(level, field, store)
+    else:
+        sweep(level, field, n, store)
+
+
+def relax_into(level, weight, rhs, src, dst, n):
     def store(c, x, y, z, value):
         dst[c, 1 + x, 1 + y, 1 + z] = src[c, 1 + x, 1 + y, 1 + z] + weight[x, y, z] * (rhs[c, x, y, z] - value)
 
-    sweep(level, src, n, store, skip_faces)
-
-
-def residual_down(level, rhs, src, res, coarse_rhs, n, skip_faces=False):
+    apply_level(level, src, n, store)
+
+
+def residual_down(level, rhs, src, res, coarse_rhs, n):
     half = n // 2
 
     def store(c, x, y, z, value):
         res[c, 1 + x, 1 + y, 1 + z] = rhs[c, x, y, z] - value
 
-    sweep(level, src, n, store, skip_faces)
+    apply_level(level, src, n, store)
 
     def body(c, carry):
         fill_low(res.at[c], n)
@@ -467,6 +527,7 @@
     idx_ref, prev_ref, own_ref, next_ref, out_own, out_one, out_two, out_three,
     fields, cells, level_a, weight_a, mid_a, mid_b, level_b, weight_b, mid_c, mid_d, level_c, weight_c,
     va, va2, vb, vb2, vc, vc2, res_a, res_b, rhs_b, rhs_c, out_ref,
+    edge_x, edge_y, edge_z, diag, sums,
 ):
     gx_prev, gx_own, gx_next = idx_ref[0], idx_ref[1], idx_ref[2]
     slab = (lane_ids(TILE) // 8) % 4
@@ -501,7 +562,6 @@
             for slot, offset in enumerate(offset_list()):
                 nonzero = sum(1 for part in offset if part != 0)
                 if nonzero == 1:
-                    level_a[slot, x, y, z] = jnp.zeros(TILE, jnp.float32)
                     continue
                 total = None
                 for s in corner_list():
@@ -509,16 +569,24 @@
                         term = near[s[0]][s[1]][z + 1 - s[2]]
                         total = term if total is None else total + term
                 if nonzero == 0:
-                    total = (ELEMENT_TERMS[0] / ELEMENT_TERMS[3]) * total + fields[1, x, y, z]
+                    mass = fields[1, x, y, z]
+                    diag[x, y, z] = ((ELEMENT_TERMS[0] - ELEMENT_TERMS[3]) / ELEMENT_TERMS[3]) * total + mass
+                    total = (ELEMENT_TERMS[0] / ELEMENT_TERMS[3]) * total + mass
                     weight_a[x, y, z] = jnp.where(inside, OMEGA / jnp.where(inside, total, 1.0), 0.0)
                 level_a[slot, x, y, z] = total
         return carry
 
     lax.fori_loop(0, 16, build, 0)
 
-    triple_product(level_a, mid_a, mid_b, level_b, 4)
+    edge_z[...] = (cells[1:, 1:] + cells[:4, 1:]) + (cells[1:, :4] + cells[:4, :4])
+    over_z = cells[:, :, 1:] + cells[:, :, :4]
+    edge_x[...] = over_z[:, 1:] + over_z[:, :4]
+    edge_y[...] = over_z[1:] + over_z[:4]
+    fine = (cells, edge_x, edge_y, edge_z, diag, sums)
+
+    triple_product(level_a, mid_a, mid_b, level_b, 4, True)
     weight_b[...] = jnp.where(inside, OMEGA / jnp.where(inside, level_b[13], 1.0), 0.0)
-    triple_product(level_b, mid_c, mid_d, level_c, 2)
+    triple_product(level_b, mid_c, mid_d, level_c, 2, False)
     weight_c[...] = jnp.where(inside, OMEGA / jnp.where(inside, level_c[13], 1.0), 0.0)
 
     position, force = fields.at[2:5], fields.at[5:8]
@@ -530,11 +598,11 @@
 
     lax.fori_loop(0, 3, load, 0)
     fill_all(va, 4)
-    relax_into(level_a, weight_a, force, va, va2, 4, True)
+    relax_into(fine, weight_a, force, va, va2, 4)
     fill_all(va2, 4)
-    relax_into(level_a, weight_a, force, va2, va, 4, True)
+    relax_into(fine, weight_a, force, va2, va, 4)
     fill_all(va, 4)
-    residual_down(level_a, force, va, res_a, rhs_b, 4, True)
+    residual_down(fine, force, va, res_a, rhs_b, 4)
 
     for c in range(3):
         for x in range(2):
@@ -563,9 +631,9 @@
 
     add_prolonged(vb2, va, inside, 2)
     fill_all(va, 4)
-    relax_into(level_a, weight_a, force, va, va2, 4, True)
+    relax_into(fine, weight_a, force, va, va2, 4)
     fill_all(va2, 4)
-    relax_into(level_a, weight_a, force, va2, va, 4, True)
+    relax_into(fine, weight_a, force, va2, va, 4)
 
     def own_slab(tiles):
         total = None
@@ -574,11 +642,15 @@
             total = moved if total is None else jnp.where(slab == group, moved, total)
         return total
 
-    for c in range(3):
+    def send_field(c, carry):
         for yp in range(4):
             lines = [own_slab([va[c, 1 + xp, 1 + yp, 1 + zp] for zp in range(4)]) for xp in range(4)]
             for dest, tile in enumerate(swap_groups(lines, 32)):
                 out_ref[lax.bitwise_xor(gx_own, dest), pl.ds(32 * c + yp, ROWS, stride=4), :] = tile
+        return carry
+
+    lax.fori_loop(0, 3, send_field, 0)
+
     for g in range(7):
         for yp in range(2):
             lines = [
@@ -680,6 +752,7 @@
             buf(3, 6, 6, 6), buf(3, 6, 6, 6), buf(3, 4, 4, 4), buf(3, 4, 4, 4), buf(3, 3, 3, 3), buf(3, 3, 3, 3),
             buf(3, 5, 5, 5), buf(3, 3, 3, 3), buf(3, 2, 2, 2), buf(3, 1, 1, 1),
             pltpu.VMEM((4, 208, LANES), f32),
+            buf(5, 4, 4), buf(4, 5, 4), buf(4, 4, 5), buf(4, 4, 4), buf(3, 5, 5, 5),
         ],
         compiler_params=pltpu.CompilerParams(vmem_limit_bytes=48 * 1024 * 1024),
         name="cycle",

time: 54.7 us -> 51.5 us (0.941)
  Pallas kernels: 25.6 us -> 22.4 us
    pallas_call x1, Pallas kernels: 21.4 us -> 18.2 us  [shards_by_slab(): pl.pallas_call(cycle_kernel, out_shape=[jax.ShapeDtypeStruct((104, LANES)...]
where the time goes in v3:
time: 51.5 us; the launch traced here: 51.2 us
  Pallas kernels  22.4 us (43%)
  waiting for transfers between devices  14.1 us (27%)
  starting transfers between devices  10.7 us (21%)
  local copies, waits for them, and re-layouts  2.28 us (4%)
  other arithmetic  0.99 us (2%)
  between operations  0.77 us (1%)
    pallas_call x1, Pallas kernels, shards_by_slab(): pl.pallas_call(cycle_kernel, out_shape=[jax.ShapeDtypeStruct((104, LANES)...  18.2 us
    ppermute x2, waiting for transfers between devices, swap_in_chain(): return lax.ppermute(mine, ('gx', 'gy', 'gz'), pairs)  6.06 us
    ppermute x3, starting transfers between devices, shards_by_slab(): mine.append(lax.ppermute(packed[j], 'gx', [(i, i ^ j) for i in range(4)]))  4.6 us
    ppermute x3, waiting for transfers between devices, shards_by_slab(): mine.append(lax.ppermute(packed[j], 'gx', [(i, i ^ j) for i in range(4)]))  4.13 us
    ppermute x3, starting transfers between devices, shards_by_slab(): back.append(lax.ppermute(message[j], 'gx', [(i, i ^ j) for i in range(4)]))  3.49 us
    ppermute x3, waiting for transfers between devices, shards_by_slab(): back.append(lax.ppermute(message[j], 'gx', [(i, i ^ j) for i in range(4)]))  2.54 us
    pallas_call x1, Pallas kernels, shards_by_slab(): pl.pallas_call(pack_kernel, out_shape=jax.ShapeDtypeStruct((4, 8, 16, LAN...  2.14 us
    ppermute x2, starting transfers between devices, swap_in_chain(): return lax.ppermute(mine, ('gx', 'gy', 'gz'), pairs)  2.11 us
  transfers between devices with their start and end apart: 11, of which 8 were waited for; matrix products, arithmetic and copies ran while one was open for 0% of the time, Pallas kernels for 0%

profile of v3, /device:TPU:0, one launch (start us, length us, event | category | flops | bytes accessed | tf_op | source)
XLA Modules:
  0.0 51.2 jit_solution(16967346976706031972)
XLA Ops:
  0.7 0.7 %pad_add_fusion.place_ref = s32[4]{0:T(128)} fusion(s32[1]{0:T(128)} %bitcast.3, s32[1]{0:T(128)} %bitcast.2, s32[1]{0:T(128)} %bitcast.1, s32[1]{0:T(128)} %bitcast), kind=kLoop, calls=%fused_computation.15 | loop fusion | flops 12 | bytes 32 | tf_op jit(solution)/shard_map/stack | solution.py:696
  1.3 2.1 %pack.1 = f32[4,8,16,128]{3,2,1,0:T(8,128)} custom-call(s32[4]{0:T(128)} %pad_add_fusion.place_ref, f32[8]{0:T(128)} %mod_ref.1, f32[4,16,128]{2,1,0:T(8,128)} %cw_ref.1, f32[4,16,128]{2,1,0:T(8,128)} %wg_ref.1, s32[4,16,128]{2,1,0:T(8,128)} %mat_ref.1, f32[4,16,128]{2,1,0:T(8,128)} %mass_ref.1, s32[4,16,128]{2,1,0:T(8,128)} %pin_ref.1, ...), custom_call_target="tpu_custom_call" | custom-call | tf_op jit(solution)/shard_map/pack/pallas_call | solution.py:697
  3.5 1.0 %fusion.2 = (f32[1,8,16,128]{3,2,1,0:T(8,128)S(1)}, f32[8,16,128]{2,1,0:T(8,128)S(1)}, f32[8,16,128]{2,1,0:T(8,128)S(1)}, f32[8,16,128]{2,1,0:T(8,128)S(1)}) fusion(f32[4,8,16,128]{3,2,1,0:T(8,128)} %pack.1), kind=kLoop, calls=%fused_computation.16 | loop fusion | bytes 524288 | tf_op jit(solution)/shard_map/slice | solution.py:705
  4.4 4.0 %collective-permute-start.2 = (f32[8,16,128]{2,1,0:T(8,128)S(1)}, f32[8,16,128]{2,1,0:T(8,128)S(1)}, u32[]{:S(2)}, u32[]{:S(2)}) collective-permute-start(f32[8,16,128]{2,1,0:T(8,128)S(1)} %get-tuple-element.19), channel_id=1, source_target_pairs={{0,24},{8,16},{16,8},{24,0},{1,25},{9,17},{17,9},{25,1},{2,26},{10... | collective-permute-start | bytes 196616 | tf_op jit(solution)/shard_map/ppermute | solution.py:707
  8.4 0.5 collective-permute-start.1
  8.9 0.1 collective-permute-start
  9.0 1.6 %collective-permute-done.2 = f32[8,16,128]{2,1,0:T(8,128)S(1)} collective-permute-done((f32[8,16,128]{2,1,0:T(8,128)S(1)}, f32[8,16,128]{2,1,0:T(8,128)S(1)}, u32[]{:S(2)}, u32[]{:S(2)}) %collective-permute-start.2) | collective-permute-done | bytes 65568 | tf_op jit(solution)/shard_map/ppermute | solution.py:707
  10.6 2.0 %collective-permute-done.1 = f32[8,16,128]{2,1,0:T(8,128)S(1)} collective-permute-done((f32[8,16,128]{2,1,0:T(8,128)S(1)}, f32[8,16,128]{2,1,0:T(8,128)S(1)}, u32[]{:S(2)}, u32[]{:S(2)}) %collective-permute-start.1) | collective-permute-done | bytes 65568 | tf_op jit(solution)/shard_map/ppermute | solution.py:707
  12.7 0.5 collective-permute-done
  13.2 0.1 collective-permute-start.5
  13.3 2.0 %collective-permute-start.3 = (f32[4,8,16,128]{3,2,1,0:T(8,128)S(1)}, f32[4,8,16,128]{3,2,1,0:T(8,128)S(1)}, u32[]{:S(2)}, u32[]{:S(2)}) collective-permute-start(f32[4,8,16,128]{3,2,1,0:T(8,128)S(1)} %pad_maximum_fusion.2), channel_id=1, source_target_pairs={{0,8},{8,0},{24,16},{16,24},{17,25},{25,17},{9,1},{1,9},{2,10},{10... | collective-permute-start | bytes 786440 | tf_op jit(solution)/shard_map/ppermute | solution.py:718
  15.3 0.0 collective-permute-start.7
  15.3 0.1 stack.67.idx_ref
  15.4 0.0 collective-permute-done.5
  15.4 0.5 %collective-permute-start.6 = (f32[4,8,16,128]{3,2,1,0:T(8,128)S(1)}, f32[4,8,16,128]{3,2,1,0:T(8,128)S(1)}, u32[]{:S(2)}, u32[]{:S(2)}) collective-permute-start(f32[4,8,16,128]{3,2,1,0:T(8,128)S(1)} %collective-permute-done.5), channel_id=1, source_target_pairs={{0,4},{4,0},{1,5},{5,1},{2,6},{6,2},{3,7},{7,3},{8,12},{12,8},{9,1... | collective-permute-start | bytes 786440 | tf_op jit(solution)/shard_map/ppermute | solution.py:723
  15.9 6.1 %collective-permute-done.3 = f32[4,8,16,128]{3,2,1,0:T(8,128)S(1)} collective-permute-done((f32[4,8,16,128]{3,2,1,0:T(8,128)S(1)}, f32[4,8,16,128]{3,2,1,0:T(8,128)S(1)}, u32[]{:S(2)}, u32[]{:S(2)}) %collective-permute-start.3) | collective-permute-done | bytes 262176 | tf_op jit(solution)/shard_map/ppermute | solution.py:718
  22.0 0.0 collective-permute-start.4
  22.0 0.0 collective-permute-done.7
  22.0 0.1 pad_maximum_fusion.1.own_ref
  22.1 0.0 collective-permute-done.6
  22.2 1.4 %collective-permute-done.4 = f32[4,8,16,128]{3,2,1,0:T(8,128)S(1)} collective-permute-done((f32[4,8,16,128]{3,2,1,0:T(8,128)S(1)}, f32[4,8,16,128]{3,2,1,0:T(8,128)S(1)}, u32[]{:S(2)}, u32[]{:S(2)}) %collective-permute-start.4) | collective-permute-done | bytes 262176 | tf_op jit(solution)/shard_map/ppermute | solution.py:723
  23.6 0.1 fusion
  23.7 18.2 %cycle.1 = (f32[104,128]{1,0:T(8,128)S(1)}, f32[104,128]{1,0:T(8,128)S(1)}, f32[104,128]{1,0:T(8,128)S(1)}, f32[104,128]{1,0:T(8,128)S(1)}) custom-call(s32[6]{0:T(128)S(1)} %stack.67.idx_ref, f32[4,8,32,128]{3,2,1,0:T(8,128)S(1)} %get-tuple-element.11.prev_ref, f32[4,8,32,128]{3,2,1,0:T(8,128)S(1)} %pad_maximum_fusion.1.own_ref, ...), custom_call_target="tpu_custom_call" | custom-call | tf_op jit(solution)/shard_map/cycle/pallas_call | solution.py:743
  41.9 0.0 copy-start
  41.9 0.6 %copy-done = f32[104,128]{1,0:T(8,128)} copy-done((f32[104,128]{1,0:T(8,128)}, f32[104,128]{1,0:T(8,128)S(1)}, u32[]{:S(2)}) %copy-start) | copy-done | bytes 53272
  42.5 0.3 collective-permute-start.8
  42.8 0.7 %collective-permute-start.9 = (f32[104,128]{1,0:T(8,128)S(1)}, f32[104,128]{1,0:T(8,128)S(1)}, u32[]{:S(2)}, u32[]{:S(2)}) collective-permute-start(f32[104,128]{1,0:T(8,128)S(1)} %get-tuple-element.8), channel_id=1, source_target_pairs={{0,16},{8,24},{16,0},{24,8},{1,17},{9,25},{17,1},{25,9},{2,18},{10... | collective-permute-start | bytes 159752 | tf_op jit(solution)/shard_map/ppermute | solution.py:763
  43.5 2.5 %collective-permute-start.10 = (f32[104,128]{1,0:T(8,128)S(1)}, f32[104,128]{1,0:T(8,128)S(1)}, u32[]{:S(2)}, u32[]{:S(2)}) collective-permute-start(f32[104,128]{1,0:T(8,128)S(1)} %get-tuple-element.9), channel_id=1, source_target_pairs={{0,24},{8,16},{16,8},{24,0},{1,25},{9,17},{17,9},{25,1},{2,26},{10... | collective-permute-start | bytes 159752 | tf_op jit(solution)/shard_map/ppermute | solution.py:763
  46.0 1.0 %collective-permute-done.8.one_ref = f32[104,128]{1,0:T(8,128)S(1)} collective-permute-done((f32[104,128]{1,0:T(8,128)S(1)}, f32[104,128]{1,0:T(8,128)S(1)}, u32[]{:S(2)}, u32[]{:S(2)}) %collective-permute-start.8) | collective-permute-done | bytes 53280 | tf_op jit(solution)/shard_map/ppermute | solution.py:763
  47.0 0.0 copy-start.1
  47.0 0.5 %collective-permute-done.9.two_ref = f32[104,128]{1,0:T(8,128)S(1)} collective-permute-done((f32[104,128]{1,0:T(8,128)S(1)}, f32[104,128]{1,0:T(8,128)S(1)}, u32[]{:S(2)}, u32[]{:S(2)}) %collective-permute-start.9) | collective-permute-done | bytes 53280 | tf_op jit(solution)/shard_map/ppermute | solution.py:763
  47.5 0.0 copy-start.2
  47.5 1.1 %collective-permute-done.10.three_ref = f32[104,128]{1,0:T(8,128)S(1)} collective-permute-done((f32[104,128]{1,0:T(8,128)S(1)}, f32[104,128]{1,0:T(8,128)S(1)}, u32[]{:S(2)}, u32[]{:S(2)}) %collective-permute-start.10) | collective-permute-done | bytes 53280 | tf_op jit(solution)/shard_map/ppermute | solution.py:763
  48.5 0.0 copy-start.3
  48.5 0.0 copy-done.1
  48.6 0.0 copy-done.2
  48.6 0.6 %copy-done.3 = f32[104,128]{1,0:T(8,128)} copy-done((f32[104,128]{1,0:T(8,128)}, f32[104,128]{1,0:T(8,128)S(1)}, u32[]{:S(2)}) %copy-start.3) | copy-done | bytes 53272
  49.2 2.1 %unpack.1 = (f32[3,4,16,128]{3,2,1,0:T(8,128)}, f32[27,2,8,64]{3,2,1,0:T(8,128)}) custom-call(s32[4]{0:T(128)} %pad_add_fusion.place_ref, f32[104,128]{1,0:T(8,128)} %copy-done, f32[104,128]{1,0:T(8,128)} %copy-done.1, f32[104,128]{1,0:T(8,128)} %copy-done.2, f32[104,128]{1,0:T(8,128)} %copy-done.3), custom_call_target="tpu_custom_call" | custom-call | tf_op jit(solution)/shard_map/unpack/pallas_call | solution.py:764
  (4 shorter events, 0.1 us)
Async XLA Ops:
  4.4 6.2 %collective-permute-start.2 = (f32[8,16,128]{2,1,0:T(8,128)S(1)}, f32[8,16,128]{2,1,0:T(8,128)S(1)}, u32[]{:S(2)}, u32[]{:S(2)}) collective-permute-start(f32[8,16,128]{2,1,0:T(8,128)S(1)} %get-tuple-element.19), channel_id=1, source_target_pairs={{0,24},{8,16},{16,8},{24,0},{1,25},{9,17},{17,9},{25,1},{2,26},{10... | collective-permute-start | bytes 196616 | tf_op jit(solution)/shard_map/ppermute | solution.py:707
  8.4 4.3 %collective-permute-start.1 = (f32[8,16,128]{2,1,0:T(8,128)S(1)}, f32[8,16,128]{2,1,0:T(8,128)S(1)}, u32[]{:S(2)}, u32[]{:S(2)}) collective-permute-start(f32[8,16,128]{2,1,0:T(8,128)S(1)} %get-tuple-element.20), channel_id=1, source_target_pairs={{0,16},{8,24},{16,0},{24,8},{1,17},{9,25},{17,1},{25,9},{2,18},{10... | collective-permute-start | bytes 196616 | tf_op jit(solution)/shard_map/ppermute | solution.py:707
  8.9 4.3 %collective-permute-start = (f32[8,16,128]{2,1,0:T(8,128)S(1)}, f32[8,16,128]{2,1,0:T(8,128)S(1)}, u32[]{:S(2)}, u32[]{:S(2)}) collective-permute-start(f32[8,16,128]{2,1,0:T(8,128)S(1)} %get-tuple-element.21), channel_id=1, source_target_pairs={{0,8},{8,0},{16,24},{24,16},{1,9},{9,1},{17,25},{25,17},{2,10},{10... | collective-permute-start | bytes 196616 | tf_op jit(solution)/shard_map/ppermute | solution.py:707
  13.2 2.2 %collective-permute-start.5 = (f32[4,8,16,128]{3,2,1,0:T(8,128)S(1)}, f32[4,8,16,128]{3,2,1,0:T(8,128)S(1)}, u32[]{:S(2)}, u32[]{:S(2)}) collective-permute-start(f32[4,8,16,128]{3,2,1,0:T(8,128)S(1)} %pad_maximum_fusion.2), channel_id=1, source_target_pairs={{8,24},{24,8},{16,17},{17,16},{25,9},{9,25},{1,2},{2,1},{10,26},{2... | collective-permute-start | bytes 786440 | tf_op jit(solution)/shard_map/ppermute | solution.py:718
  13.3 8.7 %collective-permute-start.3 = (f32[4,8,16,128]{3,2,1,0:T(8,128)S(1)}, f32[4,8,16,128]{3,2,1,0:T(8,128)S(1)}, u32[]{:S(2)}, u32[]{:S(2)}) collective-permute-start(f32[4,8,16,128]{3,2,1,0:T(8,128)S(1)} %pad_maximum_fusion.2), channel_id=1, source_target_pairs={{0,8},{8,0},{24,16},{16,24},{17,25},{25,17},{9,1},{1,9},{2,10},{10... | collective-permute-start | bytes 786440 | tf_op jit(solution)/shard_map/ppermute | solution.py:718
  15.3 6.7 %collective-permute-start.7 = (f32[4,8,16,128]{3,2,1,0:T(8,128)S(1)}, f32[4,8,16,128]{3,2,1,0:T(8,128)S(1)}, u32[]{:S(2)}, u32[]{:S(2)}) collective-permute-start(f32[4,8,16,128]{3,2,1,0:T(8,128)S(1)} %pad_maximum_fusion.2), channel_id=1, source_target_pairs={{0,4},{4,0},{1,5},{5,1},{2,6},{6,2},{3,7},{7,3},{8,12},{12,8},{9,1... | collective-permute-start | bytes 786440 | tf_op jit(solution)/shard_map/ppermute | solution.py:723
  15.4 6.7 %collective-permute-start.6 = (f32[4,8,16,128]{3,2,1,0:T(8,128)S(1)}, f32[4,8,16,128]{3,2,1,0:T(8,128)S(1)}, u32[]{:S(2)}, u32[]{:S(2)}) collective-permute-start(f32[4,8,16,128]{3,2,1,0:T(8,128)S(1)} %collective-permute-done.5), channel_id=1, source_target_pairs={{0,4},{4,0},{1,5},{5,1},{2,6},{6,2},{3,7},{7,3},{8,12},{12,8},{9,1... | collective-permute-start | bytes 786440 | tf_op jit(solution)/shard_map/ppermute | solution.py:723
  22.0 1.5 %collective-permute-start.4 = (f32[4,8,16,128]{3,2,1,0:T(8,128)S(1)}, f32[4,8,16,128]{3,2,1,0:T(8,128)S(1)}, u32[]{:S(2)}, u32[]{:S(2)}) collective-permute-start(f32[4,8,16,128]{3,2,1,0:T(8,128)S(1)} %collective-permute-done.3), channel_id=1, source_target_pairs={{0,4},{4,0},{1,5},{5,1},{2,6},{6,2},{3,7},{7,3},{8,12},{12,8},{9,1... | collective-permute-start | bytes 786440 | tf_op jit(solution)/shard_map/ppermute | solution.py:723
  41.9 0.6 %copy-start = (f32[104,128]{1,0:T(8,128)}, f32[104,128]{1,0:T(8,128)S(1)}, u32[]{:S(2)}) copy-start(f32[104,128]{1,0:T(8,128)S(1)} %get-tuple-element.6.own_ref) | copy-start | bytes 159748
  42.5 4.4 %collective-permute-start.8 = (f32[104,128]{1,0:T(8,128)S(1)}, f32[104,128]{1,0:T(8,128)S(1)}, u32[]{:S(2)}, u32[]{:S(2)}) collective-permute-start(f32[104,128]{1,0:T(8,128)S(1)} %get-tuple-element.7), channel_id=1, source_target_pairs={{0,8},{8,0},{16,24},{24,16},{1,9},{9,1},{17,25},{25,17},{2,10},{10... | collective-permute-start | bytes 159752 | tf_op jit(solution)/shard_map/ppermute | solution.py:763
  42.8 4.7 %collective-permute-start.9 = (f32[104,128]{1,0:T(8,128)S(1)}, f32[104,128]{1,0:T(8,128)S(1)}, u32[]{:S(2)}, u32[]{:S(2)}) collective-permute-start(f32[104,128]{1,0:T(8,128)S(1)} %get-tuple-element.8), channel_id=1, source_target_pairs={{0,16},{8,24},{16,0},{24,8},{1,17},{9,25},{17,1},{25,9},{2,18},{10... | collective-permute-start | bytes 159752 | tf_op jit(solution)/shard_map/ppermute | solution.py:763
  43.5 5.0 %collective-permute-start.10 = (f32[104,128]{1,0:T(8,128)S(1)}, f32[104,128]{1,0:T(8,128)S(1)}, u32[]{:S(2)}, u32[]{:S(2)}) collective-permute-start(f32[104,128]{1,0:T(8,128)S(1)} %get-tuple-element.9), channel_id=1, source_target_pairs={{0,24},{8,16},{16,8},{24,0},{1,25},{9,17},{17,9},{25,1},{2,26},{10... | collective-permute-start | bytes 159752 | tf_op jit(solution)/shard_map/ppermute | solution.py:763
  47.0 1.6 %copy-start.1 = (f32[104,128]{1,0:T(8,128)}, f32[104,128]{1,0:T(8,128)S(1)}, u32[]{:S(2)}) copy-start(f32[104,128]{1,0:T(8,128)S(1)} %collective-permute-done.8.one_ref) | copy-start | bytes 159748
  47.5 1.1 %copy-start.2 = (f32[104,128]{1,0:T(8,128)}, f32[104,128]{1,0:T(8,128)S(1)}, u32[]{:S(2)}) copy-start(f32[104,128]{1,0:T(8,128)S(1)} %collective-permute-done.9.two_ref) | copy-start | bytes 159748
  48.5 0.6 %copy-start.3 = (f32[104,128]{1,0:T(8,128)}, f32[104,128]{1,0:T(8,128)S(1)}, u32[]{:S(2)}) copy-start(f32[104,128]{1,0:T(8,128)S(1)} %collective-permute-done.10.three_ref) | copy-start | bytes 159748

commit v4 on v3

--- a/solution.py
+++ b/solution.py
@@ -283,7 +283,25 @@
     return jnp.take_along_axis(x, jnp.broadcast_to(source, x.shape), axis=-1)
 
 
-def pack_kernel(place_ref, mod_ref, cw_ref, wg_ref, mat_ref, mass_ref, pin_ref, pos_ref, force_ref, out_ref):
+def slab_place(gx, gz):
+    order = jnp.where(gx < 2, gx, 5 - gx)
+    return jnp.where(lax.rem(gz, 2) == 0, order, 3 - order)
+
+
+def owner_of(place, gz):
+    order = jnp.where(lax.rem(gz, 2) == 0, place, 3 - place)
+    return jnp.where(order < 2, order, 5 - order)
+
+
+def slab_partners():
+    gx, gz = lax.axis_index("gx"), lax.axis_index("gz")
+    return [lax.bitwise_xor(gx, owner_of(t, gz)) for t in range(4)]
+
+
+def pack_kernel(
+    mod_ref, cw_ref, wg_ref, mat_ref, mass_ref, pin_ref, pos_ref, force_ref, out_0, out_1, out_2, out_3, out_ref,
+):
+    partners = slab_partners()
     material = mat_ref[...]
     lookup = jnp.zeros(material.shape, jnp.float32)
     for index in range(mod_ref.shape[0]):
@@ -296,13 +314,15 @@
     for f, field in enumerate(fields):
         moved = swap_groups([pick_lanes(field[x], source) for x in range(4)], 32)
         for t in range(4):
-            out_ref[place_ref[t], f] = moved[t]
-
-
-def unpack_kernel(place_ref, own_ref, one_ref, two_ref, three_ref, iterate_ref, level_ref, hold):
+            out_ref[partners[t], f] = moved[t]
+    for j, ref in enumerate((out_0, out_1, out_2, out_3)):
+        ref[...] = out_ref[j]
+
+
+def unpack_kernel(own_ref, one_ref, two_ref, three_ref, iterate_ref, level_ref, hold):
     for j, ref in enumerate((own_ref, one_ref, two_ref, three_ref)):
         hold[j] = ref[...]
-    blocks = [place_ref[t] for t in range(4)]
+    blocks = slab_partners()
     lane = lane_ids((16, LANES))
     source = (lane // 32) * 32 + (lane % 4) * 8 + (lane % 32) // 4
     for c in range(3):
@@ -524,14 +544,18 @@
 
 
 def cycle_kernel(
-    idx_ref, prev_ref, own_ref, next_ref, out_own, out_one, out_two, out_three,
+    prev_ref, own_ref, next_ref, out_own, out_one, out_two, out_three,
     fields, cells, level_a, weight_a, mid_a, mid_b, level_b, weight_b, mid_c, mid_d, level_c, weight_c,
     va, va2, vb, vb2, vc, vc2, res_a, res_b, rhs_b, rhs_c, out_ref,
     edge_x, edge_y, edge_z, diag, sums,
 ):
-    gx_prev, gx_own, gx_next = idx_ref[0], idx_ref[1], idx_ref[2]
+    gx_own, gz = lax.axis_index("gx"), lax.axis_index("gz")
+    index = 4 * gz + slab_place(gx_own, gz)
+    below, above = lax.max(index - 1, 0), lax.min(index + 1, 15)
+    gx_prev = owner_of(lax.rem(below, 4), lax.div(below, 4))
+    gx_next = owner_of(lax.rem(above, 4), lax.div(above, 4))
     slab = (lane_ids(TILE) // 8) % 4
-    inside = (slab == 1) | ((slab == 0) & (idx_ref[3] == 1)) | ((slab == 2) & (idx_ref[4] == 1))
+    inside = (slab == 1) | ((slab == 0) & (index > 0)) | ((slab == 2) & (index < 15))
 
     def arrange(step, carry):
         f = step
@@ -660,7 +684,7 @@
             for dest, tile in enumerate(swap_groups(lines, 32)):
                 out_ref[lax.bitwise_xor(gx_own, dest), pl.ds(96 + 16 * g + yp, ROWS, stride=2), :] = tile
 
-    side = idx_ref[5]
+    side = lax.axis_index("gy")
     for j, ref in enumerate((out_own, out_one, out_two, out_three)):
         for c in range(3):
             ref[16 * c:16 * c + 16] = out_ref[j, pl.ds(pl.multiple_of(32 * c + 16 * side, 16), 16), :]
@@ -668,11 +692,6 @@
             ref[48 + 8 * g:56 + 8 * g] = out_ref[j, pl.ds(pl.multiple_of(96 + 16 * g + 8 * side, 8), 8), :]
 
 
-def slab_place(gx, gz):
-    order = jnp.where(gx < 2, gx, 5 - gx)
-    return jnp.where(gz % 2 == 0, order, 3 - order)
-
-
 def slab_owner(place, gz):
     order = place if gz % 2 == 0 else 3 - place
     return SNAKE[order]
@@ -686,21 +705,15 @@
     smem = pl.BlockSpec(memory_space=pltpu.SMEM)
     gx, gy, gz = lax.axis_index("gx"), lax.axis_index("gy"), lax.axis_index("gz")
     f32 = jnp.float32
-    place = slab_place(gx, gz)
-    index = 4 * gz + place
-
-    def owner_of(place, z):
-        order = jnp.where(z % 2 == 0, place, 3 - place)
-        return jnp.where(order < 2, order, 5 - order)
-
-    partner = jnp.stack([gx ^ owner_of(t, gz) for t in range(4)]).astype(jnp.int32)
+    index = 4 * gz + slab_place(gx, gz)
     packed = pl.pallas_call(
         pack_kernel,
-        out_shape=jax.ShapeDtypeStruct((4, 8, 16, LANES), f32),
-        in_specs=[smem, smem] + vmem_specs(7),
-        out_specs=vmem_specs(1)[0],
+        out_shape=[pltpu.VMEM((8, 16, LANES), f32)] * 4,
+        in_specs=[smem] + vmem_specs(7),
+        out_specs=vmem_specs(4),
+        scratch_shapes=[pltpu.VMEM((4, 8, 16, LANES), f32)],
         name="pack",
-    )(partner, modulus, cell_weight, weight_grad, material, node_mass, pinned, positions, forces)
+    )(modulus, cell_weight, weight_grad, material, node_mass, pinned, positions, forces)
 
     mine = [packed[0]]
     for j in range(1, 4):
@@ -731,19 +744,13 @@
     before = jnp.where(odd_place, even, odd)
     after = jnp.where(odd_place, odd, even)
 
-    gx_before = owner_of((index - 1) % 4, (index - 1) // 4)
-    gx_after = owner_of((index + 1) % 4, (index + 1) // 4)
-    scalars = jnp.stack(
-        [gx_before, gx, gx_after, (index > 0).astype(jnp.int32), (index < 15).astype(jnp.int32), gy]
-    ).astype(jnp.int32)
-
     def buf(*dims):
         return pltpu.VMEM(tuple(dims) + TILE, f32)
 
     message = pl.pallas_call(
         cycle_kernel,
-        out_shape=[jax.ShapeDtypeStruct((104, LANES), f32)] * 4,
-        in_specs=[smem] + vmem_specs(3),
+        out_shape=[pltpu.VMEM((104, LANES), f32)] * 4,
+        in_specs=vmem_specs(3),
         out_specs=vmem_specs(4),
         scratch_shapes=[
             buf(8, 4, 4, 4), buf(5, 5, 5), buf(27, 4, 4, 4), buf(4, 4, 4),
@@ -756,7 +763,7 @@
         ],
         compiler_params=pltpu.CompilerParams(vmem_limit_bytes=48 * 1024 * 1024),
         name="cycle",
-    )(scalars, before, own, after)
+    )(before, own, after)
 
     back = [message[0]]
     for j in range(1, 4):
@@ -767,11 +774,11 @@
             jax.ShapeDtypeStruct(positions.shape, f32),
             jax.ShapeDtypeStruct((27, 2, 8, 64), f32),
         ],
-        in_specs=[smem] + vmem_specs(4),
+        in_specs=vmem_specs(4),
         out_specs=vmem_specs(2),
         scratch_shapes=[pltpu.VMEM((4, 104, LANES), f32)],
         name="unpack",
-    )(partner, *back)
+    )(*back)
 
 
 def solution(mesh):

time: 51.5 us -> 49 us (0.951)
  waiting for transfers between devices: 14.1 us -> 16.4 us
  starting transfers between devices: 10.7 us -> 9.05 us
  Pallas kernels: 22.4 us -> 21.1 us
  local copies, waits for them, and re-layouts: 2.28 us -> 1.24 us
  other arithmetic: 0.99 us -> 0.34 us
    ppermute x2, waiting for transfers between devices: 6.06 us -> 7.78 us  [swap_in_chain(): return lax.ppermute(mine, ('gx', 'gy', 'gz'), pairs)]
    ppermute x2, starting transfers between devices: 2.11 us -> 0.87 us  [swap_in_chain(): return lax.ppermute(mine, ('gx', 'gy', 'gz'), pairs)]
    pallas_call x2, Pallas kernels: 20.3 us -> 19.1 us  [the longest x1 17.7 us: shards_by_slab(): pl.pallas_call(cycle_kernel, out_shape=[pltpu.VMEM((104, LANES), f32)] *...]
    ppermute x3, waiting for transfers between devices: 4.13 us -> 5.14 us  [shards_by_slab(): mine.append(lax.ppermute(packed[j], 'gx', [(i, i ^ j) for i in range(4)]))]
    slice x1 -> x0, local copies, waits for them, and re-layouts: 0.95 us -> none  [shards_by_slab(): mine = [packed[0]]]
    another operation x1 -> x0, other arithmetic: 0.65 us -> none  [shards_by_slab(): jnp.stack([gx ^ owner_of(t, gz) for t in range(4)]).astype(jnp.int32)]
  transfers between devices with their start and end apart: 11 -> 11, of which waited for: 8 -> 9; matrix products, arithmetic and copies ran while one was open for 0% -> 0% of each run, Pallas kernels for 0% -> 0%
where the time goes in v4:
time: 49 us; the launch traced here: 48.8 us
  Pallas kernels  21.1 us (43%)
  waiting for transfers between devices  16.4 us (33%)
  starting transfers between devices  9.05 us (18%)
  local copies, waits for them, and re-layouts  1.24 us (3%)
  between operations  0.73 us (1%)
    pallas_call x1, Pallas kernels, shards_by_slab(): pl.pallas_call(cycle_kernel, out_shape=[pltpu.VMEM((104, LANES), f32)] *...  17.7 us
    ppermute x2, waiting for transfers between devices, swap_in_chain(): return lax.ppermute(mine, ('gx', 'gy', 'gz'), pairs)  7.78 us
    ppermute x3, waiting for transfers between devices, shards_by_slab(): mine.append(lax.ppermute(packed[j], 'gx', [(i, i ^ j) for i in range(4)]))  5.14 us
    ppermute x3, starting transfers between devices, shards_by_slab(): mine.append(lax.ppermute(packed[j], 'gx', [(i, i ^ j) for i in range(4)]))  4.54 us
    ppermute x3, starting transfers between devices, shards_by_slab(): back.append(lax.ppermute(message[j], 'gx', [(i, i ^ j) for i in range(4)]))  3.49 us
    ppermute x3, waiting for transfers between devices, shards_by_slab(): back.append(lax.ppermute(message[j], 'gx', [(i, i ^ j) for i in range(4)]))  2.11 us
    pallas_call x1, Pallas kernels, shards_by_slab(): pl.pallas_call(unpack_kernel, out_shape=[jax.ShapeDtypeStruct(positions.s...  1.98 us
    pallas_call x1, Pallas kernels, shards_by_slab(): pl.pallas_call(pack_kernel, out_shape=[pltpu.VMEM((8, 16, LANES), f32)] *...  1.45 us
  transfers between devices with their start and end apart: 11, of which 9 were waited for; matrix products, arithmetic and copies ran while one was open for 0% of the time, Pallas kernels for 0%

profile of v4, /device:TPU:0, one launch (start us, length us, event | category | flops | bytes accessed | tf_op | source)
XLA Modules:
  0.0 48.8 jit_solution(2766207726428918941)
XLA Ops:
  0.6 1.5 %pack.1 = (f32[8,16,128]{2,1,0:T(8,128)S(1)}, f32[8,16,128]{2,1,0:T(8,128)S(1)}, f32[8,16,128]{2,1,0:T(8,128)S(1)}, f32[8,16,128]{2,1,0:T(8,128)S(1)}) custom-call(f32[8]{0:T(128)} %mod_ref.1, f32[4,16,128]{2,1,0:T(8,128)} %cw_ref.1, f32[4,16,128]{2,1,0:T(8,128)} %wg_ref.1, s32[4,16,128]{2,1,0:T(8,128)} %mat_ref.1, f32[4,16,128]{2,1,0:T(8,128)} %mass_ref.1, ...), custom_call_target="tpu_custom_call" | custom-call | tf_op jit(solution)/shard_map/pack/pallas_call | solution.py:709
  2.1 3.0 %collective-permute-start = (f32[8,16,128]{2,1,0:T(8,128)S(1)}, f32[8,16,128]{2,1,0:T(8,128)S(1)}, u32[]{:S(2)}, u32[]{:S(2)}) collective-permute-start(f32[8,16,128]{2,1,0:T(8,128)S(1)} %get-tuple-element.11), channel_id=1, source_target_pairs={{0,8},{8,0},{16,24},{24,16},{1,9},{9,1},{17,25},{25,17},{2,10},{10... | collective-permute-start | bytes 196616 | tf_op jit(solution)/shard_map/ppermute | solution.py:720
  5.1 1.5 %collective-permute-start.1 = (f32[8,16,128]{2,1,0:T(8,128)S(1)}, f32[8,16,128]{2,1,0:T(8,128)S(1)}, u32[]{:S(2)}, u32[]{:S(2)}) collective-permute-start(f32[8,16,128]{2,1,0:T(8,128)S(1)} %get-tuple-element.12), channel_id=1, source_target_pairs={{0,16},{8,24},{16,0},{24,8},{1,17},{9,25},{17,1},{25,9},{2,18},{10... | collective-permute-start | bytes 196616 | tf_op jit(solution)/shard_map/ppermute | solution.py:720
  6.6 0.0 collective-permute-start.2
  6.6 0.8 %collective-permute-done = f32[8,16,128]{2,1,0:T(8,128)S(1)} collective-permute-done((f32[8,16,128]{2,1,0:T(8,128)S(1)}, f32[8,16,128]{2,1,0:T(8,128)S(1)}, u32[]{:S(2)}, u32[]{:S(2)}) %collective-permute-start) | collective-permute-done | bytes 65568 | tf_op jit(solution)/shard_map/ppermute | solution.py:720
  7.5 1.9 %collective-permute-done.1 = f32[8,16,128]{2,1,0:T(8,128)S(1)} collective-permute-done((f32[8,16,128]{2,1,0:T(8,128)S(1)}, f32[8,16,128]{2,1,0:T(8,128)S(1)}, u32[]{:S(2)}, u32[]{:S(2)}) %collective-permute-start.1) | collective-permute-done | bytes 65568 | tf_op jit(solution)/shard_map/ppermute | solution.py:720
  9.4 2.4 %collective-permute-done.2 = f32[8,16,128]{2,1,0:T(8,128)S(1)} collective-permute-done((f32[8,16,128]{2,1,0:T(8,128)S(1)}, f32[8,16,128]{2,1,0:T(8,128)S(1)}, u32[]{:S(2)}, u32[]{:S(2)}) %collective-permute-start.2) | collective-permute-done | bytes 65568 | tf_op jit(solution)/shard_map/ppermute | solution.py:720
  11.8 0.1 collective-permute-start.5
  11.9 0.8 %collective-permute-start.3 = (f32[4,8,16,128]{3,2,1,0:T(8,128)S(1)}, f32[4,8,16,128]{3,2,1,0:T(8,128)S(1)}, u32[]{:S(2)}, u32[]{:S(2)}) collective-permute-start(f32[4,8,16,128]{3,2,1,0:T(8,128)S(1)} %pad_maximum_fusion.2), channel_id=1, source_target_pairs={{0,8},{8,0},{24,16},{16,24},{17,25},{25,17},{9,1},{1,9},{2,10},{10... | collective-permute-start | bytes 786440 | tf_op jit(solution)/shard_map/ppermute | solution.py:731
  12.7 0.0 collective-permute-start.7
  12.7 0.7 %collective-permute-done.5 = f32[4,8,16,128]{3,2,1,0:T(8,128)S(1)} collective-permute-done((f32[4,8,16,128]{3,2,1,0:T(8,128)S(1)}, f32[4,8,16,128]{3,2,1,0:T(8,128)S(1)}, u32[]{:S(2)}, u32[]{:S(2)}) %collective-permute-start.5) | collective-permute-done | bytes 262176 | tf_op jit(solution)/shard_map/ppermute | solution.py:731
  13.4 0.1 collective-permute-start.6
  13.5 7.1 %collective-permute-done.3 = f32[4,8,16,128]{3,2,1,0:T(8,128)S(1)} collective-permute-done((f32[4,8,16,128]{3,2,1,0:T(8,128)S(1)}, f32[4,8,16,128]{3,2,1,0:T(8,128)S(1)}, u32[]{:S(2)}, u32[]{:S(2)}) %collective-permute-start.3) | collective-permute-done | bytes 262176 | tf_op jit(solution)/shard_map/ppermute | solution.py:731
  20.6 0.0 collective-permute-start.4
  20.6 0.0 collective-permute-done.7
  20.7 0.1 pad_maximum_fusion.1.own_ref
  20.7 0.0 collective-permute-done.6
  20.8 1.4 %collective-permute-done.4 = f32[4,8,16,128]{3,2,1,0:T(8,128)S(1)} collective-permute-done((f32[4,8,16,128]{3,2,1,0:T(8,128)S(1)}, f32[4,8,16,128]{3,2,1,0:T(8,128)S(1)}, u32[]{:S(2)}, u32[]{:S(2)}) %collective-permute-start.4) | collective-permute-done | bytes 262176 | tf_op jit(solution)/shard_map/ppermute | solution.py:736
  22.2 0.1 fusion
  22.3 17.7 %cycle.1 = (f32[104,128]{1,0:T(8,128)S(1)}, f32[104,128]{1,0:T(8,128)S(1)}, f32[104,128]{1,0:T(8,128)S(1)}, f32[104,128]{1,0:T(8,128)S(1)}) custom-call(f32[4,8,32,128]{3,2,1,0:T(8,128)S(1)} %get-tuple-element.19.prev_ref, f32[4,8,32,128]{3,2,1,0:T(8,128)S(1)} %pad_maximum_fusion.1.own_ref, f32[4,8,32,128]{3,2,1,0:T(8,128)S(1)} %get-tuple-element.18.next_ref), custom_call_target="tpu_custom_call" | custom-call | tf_op jit(solution)/shard_map/cycle/pallas_call | solution.py:750
  40.0 0.0 copy-start
  40.0 0.6 %copy-done = f32[104,128]{1,0:T(8,128)} copy-done((f32[104,128]{1,0:T(8,128)}, f32[104,128]{1,0:T(8,128)S(1)}, u32[]{:S(2)}) %copy-start) | copy-done | bytes 53272
  40.6 0.3 collective-permute-start.8
  40.9 0.0 collective-permute-start.9
  40.9 3.2 %collective-permute-start.10 = (f32[104,128]{1,0:T(8,128)S(1)}, f32[104,128]{1,0:T(8,128)S(1)}, u32[]{:S(2)}, u32[]{:S(2)}) collective-permute-start(f32[104,128]{1,0:T(8,128)S(1)} %get-tuple-element.17), channel_id=1, source_target_pairs={{0,24},{8,16},{16,8},{24,0},{1,25},{9,17},{17,9},{25,1},{2,26},{10... | collective-permute-start | bytes 159752 | tf_op jit(solution)/shard_map/ppermute | solution.py:770
  44.1 1.0 %collective-permute-done.8.one_ref = f32[104,128]{1,0:T(8,128)S(1)} collective-permute-done((f32[104,128]{1,0:T(8,128)S(1)}, f32[104,128]{1,0:T(8,128)S(1)}, u32[]{:S(2)}, u32[]{:S(2)}) %collective-permute-start.8) | collective-permute-done | bytes 53280 | tf_op jit(solution)/shard_map/ppermute | solution.py:770
  45.1 0.0 copy-start.1
  45.1 0.5 %collective-permute-done.9.two_ref = f32[104,128]{1,0:T(8,128)S(1)} collective-permute-done((f32[104,128]{1,0:T(8,128)S(1)}, f32[104,128]{1,0:T(8,128)S(1)}, u32[]{:S(2)}, u32[]{:S(2)}) %collective-permute-start.9) | collective-permute-done | bytes 53280 | tf_op jit(solution)/shard_map/ppermute | solution.py:770
  45.6 0.0 copy-start.2
  45.6 0.6 %collective-permute-done.10.three_ref = f32[104,128]{1,0:T(8,128)S(1)} collective-permute-done((f32[104,128]{1,0:T(8,128)S(1)}, f32[104,128]{1,0:T(8,128)S(1)}, u32[]{:S(2)}, u32[]{:S(2)}) %collective-permute-start.10) | collective-permute-done | bytes 53280 | tf_op jit(solution)/shard_map/ppermute | solution.py:770
  46.2 0.0 copy-start.3
  46.2 0.0 copy-done.1
  46.2 0.0 copy-done.2
  46.2 0.6 %copy-done.3 = f32[104,128]{1,0:T(8,128)} copy-done((f32[104,128]{1,0:T(8,128)}, f32[104,128]{1,0:T(8,128)S(1)}, u32[]{:S(2)}) %copy-start.3) | copy-done | bytes 53272
  46.9 2.0 %unpack.1 = (f32[3,4,16,128]{3,2,1,0:T(8,128)}, f32[27,2,8,64]{3,2,1,0:T(8,128)}) custom-call(f32[104,128]{1,0:T(8,128)} %copy-done, f32[104,128]{1,0:T(8,128)} %copy-done.1, f32[104,128]{1,0:T(8,128)} %copy-done.2, f32[104,128]{1,0:T(8,128)} %copy-done.3), custom_call_target="tpu_custom_call" | custom-call | tf_op jit(solution)/shard_map/unpack/pallas_call | solution.py:771
  (4 shorter events, 0.1 us)
Async XLA Ops:
  2.1 5.4 %collective-permute-start = (f32[8,16,128]{2,1,0:T(8,128)S(1)}, f32[8,16,128]{2,1,0:T(8,128)S(1)}, u32[]{:S(2)}, u32[]{:S(2)}) collective-permute-start(f32[8,16,128]{2,1,0:T(8,128)S(1)} %get-tuple-element.11), channel_id=1, source_target_pairs={{0,8},{8,0},{16,24},{24,16},{1,9},{9,1},{17,25},{25,17},{2,10},{10... | collective-permute-start | bytes 196616 | tf_op jit(solution)/shard_map/ppermute | solution.py:720
  5.1 4.3 %collective-permute-start.1 = (f32[8,16,128]{2,1,0:T(8,128)S(1)}, f32[8,16,128]{2,1,0:T(8,128)S(1)}, u32[]{:S(2)}, u32[]{:S(2)}) collective-permute-start(f32[8,16,128]{2,1,0:T(8,128)S(1)} %get-tuple-element.12), channel_id=1, source_target_pairs={{0,16},{8,24},{16,0},{24,8},{1,17},{9,25},{17,1},{25,9},{2,18},{10... | collective-permute-start | bytes 196616 | tf_op jit(solution)/shard_map/ppermute | solution.py:720
  6.6 5.2 %collective-permute-start.2 = (f32[8,16,128]{2,1,0:T(8,128)S(1)}, f32[8,16,128]{2,1,0:T(8,128)S(1)}, u32[]{:S(2)}, u32[]{:S(2)}) collective-permute-start(f32[8,16,128]{2,1,0:T(8,128)S(1)} %get-tuple-element.13), channel_id=1, source_target_pairs={{0,24},{8,16},{16,8},{24,0},{1,25},{9,17},{17,9},{25,1},{2,26},{10... | collective-permute-start | bytes 196616 | tf_op jit(solution)/shard_map/ppermute | solution.py:720
  11.8 1.6 %collective-permute-start.5 = (f32[4,8,16,128]{3,2,1,0:T(8,128)S(1)}, f32[4,8,16,128]{3,2,1,0:T(8,128)S(1)}, u32[]{:S(2)}, u32[]{:S(2)}) collective-permute-start(f32[4,8,16,128]{3,2,1,0:T(8,128)S(1)} %pad_maximum_fusion.2), channel_id=1, source_target_pairs={{8,24},{24,8},{16,17},{17,16},{25,9},{9,25},{1,2},{2,1},{10,26},{2... | collective-permute-start | bytes 786440 | tf_op jit(solution)/shard_map/ppermute | solution.py:731
  11.9 8.7 %collective-permute-start.3 = (f32[4,8,16,128]{3,2,1,0:T(8,128)S(1)}, f32[4,8,16,128]{3,2,1,0:T(8,128)S(1)}, u32[]{:S(2)}, u32[]{:S(2)}) collective-permute-start(f32[4,8,16,128]{3,2,1,0:T(8,128)S(1)} %pad_maximum_fusion.2), channel_id=1, source_target_pairs={{0,8},{8,0},{24,16},{16,24},{17,25},{25,17},{9,1},{1,9},{2,10},{10... | collective-permute-start | bytes 786440 | tf_op jit(solution)/shard_map/ppermute | solution.py:731
  12.7 7.9 %collective-permute-start.7 = (f32[4,8,16,128]{3,2,1,0:T(8,128)S(1)}, f32[4,8,16,128]{3,2,1,0:T(8,128)S(1)}, u32[]{:S(2)}, u32[]{:S(2)}) collective-permute-start(f32[4,8,16,128]{3,2,1,0:T(8,128)S(1)} %pad_maximum_fusion.2), channel_id=1, source_target_pairs={{0,4},{4,0},{1,5},{5,1},{2,6},{6,2},{3,7},{7,3},{8,12},{12,8},{9,1... | collective-permute-start | bytes 786440 | tf_op jit(solution)/shard_map/ppermute | solution.py:736
  13.4 7.3 %collective-permute-start.6 = (f32[4,8,16,128]{3,2,1,0:T(8,128)S(1)}, f32[4,8,16,128]{3,2,1,0:T(8,128)S(1)}, u32[]{:S(2)}, u32[]{:S(2)}) collective-permute-start(f32[4,8,16,128]{3,2,1,0:T(8,128)S(1)} %collective-permute-done.5), channel_id=1, source_target_pairs={{0,4},{4,0},{1,5},{5,1},{2,6},{6,2},{3,7},{7,3},{8,12},{12,8},{9,1... | collective-permute-start | bytes 786440 | tf_op jit(solution)/shard_map/ppermute | solution.py:736
  20.6 1.5 %collective-permute-start.4 = (f32[4,8,16,128]{3,2,1,0:T(8,128)S(1)}, f32[4,8,16,128]{3,2,1,0:T(8,128)S(1)}, u32[]{:S(2)}, u32[]{:S(2)}) collective-permute-start(f32[4,8,16,128]{3,2,1,0:T(8,128)S(1)} %collective-permute-done.3), channel_id=1, source_target_pairs={{0,4},{4,0},{1,5},{5,1},{2,6},{6,2},{3,7},{7,3},{8,12},{12,8},{9,1... | collective-permute-start | bytes 786440 | tf_op jit(solution)/shard_map/ppermute | solution.py:736
  40.0 0.6 %copy-start = (f32[104,128]{1,0:T(8,128)}, f32[104,128]{1,0:T(8,128)S(1)}, u32[]{:S(2)}) copy-start(f32[104,128]{1,0:T(8,128)S(1)} %get-tuple-element.14.own_ref) | copy-start | bytes 159748
  40.6 4.4 %collective-permute-start.8 = (f32[104,128]{1,0:T(8,128)S(1)}, f32[104,128]{1,0:T(8,128)S(1)}, u32[]{:S(2)}, u32[]{:S(2)}) collective-permute-start(f32[104,128]{1,0:T(8,128)S(1)} %get-tuple-element.15), channel_id=1, source_target_pairs={{0,8},{8,0},{16,24},{24,16},{1,9},{9,1},{17,25},{25,17},{2,10},{10... | collective-permute-start | bytes 159752 | tf_op jit(solution)/shard_map/ppermute | solution.py:770
  40.9 4.7 %collective-permute-start.9 = (f32[104,128]{1,0:T(8,128)S(1)}, f32[104,128]{1,0:T(8,128)S(1)}, u32[]{:S(2)}, u32[]{:S(2)}) collective-permute-start(f32[104,128]{1,0:T(8,128)S(1)} %get-tuple-element.16), channel_id=1, source_target_pairs={{0,16},{8,24},{16,0},{24,8},{1,17},{9,25},{17,1},{25,9},{2,18},{10... | collective-permute-start | bytes 159752 | tf_op jit(solution)/shard_map/ppermute | solution.py:770
  40.9 5.3 %collective-permute-start.10 = (f32[104,128]{1,0:T(8,128)S(1)}, f32[104,128]{1,0:T(8,128)S(1)}, u32[]{:S(2)}, u32[]{:S(2)}) collective-permute-start(f32[104,128]{1,0:T(8,128)S(1)} %get-tuple-element.17), channel_id=1, source_target_pairs={{0,24},{8,16},{16,8},{24,0},{1,25},{9,17},{17,9},{25,1},{2,26},{10... | collective-permute-start | bytes 159752 | tf_op jit(solution)/shard_map/ppermute | solution.py:770
  45.1 1.2 %copy-start.1 = (f32[104,128]{1,0:T(8,128)}, f32[104,128]{1,0:T(8,128)S(1)}, u32[]{:S(2)}) copy-start(f32[104,128]{1,0:T(8,128)S(1)} %collective-permute-done.8.one_ref) | copy-start | bytes 159748
  45.6 0.6 %copy-start.2 = (f32[104,128]{1,0:T(8,128)}, f32[104,128]{1,0:T(8,128)S(1)}, u32[]{:S(2)}) copy-start(f32[104,128]{1,0:T(8,128)S(1)} %collective-permute-done.9.two_ref) | copy-start | bytes 159748
  46.2 0.6 %copy-start.3 = (f32[104,128]{1,0:T(8,128)}, f32[104,128]{1,0:T(8,128)S(1)}, u32[]{:S(2)}) copy-start(f32[104,128]{1,0:T(8,128)S(1)} %collective-permute-done.10.three_ref) | copy-start | bytes 159748

commit v5 on v4

--- a/solution.py
+++ b/solution.py
@@ -777,6 +777,7 @@
         in_specs=vmem_specs(4),
         out_specs=vmem_specs(2),
         scratch_shapes=[pltpu.VMEM((4, 104, LANES), f32)],
+        compiler_params=pltpu.CompilerParams(vmem_limit_bytes=8 * 1024 * 1024),
         name="unpack",
     )(*back)
 

time: 49 us -> 46.9 us (0.957)
  local copies, waits for them, and re-layouts: 1.24 us -> 0 us
  Pallas kernels: 21.1 us -> 20.2 us
    unnamed x8 -> x0, local copies, waits for them, and re-layouts: 1.24 us -> none
    pallas_call x1, Pallas kernels: 1.98 us -> 1.1 us  [shards_by_slab(): pl.pallas_call(unpack_kernel, out_shape=[jax.ShapeDtypeStruct(positions.s...]
where the time goes in v5:
time: 46.9 us; the launch traced here: 46.8 us
  Pallas kernels  20.2 us (43%)
  waiting for transfers between devices  16.4 us (35%)
  starting transfers between devices  9.11 us (19%)
  between operations  0.72 us (2%)
    pallas_call x1, Pallas kernels, shards_by_slab(): pl.pallas_call(cycle_kernel, out_shape=[pltpu.VMEM((104, LANES), f32)] *...  17.7 us
    ppermute x2, waiting for transfers between devices, swap_in_chain(): return lax.ppermute(mine, ('gx', 'gy', 'gz'), pairs)  7.78 us
    ppermute x3, waiting for transfers between devices, shards_by_slab(): mine.append(lax.ppermute(packed[j], 'gx', [(i, i ^ j) for i in range(4)]))  5.14 us
    ppermute x3, starting transfers between devices, shards_by_slab(): mine.append(lax.ppermute(packed[j], 'gx', [(i, i ^ j) for i in range(4)]))  4.54 us
    ppermute x3, starting transfers between devices, shards_by_slab(): back.append(lax.ppermute(message[j], 'gx', [(i, i ^ j) for i in range(4)]))  3.55 us
    ppermute x3, waiting for transfers between devices, shards_by_slab(): back.append(lax.ppermute(message[j], 'gx', [(i, i ^ j) for i in range(4)]))  2.11 us
    pallas_call x1, Pallas kernels, shards_by_slab(): pl.pallas_call(pack_kernel, out_shape=[pltpu.VMEM((8, 16, LANES), f32)] *...  1.45 us
    ppermute x3, waiting for transfers between devices, both_halves(): other = lax.ppermute(half, 'gy', [(0, 1), (1, 0)])  1.36 us
  transfers between devices with their start and end apart: 11, of which 9 were waited for; matrix products, arithmetic and copies ran while one was open for 0% of the time, Pallas kernels for 0%

profile of v5, /device:TPU:0, one launch (start us, length us, event | category | flops | bytes accessed | tf_op | source)
XLA Modules:
  0.0 46.8 jit_solution(14711752978825940335)
XLA Ops:
  0.6 1.5 %pack.1 = (f32[8,16,128]{2,1,0:T(8,128)S(1)}, f32[8,16,128]{2,1,0:T(8,128)S(1)}, f32[8,16,128]{2,1,0:T(8,128)S(1)}, f32[8,16,128]{2,1,0:T(8,128)S(1)}) custom-call(f32[8]{0:T(128)} %mod_ref.1, f32[4,16,128]{2,1,0:T(8,128)} %cw_ref.1, f32[4,16,128]{2,1,0:T(8,128)} %wg_ref.1, s32[4,16,128]{2,1,0:T(8,128)} %mat_ref.1, f32[4,16,128]{2,1,0:T(8,128)} %mass_ref.1, ...), custom_call_target="tpu_custom_call" | custom-call | tf_op jit(solution)/shard_map/pack/pallas_call | solution.py:709
  2.1 3.0 %collective-permute-start = (f32[8,16,128]{2,1,0:T(8,128)S(1)}, f32[8,16,128]{2,1,0:T(8,128)S(1)}, u32[]{:S(2)}, u32[]{:S(2)}) collective-permute-start(f32[8,16,128]{2,1,0:T(8,128)S(1)} %get-tuple-element.11), channel_id=1, source_target_pairs={{0,8},{8,0},{16,24},{24,16},{1,9},{9,1},{17,25},{25,17},{2,10},{10... | collective-permute-start | bytes 196616 | tf_op jit(solution)/shard_map/ppermute | solution.py:720
  5.1 1.5 %collective-permute-start.1 = (f32[8,16,128]{2,1,0:T(8,128)S(1)}, f32[8,16,128]{2,1,0:T(8,128)S(1)}, u32[]{:S(2)}, u32[]{:S(2)}) collective-permute-start(f32[8,16,128]{2,1,0:T(8,128)S(1)} %get-tuple-element.12), channel_id=1, source_target_pairs={{0,16},{8,24},{16,0},{24,8},{1,17},{9,25},{17,1},{25,9},{2,18},{10... | collective-permute-start | bytes 196616 | tf_op jit(solution)/shard_map/ppermute | solution.py:720
  6.6 0.0 collective-permute-start.2
  6.6 0.8 %collective-permute-done = f32[8,16,128]{2,1,0:T(8,128)S(1)} collective-permute-done((f32[8,16,128]{2,1,0:T(8,128)S(1)}, f32[8,16,128]{2,1,0:T(8,128)S(1)}, u32[]{:S(2)}, u32[]{:S(2)}) %collective-permute-start) | collective-permute-done | bytes 65568 | tf_op jit(solution)/shard_map/ppermute | solution.py:720
  7.5 1.9 %collective-permute-done.1 = f32[8,16,128]{2,1,0:T(8,128)S(1)} collective-permute-done((f32[8,16,128]{2,1,0:T(8,128)S(1)}, f32[8,16,128]{2,1,0:T(8,128)S(1)}, u32[]{:S(2)}, u32[]{:S(2)}) %collective-permute-start.1) | collective-permute-done | bytes 65568 | tf_op jit(solution)/shard_map/ppermute | solution.py:720
  9.4 2.4 %collective-permute-done.2 = f32[8,16,128]{2,1,0:T(8,128)S(1)} collective-permute-done((f32[8,16,128]{2,1,0:T(8,128)S(1)}, f32[8,16,128]{2,1,0:T(8,128)S(1)}, u32[]{:S(2)}, u32[]{:S(2)}) %collective-permute-start.2) | collective-permute-done | bytes 65568 | tf_op jit(solution)/shard_map/ppermute | solution.py:720
  11.8 0.1 collective-permute-start.5
  11.9 0.8 %collective-permute-start.3 = (f32[4,8,16,128]{3,2,1,0:T(8,128)S(1)}, f32[4,8,16,128]{3,2,1,0:T(8,128)S(1)}, u32[]{:S(2)}, u32[]{:S(2)}) collective-permute-start(f32[4,8,16,128]{3,2,1,0:T(8,128)S(1)} %pad_maximum_fusion.2), channel_id=1, source_target_pairs={{0,8},{8,0},{24,16},{16,24},{17,25},{25,17},{9,1},{1,9},{2,10},{10... | collective-permute-start | bytes 786440 | tf_op jit(solution)/shard_map/ppermute | solution.py:731
  12.7 0.0 collective-permute-start.7
  12.7 0.7 %collective-permute-done.5 = f32[4,8,16,128]{3,2,1,0:T(8,128)S(1)} collective-permute-done((f32[4,8,16,128]{3,2,1,0:T(8,128)S(1)}, f32[4,8,16,128]{3,2,1,0:T(8,128)S(1)}, u32[]{:S(2)}, u32[]{:S(2)}) %collective-permute-start.5) | collective-permute-done | bytes 262176 | tf_op jit(solution)/shard_map/ppermute | solution.py:731
  13.4 0.1 collective-permute-start.6
  13.5 7.1 %collective-permute-done.3 = f32[4,8,16,128]{3,2,1,0:T(8,128)S(1)} collective-permute-done((f32[4,8,16,128]{3,2,1,0:T(8,128)S(1)}, f32[4,8,16,128]{3,2,1,0:T(8,128)S(1)}, u32[]{:S(2)}, u32[]{:S(2)}) %collective-permute-start.3) | collective-permute-done | bytes 262176 | tf_op jit(solution)/shard_map/ppermute | solution.py:731
  20.6 0.0 collective-permute-start.4
  20.6 0.0 collective-permute-done.7
  20.7 0.1 pad_maximum_fusion.1.own_ref
  20.7 0.0 collective-permute-done.6
  20.8 1.4 %collective-permute-done.4 = f32[4,8,16,128]{3,2,1,0:T(8,128)S(1)} collective-permute-done((f32[4,8,16,128]{3,2,1,0:T(8,128)S(1)}, f32[4,8,16,128]{3,2,1,0:T(8,128)S(1)}, u32[]{:S(2)}, u32[]{:S(2)}) %collective-permute-start.4) | collective-permute-done | bytes 262176 | tf_op jit(solution)/shard_map/ppermute | solution.py:736
  22.2 0.1 fusion
  22.3 17.7 %cycle.1 = (f32[104,128]{1,0:T(8,128)S(1)}, f32[104,128]{1,0:T(8,128)S(1)}, f32[104,128]{1,0:T(8,128)S(1)}, f32[104,128]{1,0:T(8,128)S(1)}) custom-call(f32[4,8,32,128]{3,2,1,0:T(8,128)S(1)} %get-tuple-element.19.prev_ref, f32[4,8,32,128]{3,2,1,0:T(8,128)S(1)} %pad_maximum_fusion.1.own_ref, f32[4,8,32,128]{3,2,1,0:T(8,128)S(1)} %get-tuple-element.18.next_ref), custom_call_target="tpu_custom_call" | custom-call | tf_op jit(solution)/shard_map/cycle/pallas_call | solution.py:750
  40.0 0.3 collective-permute-start.8
  40.3 0.0 collective-permute-start.9
  40.4 3.2 %collective-permute-start.10 = (f32[104,128]{1,0:T(8,128)S(1)}, f32[104,128]{1,0:T(8,128)S(1)}, u32[]{:S(2)}, u32[]{:S(2)}) collective-permute-start(f32[104,128]{1,0:T(8,128)S(1)} %get-tuple-element.17), channel_id=1, source_target_pairs={{0,24},{8,16},{16,8},{24,0},{1,25},{9,17},{17,9},{25,1},{2,26},{10... | collective-permute-start | bytes 159752 | tf_op jit(solution)/shard_map/ppermute | solution.py:770
  43.6 0.9 %collective-permute-done.8.one_ref = f32[104,128]{1,0:T(8,128)S(1)} collective-permute-done((f32[104,128]{1,0:T(8,128)S(1)}, f32[104,128]{1,0:T(8,128)S(1)}, u32[]{:S(2)}, u32[]{:S(2)}) %collective-permute-start.8) | collective-permute-done | bytes 53280 | tf_op jit(solution)/shard_map/ppermute | solution.py:770
  44.4 0.6 %collective-permute-done.9.two_ref = f32[104,128]{1,0:T(8,128)S(1)} collective-permute-done((f32[104,128]{1,0:T(8,128)S(1)}, f32[104,128]{1,0:T(8,128)S(1)}, u32[]{:S(2)}, u32[]{:S(2)}) %collective-permute-start.9) | collective-permute-done | bytes 53280 | tf_op jit(solution)/shard_map/ppermute | solution.py:770
  45.0 0.6 %collective-permute-done.10.three_ref = f32[104,128]{1,0:T(8,128)S(1)} collective-permute-done((f32[104,128]{1,0:T(8,128)S(1)}, f32[104,128]{1,0:T(8,128)S(1)}, u32[]{:S(2)}, u32[]{:S(2)}) %collective-permute-start.10) | collective-permute-done | bytes 53280 | tf_op jit(solution)/shard_map/ppermute | solution.py:770
  45.7 1.1 %unpack.1 = (f32[3,4,16,128]{3,2,1,0:T(8,128)}, f32[27,2,8,64]{3,2,1,0:T(8,128)}) custom-call(f32[104,128]{1,0:T(8,128)S(1)} %get-tuple-element.14.own_ref, f32[104,128]{1,0:T(8,128)S(1)} %collective-permute-done.8.one_ref, f32[104,128]{1,0:T(8,128)S(1)} %collective-permute-done.9.two_ref, f32[104,128]{1,0:T(8,128)S(1)} %collective-permute-done.10.three_ref), custom_call_target="tpu_custom_call" | custom-call | tf_op jit(solution)/shard_map/unpack/pallas_call | solution.py:771
  (4 shorter events, 0.1 us)
Async XLA Ops:
  2.1 5.4 %collective-permute-start = (f32[8,16,128]{2,1,0:T(8,128)S(1)}, f32[8,16,128]{2,1,0:T(8,128)S(1)}, u32[]{:S(2)}, u32[]{:S(2)}) collective-permute-start(f32[8,16,128]{2,1,0:T(8,128)S(1)} %get-tuple-element.11), channel_id=1, source_target_pairs={{0,8},{8,0},{16,24},{24,16},{1,9},{9,1},{17,25},{25,17},{2,10},{10... | collective-permute-start | bytes 196616 | tf_op jit(solution)/shard_map/ppermute | solution.py:720
  5.1 4.3 %collective-permute-start.1 = (f32[8,16,128]{2,1,0:T(8,128)S(1)}, f32[8,16,128]{2,1,0:T(8,128)S(1)}, u32[]{:S(2)}, u32[]{:S(2)}) collective-permute-start(f32[8,16,128]{2,1,0:T(8,128)S(1)} %get-tuple-element.12), channel_id=1, source_target_pairs={{0,16},{8,24},{16,0},{24,8},{1,17},{9,25},{17,1},{25,9},{2,18},{10... | collective-permute-start | bytes 196616 | tf_op jit(solution)/shard_map/ppermute | solution.py:720
  6.6 5.2 %collective-permute-start.2 = (f32[8,16,128]{2,1,0:T(8,128)S(1)}, f32[8,16,128]{2,1,0:T(8,128)S(1)}, u32[]{:S(2)}, u32[]{:S(2)}) collective-permute-start(f32[8,16,128]{2,1,0:T(8,128)S(1)} %get-tuple-element.13), channel_id=1, source_target_pairs={{0,24},{8,16},{16,8},{24,0},{1,25},{9,17},{17,9},{25,1},{2,26},{10... | collective-permute-start | bytes 196616 | tf_op jit(solution)/shard_map/ppermute | solution.py:720
  11.8 1.6 %collective-permute-start.5 = (f32[4,8,16,128]{3,2,1,0:T(8,128)S(1)}, f32[4,8,16,128]{3,2,1,0:T(8,128)S(1)}, u32[]{:S(2)}, u32[]{:S(2)}) collective-permute-start(f32[4,8,16,128]{3,2,1,0:T(8,128)S(1)} %pad_maximum_fusion.2), channel_id=1, source_target_pairs={{8,24},{24,8},{16,17},{17,16},{25,9},{9,25},{1,2},{2,1},{10,26},{2... | collective-permute-start | bytes 786440 | tf_op jit(solution)/shard_map/ppermute | solution.py:731
  11.9 8.7 %collective-permute-start.3 = (f32[4,8,16,128]{3,2,1,0:T(8,128)S(1)}, f32[4,8,16,128]{3,2,1,0:T(8,128)S(1)}, u32[]{:S(2)}, u32[]{:S(2)}) collective-permute-start(f32[4,8,16,128]{3,2,1,0:T(8,128)S(1)} %pad_maximum_fusion.2), channel_id=1, source_target_pairs={{0,8},{8,0},{24,16},{16,24},{17,25},{25,17},{9,1},{1,9},{2,10},{10... | collective-permute-start | bytes 786440 | tf_op jit(solution)/shard_map/ppermute | solution.py:731
  12.7 7.9 %collective-permute-start.7 = (f32[4,8,16,128]{3,2,1,0:T(8,128)S(1)}, f32[4,8,16,128]{3,2,1,0:T(8,128)S(1)}, u32[]{:S(2)}, u32[]{:S(2)}) collective-permute-start(f32[4,8,16,128]{3,2,1,0:T(8,128)S(1)} %pad_maximum_fusion.2), channel_id=1, source_target_pairs={{0,4},{4,0},{1,5},{5,1},{2,6},{6,2},{3,7},{7,3},{8,12},{12,8},{9,1... | collective-permute-start | bytes 786440 | tf_op jit(solution)/shard_map/ppermute | solution.py:736
  13.4 7.3 %collective-permute-start.6 = (f32[4,8,16,128]{3,2,1,0:T(8,128)S(1)}, f32[4,8,16,128]{3,2,1,0:T(8,128)S(1)}, u32[]{:S(2)}, u32[]{:S(2)}) collective-permute-start(f32[4,8,16,128]{3,2,1,0:T(8,128)S(1)} %collective-permute-done.5), channel_id=1, source_target_pairs={{0,4},{4,0},{1,5},{5,1},{2,6},{6,2},{3,7},{7,3},{8,12},{12,8},{9,1... | collective-permute-start | bytes 786440 | tf_op jit(solution)/shard_map/ppermute | solution.py:736
  20.6 1.5 %collective-permute-start.4 = (f32[4,8,16,128]{3,2,1,0:T(8,128)S(1)}, f32[4,8,16,128]{3,2,1,0:T(8,128)S(1)}, u32[]{:S(2)}, u32[]{:S(2)}) collective-permute-start(f32[4,8,16,128]{3,2,1,0:T(8,128)S(1)} %collective-permute-done.3), channel_id=1, source_target_pairs={{0,4},{4,0},{1,5},{5,1},{2,6},{6,2},{3,7},{7,3},{8,12},{12,8},{9,1... | collective-permute-start | bytes 786440 | tf_op jit(solution)/shard_map/ppermute | solution.py:736
  40.0 4.4 %collective-permute-start.8 = (f32[104,128]{1,0:T(8,128)S(1)}, f32[104,128]{1,0:T(8,128)S(1)}, u32[]{:S(2)}, u32[]{:S(2)}) collective-permute-start(f32[104,128]{1,0:T(8,128)S(1)} %get-tuple-element.15), channel_id=1, source_target_pairs={{0,8},{8,0},{16,24},{24,16},{1,9},{9,1},{17,25},{25,17},{2,10},{10... | collective-permute-start | bytes 159752 | tf_op jit(solution)/shard_map/ppermute | solution.py:770
  40.3 4.7 %collective-permute-start.9 = (f32[104,128]{1,0:T(8,128)S(1)}, f32[104,128]{1,0:T(8,128)S(1)}, u32[]{:S(2)}, u32[]{:S(2)}) collective-permute-start(f32[104,128]{1,0:T(8,128)S(1)} %get-tuple-element.16), channel_id=1, source_target_pairs={{0,16},{8,24},{16,0},{24,8},{1,17},{9,25},{17,1},{25,9},{2,18},{10... | collective-permute-start | bytes 159752 | tf_op jit(solution)/shard_map/ppermute | solution.py:770
  40.4 5.3 %collective-permute-start.10 = (f32[104,128]{1,0:T(8,128)S(1)}, f32[104,128]{1,0:T(8,128)S(1)}, u32[]{:S(2)}, u32[]{:S(2)}) collective-permute-start(f32[104,128]{1,0:T(8,128)S(1)} %get-tuple-element.17), channel_id=1, source_target_pairs={{0,24},{8,16},{16,8},{24,0},{1,25},{9,17},{17,9},{25,1},{2,26},{10... | collective-permute-start | bytes 159752 | tf_op jit(solution)/shard_map/ppermute | solution.py:770

commit v6 on v5

--- a/solution.py
+++ b/solution.py
@@ -514,7 +514,7 @@
                     coarse_rhs[c, i, j, k] = 0.5 * (line[2 * k] + line[2 * k + 2]) + line[2 * k + 1]
         return carry
 
-    lax.fori_loop(0, 3, body, 0, unroll=n < 4)
+    lax.fori_loop(0, 3, body, 0, unroll=True)
 
 
 def add_prolonged(coarse, fine, inside, half):
@@ -540,7 +540,7 @@
         fill_both(ref.at[c], n)
         return carry
 
-    lax.fori_loop(0, 3, body, 0, unroll=n < 4)
+    lax.fori_loop(0, 3, body, 0, unroll=True)
 
 
 def cycle_kernel(

time: 46.9 us -> 45.4 us (0.968)
  Pallas kernels: 20.2 us -> 18.7 us
    pallas_call x1, Pallas kernels: 17.7 us -> 16.1 us  [shards_by_slab(): pl.pallas_call(cycle_kernel, out_shape=[pltpu.VMEM((104, LANES), f32)] *...]
where the time goes in v6:
time: 45.4 us; the launch traced here: 45.2 us
  Pallas kernels  18.7 us (41%)
  waiting for transfers between devices  16.4 us (36%)
  starting transfers between devices  9.11 us (20%)
  between operations  0.72 us (2%)
    pallas_call x1, Pallas kernels, shards_by_slab(): pl.pallas_call(cycle_kernel, out_shape=[pltpu.VMEM((104, LANES), f32)] *...  16.1 us
    ppermute x2, waiting for transfers between devices, swap_in_chain(): return lax.ppermute(mine, ('gx', 'gy', 'gz'), pairs)  7.78 us
    ppermute x3, waiting for transfers between devices, shards_by_slab(): mine.append(lax.ppermute(packed[j], 'gx', [(i, i ^ j) for i in range(4)]))  5.14 us
    ppermute x3, starting transfers between devices, shards_by_slab(): mine.append(lax.ppermute(packed[j], 'gx', [(i, i ^ j) for i in range(4)]))  4.54 us
    ppermute x3, starting transfers between devices, shards_by_slab(): back.append(lax.ppermute(message[j], 'gx', [(i, i ^ j) for i in range(4)]))  3.55 us
    ppermute x3, waiting for transfers between devices, shards_by_slab(): back.append(lax.ppermute(message[j], 'gx', [(i, i ^ j) for i in range(4)]))  2.11 us
    pallas_call x1, Pallas kernels, shards_by_slab(): pl.pallas_call(pack_kernel, out_shape=[pltpu.VMEM((8, 16, LANES), f32)] *...  1.45 us
    ppermute x3, waiting for transfers between devices, both_halves(): other = lax.ppermute(half, 'gy', [(0, 1), (1, 0)])  1.36 us
  transfers between devices with their start and end apart: 11, of which 9 were waited for; matrix products, arithmetic and copies ran while one was open for 0% of the time, Pallas kernels for 0%

profile of v6, /device:TPU:0, one launch (start us, length us, event | category | flops | bytes accessed | tf_op | source)
XLA Modules:
  0.0 45.2 jit_solution(1989511693481663952)
XLA Ops:
  0.6 1.5 %pack.1 = (f32[8,16,128]{2,1,0:T(8,128)S(1)}, f32[8,16,128]{2,1,0:T(8,128)S(1)}, f32[8,16,128]{2,1,0:T(8,128)S(1)}, f32[8,16,128]{2,1,0:T(8,128)S(1)}) custom-call(f32[8]{0:T(128)} %mod_ref.1, f32[4,16,128]{2,1,0:T(8,128)} %cw_ref.1, f32[4,16,128]{2,1,0:T(8,128)} %wg_ref.1, s32[4,16,128]{2,1,0:T(8,128)} %mat_ref.1, f32[4,16,128]{2,1,0:T(8,128)} %mass_ref.1, ...), custom_call_target="tpu_custom_call" | custom-call | tf_op jit(solution)/shard_map/pack/pallas_call | solution.py:709
  2.1 3.0 %collective-permute-start = (f32[8,16,128]{2,1,0:T(8,128)S(1)}, f32[8,16,128]{2,1,0:T(8,128)S(1)}, u32[]{:S(2)}, u32[]{:S(2)}) collective-permute-start(f32[8,16,128]{2,1,0:T(8,128)S(1)} %get-tuple-element.11), channel_id=1, source_target_pairs={{0,8},{8,0},{16,24},{24,16},{1,9},{9,1},{17,25},{25,17},{2,10},{10... | collective-permute-start | bytes 196616 | tf_op jit(solution)/shard_map/ppermute | solution.py:720
  5.1 1.5 %collective-permute-start.1 = (f32[8,16,128]{2,1,0:T(8,128)S(1)}, f32[8,16,128]{2,1,0:T(8,128)S(1)}, u32[]{:S(2)}, u32[]{:S(2)}) collective-permute-start(f32[8,16,128]{2,1,0:T(8,128)S(1)} %get-tuple-element.12), channel_id=1, source_target_pairs={{0,16},{8,24},{16,0},{24,8},{1,17},{9,25},{17,1},{25,9},{2,18},{10... | collective-permute-start | bytes 196616 | tf_op jit(solution)/shard_map/ppermute | solution.py:720
  6.6 0.0 collective-permute-start.2
  6.6 0.8 %collective-permute-done = f32[8,16,128]{2,1,0:T(8,128)S(1)} collective-permute-done((f32[8,16,128]{2,1,0:T(8,128)S(1)}, f32[8,16,128]{2,1,0:T(8,128)S(1)}, u32[]{:S(2)}, u32[]{:S(2)}) %collective-permute-start) | collective-permute-done | bytes 65568 | tf_op jit(solution)/shard_map/ppermute | solution.py:720
  7.5 1.9 %collective-permute-done.1 = f32[8,16,128]{2,1,0:T(8,128)S(1)} collective-permute-done((f32[8,16,128]{2,1,0:T(8,128)S(1)}, f32[8,16,128]{2,1,0:T(8,128)S(1)}, u32[]{:S(2)}, u32[]{:S(2)}) %collective-permute-start.1) | collective-permute-done | bytes 65568 | tf_op jit(solution)/shard_map/ppermute | solution.py:720
  9.4 2.4 %collective-permute-done.2 = f32[8,16,128]{2,1,0:T(8,128)S(1)} collective-permute-done((f32[8,16,128]{2,1,0:T(8,128)S(1)}, f32[8,16,128]{2,1,0:T(8,128)S(1)}, u32[]{:S(2)}, u32[]{:S(2)}) %collective-permute-start.2) | collective-permute-done | bytes 65568 | tf_op jit(solution)/shard_map/ppermute | solution.py:720
  11.8 0.1 collective-permute-start.5
  11.9 0.8 %collective-permute-start.3 = (f32[4,8,16,128]{3,2,1,0:T(8,128)S(1)}, f32[4,8,16,128]{3,2,1,0:T(8,128)S(1)}, u32[]{:S(2)}, u32[]{:S(2)}) collective-permute-start(f32[4,8,16,128]{3,2,1,0:T(8,128)S(1)} %pad_maximum_fusion.2), channel_id=1, source_target_pairs={{0,8},{8,0},{24,16},{16,24},{17,25},{25,17},{9,1},{1,9},{2,10},{10... | collective-permute-start | bytes 786440 | tf_op jit(solution)/shard_map/ppermute | solution.py:731
  12.7 0.0 collective-permute-start.7
  12.7 0.7 %collective-permute-done.5 = f32[4,8,16,128]{3,2,1,0:T(8,128)S(1)} collective-permute-done((f32[4,8,16,128]{3,2,1,0:T(8,128)S(1)}, f32[4,8,16,128]{3,2,1,0:T(8,128)S(1)}, u32[]{:S(2)}, u32[]{:S(2)}) %collective-permute-start.5) | collective-permute-done | bytes 262176 | tf_op jit(solution)/shard_map/ppermute | solution.py:731
  13.4 0.1 collective-permute-start.6
  13.5 7.1 %collective-permute-done.3 = f32[4,8,16,128]{3,2,1,0:T(8,128)S(1)} collective-permute-done((f32[4,8,16,128]{3,2,1,0:T(8,128)S(1)}, f32[4,8,16,128]{3,2,1,0:T(8,128)S(1)}, u32[]{:S(2)}, u32[]{:S(2)}) %collective-permute-start.3) | collective-permute-done | bytes 262176 | tf_op jit(solution)/shard_map/ppermute | solution.py:731
  20.6 0.0 collective-permute-start.4
  20.6 0.0 collective-permute-done.7
  20.7 0.1 pad_maximum_fusion.1.own_ref
  20.7 0.0 collective-permute-done.6
  20.8 1.4 %collective-permute-done.4 = f32[4,8,16,128]{3,2,1,0:T(8,128)S(1)} collective-permute-done((f32[4,8,16,128]{3,2,1,0:T(8,128)S(1)}, f32[4,8,16,128]{3,2,1,0:T(8,128)S(1)}, u32[]{:S(2)}, u32[]{:S(2)}) %collective-permute-start.4) | collective-permute-done | bytes 262176 | tf_op jit(solution)/shard_map/ppermute | solution.py:736
  22.2 0.1 fusion
  22.3 16.1 %cycle.1 = (f32[104,128]{1,0:T(8,128)S(1)}, f32[104,128]{1,0:T(8,128)S(1)}, f32[104,128]{1,0:T(8,128)S(1)}, f32[104,128]{1,0:T(8,128)S(1)}) custom-call(f32[4,8,32,128]{3,2,1,0:T(8,128)S(1)} %get-tuple-element.19.prev_ref, f32[4,8,32,128]{3,2,1,0:T(8,128)S(1)} %pad_maximum_fusion.1.own_ref, f32[4,8,32,128]{3,2,1,0:T(8,128)S(1)} %get-tuple-element.18.next_ref), custom_call_target="tpu_custom_call" | custom-call | tf_op jit(solution)/shard_map/cycle/pallas_call | solution.py:750
  38.5 0.3 collective-permute-start.8
  38.8 0.0 collective-permute-start.9
  38.8 3.2 %collective-permute-start.10 = (f32[104,128]{1,0:T(8,128)S(1)}, f32[104,128]{1,0:T(8,128)S(1)}, u32[]{:S(2)}, u32[]{:S(2)}) collective-permute-start(f32[104,128]{1,0:T(8,128)S(1)} %get-tuple-element.17), channel_id=1, source_target_pairs={{0,24},{8,16},{16,8},{24,0},{1,25},{9,17},{17,9},{25,1},{2,26},{10... | collective-permute-start | bytes 159752 | tf_op jit(solution)/shard_map/ppermute | solution.py:770
  42.0 0.9 %collective-permute-done.8.one_ref = f32[104,128]{1,0:T(8,128)S(1)} collective-permute-done((f32[104,128]{1,0:T(8,128)S(1)}, f32[104,128]{1,0:T(8,128)S(1)}, u32[]{:S(2)}, u32[]{:S(2)}) %collective-permute-start.8) | collective-permute-done | bytes 53280 | tf_op jit(solution)/shard_map/ppermute | solution.py:770
  42.9 0.6 %collective-permute-done.9.two_ref = f32[104,128]{1,0:T(8,128)S(1)} collective-permute-done((f32[104,128]{1,0:T(8,128)S(1)}, f32[104,128]{1,0:T(8,128)S(1)}, u32[]{:S(2)}, u32[]{:S(2)}) %collective-permute-start.9) | collective-permute-done | bytes 53280 | tf_op jit(solution)/shard_map/ppermute | solution.py:770
  43.5 0.6 %collective-permute-done.10.three_ref = f32[104,128]{1,0:T(8,128)S(1)} collective-permute-done((f32[104,128]{1,0:T(8,128)S(1)}, f32[104,128]{1,0:T(8,128)S(1)}, u32[]{:S(2)}, u32[]{:S(2)}) %collective-permute-start.10) | collective-permute-done | bytes 53280 | tf_op jit(solution)/shard_map/ppermute | solution.py:770
  44.1 1.1 %unpack.1 = (f32[3,4,16,128]{3,2,1,0:T(8,128)}, f32[27,2,8,64]{3,2,1,0:T(8,128)}) custom-call(f32[104,128]{1,0:T(8,128)S(1)} %get-tuple-element.14.own_ref, f32[104,128]{1,0:T(8,128)S(1)} %collective-permute-done.8.one_ref, f32[104,128]{1,0:T(8,128)S(1)} %collective-permute-done.9.two_ref, f32[104,128]{1,0:T(8,128)S(1)} %collective-permute-done.10.three_ref), custom_call_target="tpu_custom_call" | custom-call | tf_op jit(solution)/shard_map/unpack/pallas_call | solution.py:771
  (4 shorter events, 0.1 us)
Async XLA Ops:
  2.1 5.4 %collective-permute-start = (f32[8,16,128]{2,1,0:T(8,128)S(1)}, f32[8,16,128]{2,1,0:T(8,128)S(1)}, u32[]{:S(2)}, u32[]{:S(2)}) collective-permute-start(f32[8,16,128]{2,1,0:T(8,128)S(1)} %get-tuple-element.11), channel_id=1, source_target_pairs={{0,8},{8,0},{16,24},{24,16},{1,9},{9,1},{17,25},{25,17},{2,10},{10... | collective-permute-start | bytes 196616 | tf_op jit(solution)/shard_map/ppermute | solution.py:720
  5.1 4.3 %collective-permute-start.1 = (f32[8,16,128]{2,1,0:T(8,128)S(1)}, f32[8,16,128]{2,1,0:T(8,128)S(1)}, u32[]{:S(2)}, u32[]{:S(2)}) collective-permute-start(f32[8,16,128]{2,1,0:T(8,128)S(1)} %get-tuple-element.12), channel_id=1, source_target_pairs={{0,16},{8,24},{16,0},{24,8},{1,17},{9,25},{17,1},{25,9},{2,18},{10... | collective-permute-start | bytes 196616 | tf_op jit(solution)/shard_map/ppermute | solution.py:720
  6.6 5.2 %collective-permute-start.2 = (f32[8,16,128]{2,1,0:T(8,128)S(1)}, f32[8,16,128]{2,1,0:T(8,128)S(1)}, u32[]{:S(2)}, u32[]{:S(2)}) collective-permute-start(f32[8,16,128]{2,1,0:T(8,128)S(1)} %get-tuple-element.13), channel_id=1, source_target_pairs={{0,24},{8,16},{16,8},{24,0},{1,25},{9,17},{17,9},{25,1},{2,26},{10... | collective-permute-start | bytes 196616 | tf_op jit(solution)/shard_map/ppermute | solution.py:720
  11.8 1.6 %collective-permute-start.5 = (f32[4,8,16,128]{3,2,1,0:T(8,128)S(1)}, f32[4,8,16,128]{3,2,1,0:T(8,128)S(1)}, u32[]{:S(2)}, u32[]{:S(2)}) collective-permute-start(f32[4,8,16,128]{3,2,1,0:T(8,128)S(1)} %pad_maximum_fusion.2), channel_id=1, source_target_pairs={{8,24},{24,8},{16,17},{17,16},{25,9},{9,25},{1,2},{2,1},{10,26},{2... | collective-permute-start | bytes 786440 | tf_op jit(solution)/shard_map/ppermute | solution.py:731
  11.9 8.7 %collective-permute-start.3 = (f32[4,8,16,128]{3,2,1,0:T(8,128)S(1)}, f32[4,8,16,128]{3,2,1,0:T(8,128)S(1)}, u32[]{:S(2)}, u32[]{:S(2)}) collective-permute-start(f32[4,8,16,128]{3,2,1,0:T(8,128)S(1)} %pad_maximum_fusion.2), channel_id=1, source_target_pairs={{0,8},{8,0},{24,16},{16,24},{17,25},{25,17},{9,1},{1,9},{2,10},{10... | collective-permute-start | bytes 786440 | tf_op jit(solution)/shard_map/ppermute | solution.py:731
  12.7 7.9 %collective-permute-start.7 = (f32[4,8,16,128]{3,2,1,0:T(8,128)S(1)}, f32[4,8,16,128]{3,2,1,0:T(8,128)S(1)}, u32[]{:S(2)}, u32[]{:S(2)}) collective-permute-start(f32[4,8,16,128]{3,2,1,0:T(8,128)S(1)} %pad_maximum_fusion.2), channel_id=1, source_target_pairs={{0,4},{4,0},{1,5},{5,1},{2,6},{6,2},{3,7},{7,3},{8,12},{12,8},{9,1... | collective-permute-start | bytes 786440 | tf_op jit(solution)/shard_map/ppermute | solution.py:736
  13.4 7.3 %collective-permute-start.6 = (f32[4,8,16,128]{3,2,1,0:T(8,128)S(1)}, f32[4,8,16,128]{3,2,1,0:T(8,128)S(1)}, u32[]{:S(2)}, u32[]{:S(2)}) collective-permute-start(f32[4,8,16,128]{3,2,1,0:T(8,128)S(1)} %collective-permute-done.5), channel_id=1, source_target_pairs={{0,4},{4,0},{1,5},{5,1},{2,6},{6,2},{3,7},{7,3},{8,12},{12,8},{9,1... | collective-permute-start | bytes 786440 | tf_op jit(solution)/shard_map/ppermute | solution.py:736
  20.6 1.5 %collective-permute-start.4 = (f32[4,8,16,128]{3,2,1,0:T(8,128)S(1)}, f32[4,8,16,128]{3,2,1,0:T(8,128)S(1)}, u32[]{:S(2)}, u32[]{:S(2)}) collective-permute-start(f32[4,8,16,128]{3,2,1,0:T(8,128)S(1)} %collective-permute-done.3), channel_id=1, source_target_pairs={{0,4},{4,0},{1,5},{5,1},{2,6},{6,2},{3,7},{7,3},{8,12},{12,8},{9,1... | collective-permute-start | bytes 786440 | tf_op jit(solution)/shard_map/ppermute | solution.py:736
  38.5 4.4 %collective-permute-start.8 = (f32[104,128]{1,0:T(8,128)S(1)}, f32[104,128]{1,0:T(8,128)S(1)}, u32[]{:S(2)}, u32[]{:S(2)}) collective-permute-start(f32[104,128]{1,0:T(8,128)S(1)} %get-tuple-element.15), channel_id=1, source_target_pairs={{0,8},{8,0},{16,24},{24,16},{1,9},{9,1},{17,25},{25,17},{2,10},{10... | collective-permute-start | bytes 159752 | tf_op jit(solution)/shard_map/ppermute | solution.py:770
  38.8 4.7 %collective-permute-start.9 = (f32[104,128]{1,0:T(8,128)S(1)}, f32[104,128]{1,0:T(8,128)S(1)}, u32[]{:S(2)}, u32[]{:S(2)}) collective-permute-start(f32[104,128]{1,0:T(8,128)S(1)} %get-tuple-element.16), channel_id=1, source_target_pairs={{0,16},{8,24},{16,0},{24,8},{1,17},{9,25},{17,1},{25,9},{2,18},{10... | collective-permute-start | bytes 159752 | tf_op jit(solution)/shard_map/ppermute | solution.py:770
  38.8 5.3 %collective-permute-start.10 = (f32[104,128]{1,0:T(8,128)S(1)}, f32[104,128]{1,0:T(8,128)S(1)}, u32[]{:S(2)}, u32[]{:S(2)}) collective-permute-start(f32[104,128]{1,0:T(8,128)S(1)} %get-tuple-element.17), channel_id=1, source_target_pairs={{0,24},{8,16},{16,8},{24,0},{1,25},{9,17},{17,9},{25,1},{2,26},{10... | collective-permute-start | bytes 159752 | tf_op jit(solution)/shard_map/ppermute | solution.py:770
